TPU v7x, 32 devices: a whole 2x2x4 slice. The times are simulated.
32 devices in a mesh: row: 8 (over z, y), col: 4 (over x, core).
Axes of the slice: x: 2, y: 2, z: 4, core: 2. Of those that a mesh axis runs over, the one named last changes fastest.
Arguments:
- matrix: bfloat16 [28672, 28672], P('row', 'col'), may hold values from -1.5 to 16, as said below
Outputs:
- factored: bfloat16 [28672, 28672], P('row', 'col')
Inputs may be any that keep to these rules, and one draw needn't show every extreme that they name: `matrix`: in logical order, diagonal entries lie between 12 and 16 and off-diagonal entries have magnitude at most 1.5.
All inputs are finite; a program needn't handle non-finite values.
Results may differ from a plain program's by a relative error of at most 0.0025.
The roundings to bfloat16 on the way count: a program that leaves them out, or rounds other values in their place, can miss the bound.
Values may be sent and summed in bfloat16 or wider, within the bound.
No kernel may reach another device: no remote copies, remote signals or barrier semaphores. Data moves between devices by JAX's collectives and lax.ppermute only.
A program may use at most 384 MiB of HBM per device.

v0:
```python
import jax
import jax.numpy as jnp
from jax import lax
from jax.sharding import PartitionSpec as P

NB = 256
STEPS = 2


def broadcast(block, axis, owner):
    block = jnp.where(lax.axis_index(axis) == owner, block, jnp.zeros_like(block))
    return lax.psum(block, axis)


def factor_block(block):
    work = block.astype(jnp.float32)
    size = work.shape[0]
    positions = jnp.arange(size, dtype=jnp.int32)

    def eliminate(column, work):
        values = lax.dynamic_slice_in_dim(work, column, 1, 1)[:, 0]
        pivot_row = lax.dynamic_slice_in_dim(work, column, 1, 0)[0]
        pivot = jnp.sum(jnp.where(positions == column, pivot_row, 0.0))
        scaled = jnp.where(positions > column, values / pivot, 0.0)
        across = jnp.where(positions > column, pivot_row, 0.0)
        work = work - scaled[:, None] * across[None, :]
        kept = jnp.where(positions > column, scaled, values)
        return jnp.where(positions[None, :] == column, kept[:, None], work)

    return lax.fori_loop(0, size, eliminate, work)


def invert_upper(upper):
    size = upper.shape[0]
    positions = jnp.arange(size, dtype=jnp.int32)

    def substitute(count, inverse):
        index = size - 1 - count
        line = lax.dynamic_slice_in_dim(upper, index, 1, 0)[0]
        strict = jnp.where(positions > index, line, 0.0)
        pivot = jnp.sum(jnp.where(positions == index, line, 0.0))
        unit = jnp.where(positions == index, 1.0, 0.0).astype(jnp.float32)
        fresh = (unit - jnp.dot(strict, inverse, precision=lax.Precision.HIGHEST)) / pivot
        return jnp.where(positions[:, None] == index, fresh[None, :], inverse)

    return lax.fori_loop(0, size, substitute, jnp.zeros((size, size), jnp.float32))


def invert_lower(lower):
    size = lower.shape[0]
    positions = jnp.arange(size, dtype=jnp.int32)

    def substitute(index, inverse):
        line = lax.dynamic_slice_in_dim(lower, index, 1, 0)[0]
        strict = jnp.where(positions < index, line, 0.0)
        unit = jnp.where(positions == index, 1.0, 0.0).astype(jnp.float32)
        fresh = unit - jnp.dot(strict, inverse, precision=lax.Precision.HIGHEST)
        return jnp.where(positions[:, None] == index, fresh[None, :], inverse)

    return lax.fori_loop(0, size, substitute, jnp.zeros((size, size), jnp.float32))


def solve_left(upper_inverse, panel, keep_rows):
    solved = jnp.dot(panel.astype(jnp.float32), upper_inverse, precision=lax.Precision.HIGHEST)
    return jnp.where(keep_rows[:, None], solved, 0.0).astype(jnp.bfloat16)


def solve_top(lower_inverse, panel, keep_cols):
    solved = jnp.dot(lower_inverse, panel.astype(jnp.float32), precision=lax.Precision.HIGHEST)
    return jnp.where(keep_cols[None, :], solved, 0.0).astype(jnp.bfloat16)


def on_device(matrix):
    grid_rows = lax.axis_size("row")
    grid_cols = lax.axis_size("col")
    local_rows, local_cols = matrix.shape
    row_block = jnp.arange(local_rows, dtype=jnp.int32) // NB * grid_rows + lax.axis_index("row")
    col_block = jnp.arange(local_cols, dtype=jnp.int32) // NB * grid_cols + lax.axis_index("col")
    work = matrix
    for section in range(STEPS):
        root_row = section % grid_rows
        root_col = section % grid_cols
        row_start = section // grid_rows * NB
        col_start = section // grid_cols * NB
        own_diag = work[row_start : row_start + NB, col_start : col_start + NB]
        diag_block = broadcast(own_diag, ("row", "col"), root_row * grid_cols + root_col)
        packed = factor_block(diag_block)
        upper = jnp.triu(packed)
        lower = jnp.tril(packed, -1) + jnp.eye(NB, dtype=jnp.float32)
        upper_inverse = invert_upper(upper)
        lower_inverse = invert_lower(lower)
        column_panel = work[:, col_start : col_start + NB]
        row_panel = work[row_start : row_start + NB, :]
        keep_rows = row_block > section
        keep_cols = col_block > section
        left_panel = broadcast(solve_left(upper_inverse, column_panel, keep_rows), "col", root_col)
        top_panel = broadcast(solve_top(lower_inverse, row_panel, keep_cols), "row", root_row)
        update = jnp.dot(left_panel, top_panel, preferred_element_type=jnp.float32)
        updated = (work.astype(jnp.float32) - update).astype(jnp.bfloat16)
        in_col = (col_block == section)[None, :]
        in_row = (row_block == section)[:, None]
        left_wide = jnp.tile(left_panel, (1, local_cols // NB))
        top_tall = jnp.tile(top_panel, (local_rows // NB, 1))
        packed_tiles = jnp.tile(packed.astype(jnp.bfloat16), (local_rows // NB, local_cols // NB))
        updated = jnp.where(in_col & keep_rows[:, None], left_wide, updated)
        updated = jnp.where(in_row & keep_cols[None, :], top_tall, updated)
        work = jnp.where(in_row & in_col, packed_tiles, updated)
    return work


def solution(mesh):
    in_specs = (P("row", "col"),)
    out_specs = P("row", "col")
    return jax.shard_map(
        on_device, mesh=mesh, in_specs=in_specs, out_specs=out_specs, check_vma=False
    )
```

profile of v0, /device:TPU:24, one launch (start us, length us, event | category | flops | bytes accessed | tf_op | source)
XLA Modules:
  0.0 2608.6 jit_solution(5083503190218780733)
XLA Ops:
  6.5 1.6 slice_select_fusion.1
  8.3 127.0 %all-reduce.7.cloned.1.call-done = bf16[256,256]{1,0:T(8,128)(2,1)} async-done(((bf16[256,256]{1,0:T(8,128)(2,1)}), bf16[256,256]{1,0:T(8,128)(2,1)}) %all-reduce.7.cloned.1.call-update) | async-done | bytes 131088 | tf_op jit(solution)/shard_map/psum | solution.py:12
  135.3 1.0 copy.16
  136.3 411.8 %while.94 = (s32[]{:T(128)}, f32[256,256]{0,1:T(8,128)S(1)}, s32[]{:T(128)}) while((s32[]{:T(128)}, f32[256,256]{0,1:T(8,128)S(1)}, s32[]{:T(128)}) %tuple.229), condition=%wide.region_3.4_spmd.clone.clone, body=%wide.region_1.3_spmd.clone.clone.sunk | while | flops 198913 | bytes 1060173 | solution.py:30
  548.3 424.2 %while.97 = (s32[]{:T(128)}, f32[256,256]{1,0:T(8,128)S(1)}, f32[256,256]{1,0:T(8,128)S(1)}, s32[]{:T(128)}, s32[]{:T(128)}, /*index=5*/s32[]{:T(128)}, s32[]{:T(128)}) while((s32[]{:T(128)}, f32[256,256]{1,0:T(8,128)S(1)}, f32[256,256]{1,0:T(8,128)S(1)}, s32[]{:T(128)}, s32[]{:T(128)}, /*index=5*/s32[]{:T(128)}, ...), condition=%wide.region_9.10_spmd.clone.clone, body=%wide.region_7.9_spmd.clone.clone.sunk | while | flops 985606 | bytes 796326 | solution.py:46
  554.1 0.7 subtract_divide_fusion.4
  555.8 0.7 subtract_divide_fusion.4
  557.4 0.7 subtract_divide_fusion.4
  569.0 0.7 subtract_divide_fusion.4
  570.7 0.7 subtract_divide_fusion.4
  572.3 0.7 subtract_divide_fusion.4
  585.6 0.7 subtract_divide_fusion.4
  587.2 0.7 subtract_divide_fusion.4
  588.9 0.7 subtract_divide_fusion.4
  600.5 0.7 subtract_divide_fusion.4
  602.1 0.7 subtract_divide_fusion.4
  603.8 0.7 subtract_divide_fusion.4
  617.1 0.7 subtract_divide_fusion.4
  618.7 0.7 subtract_divide_fusion.4
  620.4 0.7 subtract_divide_fusion.4
  632.0 0.7 subtract_divide_fusion.4
  633.6 0.7 subtract_divide_fusion.4
  635.3 0.7 subtract_divide_fusion.4
  648.5 0.7 subtract_divide_fusion.4
  650.2 0.7 subtract_divide_fusion.4
  651.8 0.7 subtract_divide_fusion.4
  972.5 5.8 fusion.40
  978.4 106.3 %while.96 = (s32[]{:T(128)}, f32[256,256]{1,0:T(8,128)S(1)}, f32[256,256]{1,0:T(8,128)S(1)}, s32[]{:T(128)}, s32[]{:T(128)}) while((s32[]{:T(128)}, f32[256,256]{1,0:T(8,128)S(1)}, f32[256,256]{1,0:T(8,128)S(1)}, s32[]{:T(128)}, s32[]{:T(128)}) %tuple.235), condition=%wide.region_5.6_spmd.clone.clone, body=%wide.region_4.5_spmd.clone.clone.sunk | while | flops 984579 | bytes 796256 | solution.py:60
  1084.7 6.9 fusion.35
  1092.7 19.1 tile.24
  1111.8 48.4 %copy.27 = bf16[448,8,28,256]{3,1,2,0:T(8,128)(2,1)} copy(bf16[448,8,28,256]{3,2,1,0:T(8,128)(2,1)} %bitcast.94) | data formatting | bytes 102760448
  1160.2 18.1 tile.28
  1178.3 62.2 %copy.20 = bf16[3584,7168]{1,0:T(8,128)(2,1)} copy(bf16[3584,7168]{0,1:T(8,128)(2,1)} %bitcast.97) | data formatting | bytes 102760448 | tf_op jit(solution)/shard_map/tile | solution.py:102
  1240.5 76.9 %and_select_fusion.4 = bf16[3584,7168]{1,0:T(8,128)(2,1)} fusion(bf16[3584,7168]{1,0:T(8,128)(2,1)} %bitcast.99, bf16[3584,7168]{1,0:T(8,128)(2,1)} %copy.20, pred[7168]{0:T(1024)(128)(4,1)S(1)} %fusion.52, pred[7168]{0:T(1024)(128)(4,1)S(1)} %fusion.53, pred[3584]{0:T(1024)(128)(4,1)S(1)} %fusion.61, pred[3584]{0:T(1024)(128)(4,1)S(1)} %fusion.62, ...), kind=kOutput, calls=%fused_computation.72 | convolution fusion | flops 13384548352 | bytes 211047424 | tf_op jit(solution)/shard_map/dot_general | solution.py:98
  1317.3 1.6 slice_select_fusion
  1319.1 121.5 %all-reduce.13.cloned.1.call-done = bf16[256,256]{1,0:T(8,128)(2,1)} async-done(((bf16[256,256]{1,0:T(8,128)(2,1)}), bf16[256,256]{1,0:T(8,128)(2,1)}) %all-reduce.13.cloned.1.call-update) | async-done | bytes 131088 | tf_op jit(solution)/shard_map/psum | solution.py:12
  1440.5 1.0 copy.21
  1441.5 379.6 %while.95 = (s32[]{:T(128)}, f32[256,256]{0,1:T(8,128)S(1)}, s32[]{:T(128)}) while((s32[]{:T(128)}, f32[256,256]{0,1:T(8,128)S(1)}, s32[]{:T(128)}) %tuple.238), condition=%wide.region_14.15_spmd.clone.clone, body=%wide.region_12.14_spmd.clone.clone.sunk | while | flops 198913 | bytes 1060173 | solution.py:30
  1821.3 434.1 %while.99 = (s32[]{:T(128)}, f32[256,256]{1,0:T(8,128)S(1)}, f32[256,256]{1,0:T(8,128)S(1)}, s32[]{:T(128)}, s32[]{:T(128)}, /*index=5*/s32[]{:T(128)}, s32[]{:T(128)}) while((s32[]{:T(128)}, f32[256,256]{1,0:T(8,128)S(1)}, f32[256,256]{1,0:T(8,128)S(1)}, s32[]{:T(128)}, s32[]{:T(128)}, /*index=5*/s32[]{:T(128)}, ...), condition=%wide.region_20.21_spmd.clone.clone, body=%wide.region_18.20_spmd.clone.clone.sunk | while | flops 985606 | bytes 796326 | solution.py:46
  2255.5 4.6 fusion.38
  2260.4 106.3 %while.98 = (s32[]{:T(128)}, f32[256,256]{1,0:T(8,128)S(1)}, f32[256,256]{1,0:T(8,128)S(1)}, s32[]{:T(128)}, s32[]{:T(128)}) while((s32[]{:T(128)}, f32[256,256]{1,0:T(8,128)S(1)}, f32[256,256]{1,0:T(8,128)S(1)}, s32[]{:T(128)}, s32[]{:T(128)}) %tuple.259), condition=%wide.region_16.17_spmd.clone.clone, body=%wide.region_15.16_spmd.clone.clone.sunk | while | flops 984579 | bytes 796256 | solution.py:60
  2366.7 6.9 fusion.34
  2373.8 19.1 tile.60
  2392.9 48.5 %copy.28 = bf16[448,8,28,256]{3,1,2,0:T(8,128)(2,1)} copy(bf16[448,8,28,256]{3,2,1,0:T(8,128)(2,1)} %bitcast.95) | data formatting | bytes 102760448
  2441.4 2.8 copy.25
  2444.1 17.0 tile.64
  2461.1 62.3 %copy.26 = bf16[3584,7168]{1,0:T(8,128)(2,1)} copy(bf16[3584,7168]{0,1:T(8,128)(2,1)} %bitcast.96) | data formatting | bytes 102760448 | tf_op jit(solution)/shard_map/tile | solution.py:102
  2523.5 78.3 %and_select_fusion.5 = bf16[3584,7168]{1,0:T(8,128)(2,1)} fusion(bf16[3584,7168]{1,0:T(8,128)(2,1)} %bitcast.98, bf16[3584,7168]{1,0:T(8,128)(2,1)} %copy.26, pred[7168]{0:T(1024)(128)(4,1)S(1)} %copy-done.4, pred[7168]{0:T(1024)(128)(4,1)S(1)} %fusion.54, pred[3584]{0:T(1024)(128)(4,1)S(1)} %fusion.60, pred[3584]{0:T(1024)(128)(4,1)S(1)} %fusion.63, ...), kind=kOutput, calls=%fused_computation.73 | convolution fusion | flops 13384548352 | bytes 211047424 | tf_op jit(solution)/shard_map/dot_general | solution.py:98
  (9246 shorter events, 1766.9 us)
Async XLA Ops:
  6.5 128.7 %all-reduce.7.cloned.1.call-start = ((), (), s32[]{:S(2)}) async-start(), calls=%async_computation | async-start | bytes 262144 | tf_op jit(solution)/shard_map/psum | solution.py:12
  8.1 1152.0 %all-reduce.11.cloned.1.call-start = ((), (), s32[]{:S(2)}) async-start(), calls=%async_computation.2 | async-start | bytes 3670016 | tf_op jit(solution)/shard_map/psum | solution.py:12
  8.3 1103.5 %copy-start.5 = (s32[256]{0:T(256)}, s32[256]{0:T(256)S(1)}, u32[]{:S(2)}) copy-start(s32[256]{0:T(256)S(1)} %iota_add_fusion) | copy-start | bytes 3076
  978.3 262.1 %all-reduce.9.cloned.1.call-start = ((), (), s32[]{:S(2)}) async-start(), calls=%async_computation.1 | async-start | bytes 7340032 | tf_op jit(solution)/shard_map/psum | solution.py:12
  1091.6 348.9 %all-reduce.13.cloned.1.call-start = ((), (), s32[]{:S(2)}) async-start(), calls=%async_computation.3 | async-start | bytes 262144 | tf_op jit(solution)/shard_map/psum | solution.py:12
  1178.3 62.2 %copy-start.3 = (bf16[3584,256]{0,1:T(8,128)(2,1)S(1)}, bf16[3584,256]{0,1:T(8,128)(2,1)}, u32[]{:S(2)}) copy-start(bf16[3584,256]{0,1:T(8,128)(2,1)} %all-reduce.11.cloned.1.call-done) | copy-start | bytes 5505028
  1240.5 580.8 %copy-start.6 = (s32[256]{0:T(256)S(1)}, s32[256]{0:T(256)}, u32[]{:S(2)}) copy-start(s32[256]{0:T(256)} %copy-done.5) | copy-start | bytes 3076
  1240.5 580.9 %copy-start.1 = (f32[256,256]{1,0:T(8,128)S(1)}, f32[256,256]{1,0:T(8,128)}, u32[]{:S(2)}) copy-start(f32[256,256]{1,0:T(8,128)} %custom-call.3) | copy-start | bytes 786436
  1317.3 943.0 %copy-start = (f32[256,256]{1,0:T(8,128)S(1)}, f32[256,256]{1,0:T(8,128)}, u32[]{:S(2)}) copy-start(f32[256,256]{1,0:T(8,128)} %custom-call.2) | copy-start | bytes 786436
  1317.3 1049.4 %copy-start.4 = (pred[7168]{0:T(1024)(128)(4,1)S(1)}, pred[7168]{0:T(1024)(128)(4,1)}, u32[]{:S(2)}) copy-start(pred[7168]{0:T(1024)(128)(4,1)} %fusion.51) | copy-start | bytes 21508
  1319.0 1122.4 %all-reduce.17.cloned.1.call-start = ((), (), s32[]{:S(2)}) async-start(), calls=%async_computation.5 | async-start | bytes 3670016 | tf_op jit(solution)/shard_map/psum | solution.py:12
  2260.1 263.3 %all-reduce.15.cloned.1.call-start = ((), (), s32[]{:S(2)}) async-start(), calls=%async_computation.4 | async-start | bytes 7340032 | tf_op jit(solution)/shard_map/psum | solution.py:12
  2461.1 62.4 %copy-start.2 = (bf16[3584,256]{1,0:T(8,128)(2,1)S(1)}, bf16[3584,256]{1,0:T(8,128)(2,1)}, u32[]{:S(2)}) copy-start(bf16[3584,256]{1,0:T(8,128)(2,1)} %all-reduce.17.cloned.1.call-done) | copy-start | bytes 5505028
Sparse Core Ops, SparseCore 0:
  12.9 122.3 all-reduce.6
  978.4 47.3 all-reduce.10
  1091.7 140.8 all-reduce.8
  1319.1 121.3 all-reduce.12
  2260.2 47.2 all-reduce.16
  2373.8 140.8 all-reduce.14
where the time goes:
time: 2630 us; the launch traced here: 2610 us
  other arithmetic  1510 us (57%)
  local copies, waits for them, and re-layouts  376 us (14%)
  matrix products  375 us (14%)
  waiting for transfers between devices  249 us (9%)
  loops' own time  82.9 us (3%)
    div x512, other arithmetic, substitute(): (unit - jnp.dot(strict, inverse, precision=lax.Precision.HIGHEST)) / pivot  347 us
    reduce_sum x512, other arithmetic, substitute(): pivot = jnp.sum(jnp.where(positions == index, line, 0.0))  324 us
    select_n x512, other arithmetic, eliminate(): kept = jnp.where(positions > column, scaled, values)  310 us
    reduce_sum x512, other arithmetic, eliminate(): pivot = jnp.sum(jnp.where(positions == column, pivot_row, 0.0))  300 us
    psum x6, waiting for transfers between devices, broadcast(): return lax.psum(block, axis)  248 us
    another operation x4, local copies, waits for them, and re-layouts, on_device(): left_wide = jnp.tile(left_panel, (1, local_cols // NB))  160 us
    dot_general x2, matrix products, on_device(): update = jnp.dot(left_panel, top_panel, preferred_element_type=jnp.float32)  155 us
    select_n x1024, other arithmetic, substitute(): return jnp.where(positions[:, None] == index, fresh[None, :], inverse)  114 us

commit v1 on v0

v1 whole, which is shorter than its diff:
```python
import functools

import jax
import jax.numpy as jnp
from jax import lax
from jax.experimental import pallas as pl
from jax.experimental.pallas import tpu as pltpu
from jax.sharding import PartitionSpec as P

NB = 256
W = 32
MICRO = 4
CHUNKS = 14
DELAY = 2
PIECES = 4
FIRST_PIECE = 4
BATCHES = ((0, 4), (4, 7), (7, 10), (10, 12), (12, 14))
LIMIT = 56 * 2**20


def split3(x):
    high = x.astype(jnp.bfloat16)
    rest = x - high.astype(jnp.float32)
    middle = rest.astype(jnp.bfloat16)
    low = (rest - middle.astype(jnp.float32)).astype(jnp.bfloat16)
    return high, middle, low


def dot(a, b):
    return jnp.dot(a, b, preferred_element_type=jnp.float32)


def factor_small(block):
    lane = lax.broadcasted_iota(jnp.int32, (W, 128), 1)
    row = lax.broadcasted_iota(jnp.int32, (W, 128), 0)
    work = jnp.where(lane < W, block, 0.0)
    work = work + jnp.where((lane == row + W) | (lane == row + 2 * W), 1.0, 0.0)
    packed = work
    scale = jnp.ones((W, 128), jnp.float32)
    down = lane < 2 * W
    up = (lane < W) | (lane >= 2 * W)
    for first in range(0, W, MICRO):
        columns = [
            jnp.broadcast_to(work[:, j : j + 1], (W, 128)) for j in range(first, first + MICRO)
        ]
        for step in range(MICRO):
            j = first + step
            column = columns[step]
            inverse = 1.0 / column[j : j + 1, :]
            factor = jnp.where(row == j, 0.0, column * inverse)
            for later in range(step + 1, MICRO):
                other = columns[later]
                columns[later] = other - factor * other[j : j + 1, :]
            line = work[j : j + 1, :]
            packed = jnp.where((row == j) & (lane >= j), line, packed)
            packed = jnp.where((lane == j) & (row > j), factor, packed)
            scale = jnp.where(row == j, inverse, scale)
            masked = jnp.where(((row > j) & down) | ((row < j) & up), factor, 0.0)
            work = work - masked * line
    return jnp.where(lane < W, packed, 0.0), work, work * scale


def repeat_lanes(x, first):
    lane = lax.broadcasted_iota(jnp.int32, x.shape, 1)
    x = jnp.where((lane >= first) & (lane < first + W), x, 0.0)
    x = x + pltpu.roll(x, W, 1)
    return x + pltpu.roll(x, 2 * W, 1)


def pack_left(x):
    lane = lax.broadcasted_iota(jnp.int32, x.shape, 1)
    high = x.astype(jnp.bfloat16).astype(jnp.float32)
    rest = x - high
    middle = rest.astype(jnp.bfloat16).astype(jnp.float32)
    low = rest - middle
    first = jnp.where(lane < 3 * W, high, middle)
    second = jnp.where(lane < W, middle, jnp.where(lane < 2 * W, low, 0.0))
    return jnp.concatenate([first.astype(jnp.bfloat16), second.astype(jnp.bfloat16)], axis=1)


def pack_right(x):
    high, middle, low = split3(x)
    zero = jnp.zeros_like(high)
    return jnp.concatenate([high, middle, low, high, middle, high, zero, zero], axis=0)


def block_step(k, work_ref, lower_ref, upper_ref):
    active = NB - W * k
    packed, left_small, upper_small = factor_small(work_ref[:W, :128])
    small_left = pack_left(repeat_lanes(left_small, W))
    small_upper = repeat_lanes(upper_small, 2 * W)
    small_upper = pack_right(jnp.concatenate([small_upper, small_upper], axis=1))

    work = work_ref[...]
    lower = lower_ref[...]
    upper = upper_ref[...]
    col = lax.broadcasted_iota(jnp.int32, (W, NB), 1)
    top_old = work[:W]
    top = dot(small_left, pack_right(top_old))
    live_col = (col >= W) & (col < active)
    top_live = jnp.where(live_col, top, 0.0)
    lower_top = dot(small_left, pack_right(lower[:W]))

    row = lax.broadcasted_iota(jnp.int32, (NB, 128), 0)
    live_row = (row >= W) & (row < active)
    left_old = work[:, :128]
    left = dot(pack_left(repeat_lanes(left_old, 0)), small_upper)[:, :128]
    left_live = jnp.where(live_row, left, 0.0)
    upper_left = dot(pack_left(repeat_lanes(upper[:, :128], 0)), small_upper)[:, :128]

    left_packed = pack_left(left_live)
    top_packed = pack_right(top_live)
    work_new = work - dot(left_packed, top_packed)
    lower_new = lower - dot(left_packed, pack_right(lower_top))
    upper_new = upper - dot(pack_left(upper_left), top_packed)

    lane = lax.broadcasted_iota(jnp.int32, (NB, 128), 1)
    left_side = jnp.where((lane < W) & live_row, left, work_new[:, :128])
    work_new = jnp.concatenate([left_side, work_new[:, 128:]], axis=1)
    packed_wide = jnp.concatenate([packed, jnp.zeros_like(packed)], axis=1)
    top_new = jnp.where(col < W, packed_wide, jnp.where(live_col, top, top_old))
    work_new = jnp.concatenate([work_new[W:], top_new], axis=0)
    work_ref[...] = pltpu.roll(work_new, NB - W, 1)
    lower_ref[...] = jnp.concatenate([lower_new[W:], lower_top], axis=0)
    upper_side = jnp.where(lane < W, upper_left, upper_new[:, :128])
    upper_ref[...] = pltpu.roll(
        jnp.concatenate([upper_side, upper_new[:, 128:]], axis=1), NB - W, 1
    )


def identity():
    row = lax.broadcasted_iota(jnp.int32, (NB, NB), 0)
    col = lax.broadcasted_iota(jnp.int32, (NB, NB), 1)
    return jnp.where(row == col, 1.0, 0.0).astype(jnp.float32)


def times_right(a, b):
    high, middle, low = split3(b)
    return dot(a, high) + (dot(a, middle) + dot(a, low))


def times_left(a, b):
    high, middle, low = split3(a)
    return dot(high, b) + (dot(middle, b) + dot(low, b))


def run_steps(first, count, work_ref, lower_ref, upper_ref):
    def body(k, carry):
        block_step(k, work_ref, lower_ref, upper_ref)
        return carry

    lax.fori_loop(first, first + count, body, 0)


def pick(place_ref, blocks, i, j):
    same_row = place_ref[0] % 2 == i
    same_col = place_ref[1] % 2 == j
    own, across, below, both = [block[...].astype(jnp.float32) for block in blocks]
    near = jnp.where(same_col, own, across)
    far = jnp.where(same_col, below, both)
    return jnp.where(same_row, near, far)


def first_kernel(count, n_extra, place_ref, d0, d1, d2, d3, *refs):
    work_ref, lower_ref, upper_ref = refs[n_extra:]
    work_ref[...] = pick(place_ref, (d0, d1, d2, d3), 0, 0)
    lower_ref[...] = identity()
    upper_ref[...] = identity()
    run_steps(0, count, work_ref, lower_ref, upper_ref)


def second_kernel(count, n_extra, place_ref, d0, d1, d2, d3, inv_lower, inv_upper, *refs):
    work_ref, lower_ref, upper_ref, left_ref, top_ref = refs[n_extra:]
    blocks = (d0, d1, d2, d3)
    left = times_right(pick(place_ref, blocks, 1, 0).astype(jnp.bfloat16), inv_upper[...])
    left = left.astype(jnp.bfloat16)
    top = times_left(inv_lower[...], pick(place_ref, blocks, 0, 1).astype(jnp.bfloat16))
    top = top.astype(jnp.bfloat16)
    left_ref[...] = left
    top_ref[...] = top
    block = pick(place_ref, blocks, 1, 1) - dot(left, top)
    work_ref[...] = block.astype(jnp.bfloat16).astype(jnp.float32)
    lower_ref[...] = identity()
    upper_ref[...] = identity()
    run_steps(0, count, work_ref, lower_ref, upper_ref)


def next_kernel(first, count, n_extra, work_in, lower_in, upper_in, *refs):
    work_ref, lower_ref, upper_ref = refs[n_extra:]
    work_ref[...] = work_in[...]
    lower_ref[...] = lower_in[...]
    upper_ref[...] = upper_in[...]
    run_steps(first, count, work_ref, lower_ref, upper_ref)


def vmem():
    return pl.BlockSpec(memory_space=pltpu.VMEM)


def smem():
    return pl.BlockSpec(memory_space=pltpu.SMEM)


def anywhere():
    return pl.BlockSpec(memory_space=pl.ANY)


def factor_call(body, n_out, place, operands, extra, flops):
    square = jax.ShapeDtypeStruct((NB, NB), jnp.float32)
    panel = jax.ShapeDtypeStruct((NB, NB), jnp.bfloat16)
    scalars = [] if place is None else [place]
    return pl.pallas_call(
        body,
        out_shape=[square] * 3 + [panel] * (n_out - 3),
        in_specs=[smem() for _ in scalars] + [vmem() for _ in operands] + [anywhere() for _ in extra],
        out_specs=[vmem()] * n_out,
        compiler_params=pltpu.CompilerParams(vmem_limit_bytes=LIMIT),
        cost_estimate=pl.CostEstimate(flops=flops, bytes_accessed=2**21, transcendentals=0),
    )(*scalars, *operands, *extra)


def left_kernel(place_ref, own, other, inv_first, inv_second, top, out):
    parity = place_ref[1] % 2
    own_value = own[...].astype(jnp.float32)
    other_value = other[...].astype(jnp.float32)
    first = jnp.where(parity == 0, own_value, other_value).astype(jnp.bfloat16)
    second = jnp.where(parity == 0, other_value, own_value)
    rows = lax.broadcasted_iota(jnp.int32, (own.shape[0], NB), 0)
    outer = (rows >= NB) | (pl.program_id(0) > 0)
    left = times_right(first, inv_first[...])
    left = jnp.where(outer | (place_ref[0] > 0), left, 0.0).astype(jnp.bfloat16)
    out[:, :NB] = left
    second = (second - dot(left, top[...])).astype(jnp.bfloat16)
    left = times_right(second, inv_second[...])
    left = jnp.where(outer | (place_ref[0] > 1), left, 0.0).astype(jnp.bfloat16)
    out[:, NB:] = left


def left_call(place, own, other, inv_first, inv_second, top):
    rows = own.shape[0]
    tile = rows // 4
    whole = pl.BlockSpec((NB, NB), lambda i: (0, 0))
    return pl.pallas_call(
        left_kernel,
        grid=(4,),
        out_shape=jax.ShapeDtypeStruct((rows, 2 * NB), jnp.bfloat16),
        in_specs=[
            smem(),
            pl.BlockSpec((tile, NB), lambda i: (i, 0)),
            pl.BlockSpec((tile, NB), lambda i: (i, 0)),
            whole,
            whole,
            whole,
        ],
        out_specs=pl.BlockSpec((tile, 2 * NB), lambda i: (i, 0)),
        compiler_params=pltpu.CompilerParams(vmem_limit_bytes=LIMIT),
        cost_estimate=pl.CostEstimate(
            flops=14 * rows * NB * NB, bytes_accessed=8 * rows * NB, transcendentals=0
        ),
    )(place, own, other, inv_first, inv_second, top)


def update_kernel(first, count, lines, n_extra, place_ref, matrix, left_ref, packed_first,
                  packed_second, inv_first, inv_second, left_block, *refs):
    n_sent = count + DELAY * (lines - 1)
    own = refs[:n_sent]
    other = refs[n_sent : 2 * n_sent]
    out, raw, top_ref, sems = refs[2 * n_sent + n_extra :]
    j = pl.program_id(0)
    i = pl.program_id(1)
    grid_row = place_ref[0]
    grid_col = place_ref[1]
    line = grid_row // 2
    parity = grid_row % 2
    tile, width = out.shape

    @pl.when((i == 0) & (j == 0))
    def _():
        for c in range(count):
            for k in range(lines):
                @pl.when(line == k)
                def _():
                    s = c + DELAY * k
                    pltpu.make_async_copy(own[s], raw.at[parity, c], sems.at[0, c]).start()
                    pltpu.make_async_copy(other[s], raw.at[1 - parity, c], sems.at[1, c]).start()

    @pl.when(i == 0)
    def _():
        pltpu.make_async_copy(own[0], raw.at[parity, j], sems.at[0, j]).wait()
        pltpu.make_async_copy(other[0], raw.at[1 - parity, j], sems.at[1, j]).wait()
        cols = lax.broadcasted_iota(jnp.int32, (NB, width), 1)
        outer = (cols >= NB) | (first + j > 0)
        top = times_left(inv_first[...], raw[0, j])
        top = jnp.where(outer | (grid_col > 0), top, 0.0).astype(jnp.bfloat16)
        top_ref[:NB, :] = top
        second = raw[1, j].astype(jnp.float32) - dot(left_block[...], top)
        top = times_left(inv_second[...], second.astype(jnp.bfloat16))
        top = jnp.where(outer | (grid_col > 1), top, 0.0).astype(jnp.bfloat16)
        top_ref[NB:, :] = top

    rows = pl.ds(pl.multiple_of(i * tile, tile), tile)
    for start in range(0, width, NB):
        cols = slice(start, start + NB)
        value = matrix[:, cols].astype(jnp.float32)
        value = value - dot(left_ref[rows, :NB], top_ref[:NB, cols])
        value = value.astype(jnp.bfloat16).astype(jnp.float32)
        value = value - dot(left_ref[rows, NB:], top_ref[NB:, cols])
        out[:, cols] = value.astype(jnp.bfloat16)

    @pl.when((i == 0) & (grid_row == 0))
    def _():
        out[:NB, :] = top_ref[:NB, :]

    @pl.when((i == 0) & (grid_row == 1))
    def _():
        out[:NB, :] = top_ref[NB:, :]

    if first == 0:
        @pl.when((j == 0) & (grid_col == 0))
        def _():
            out[:, :NB] = left_ref[rows, :NB]

        @pl.when((j == 0) & (grid_col == 1))
        def _():
            out[:, :NB] = left_ref[rows, NB:]

        @pl.when((j == 0) & (i == 0) & (grid_col == 0) & (grid_row == 0))
        def _():
            out[:NB, :NB] = packed_first[...].astype(jnp.bfloat16)

        @pl.when((j == 0) & (i == 0) & (grid_col == 1) & (grid_row == 0))
        def _():
            out[:NB, :NB] = top_ref[:NB, :NB]

        @pl.when((j == 0) & (i == 0) & (grid_col == 1) & (grid_row == 1))
        def _():
            out[:NB, :NB] = packed_second[...].astype(jnp.bfloat16)


def update_call(first, last, lines, place, matrix, left, squares, left_block, own, other, extra, before):
    rows, cols = matrix.shape
    width = cols // CHUNKS
    tile = rows // 4
    count = last - first
    tail = list(extra) + ([] if before is None else [before])
    whole = pl.BlockSpec((NB, NB), lambda j, i: (0, 0))
    big = pl.BlockSpec((tile, width), lambda j, i: (i, j + first))
    operands = [place, matrix, left, *squares, left_block, *own, *other, *tail]
    aliases = {} if before is None else {len(operands) - 1: 0}
    return pl.pallas_call(
        functools.partial(update_kernel, first, count, lines, len(tail)),
        grid=(count, 4),
        out_shape=jax.ShapeDtypeStruct((rows, cols), jnp.bfloat16),
        in_specs=[smem(), big, pl.BlockSpec((rows, 2 * NB), lambda j, i: (0, 0))]
        + [whole] * 5
        + [anywhere() for _ in range(len(own) + len(other) + len(tail))],
        out_specs=big,
        scratch_shapes=[
            pltpu.VMEM((2, count, NB, width), jnp.bfloat16),
            pltpu.VMEM((2 * NB, width), jnp.bfloat16),
            pltpu.SemaphoreType.DMA((2, count)),
        ],
        input_output_aliases=aliases,
        compiler_params=pltpu.CompilerParams(vmem_limit_bytes=LIMIT),
        cost_estimate=pl.CostEstimate(
            flops=4 * rows * NB * width * count,
            bytes_accessed=4 * rows * width * count,
            transcendentals=0,
        ),
    )(*operands)


def swap(size):
    return [(i, i ^ 1) for i in range(size)]


def spread(block, axis, size, index):
    stride = size // 2
    while stride >= 2:
        pairs = [(i, i + stride) for i in range(size) if i % (2 * stride) < 2]
        moved = lax.ppermute(block, axis, pairs)
        block = jnp.where(index % (2 * stride) >= stride, moved, block)
        stride //= 2
    return block


def on_device(matrix):
    grid_rows = lax.axis_size("row")
    grid_cols = lax.axis_size("col")
    grid_row = lax.axis_index("row")
    grid_col = lax.axis_index("col")
    place = jnp.stack([grid_row, grid_col]).astype(jnp.int32)
    lines = grid_rows // 2
    width = matrix.shape[1] // CHUNKS

    diag = spread(matrix[:NB, :NB], "col", grid_cols, grid_col)
    diag = spread(diag, "row", grid_rows, grid_row)
    both_swap = [
        (i * grid_cols + j, (i ^ 1) * grid_cols + (j ^ 1))
        for i in range(grid_rows)
        for j in range(grid_cols)
    ]
    blocks = (
        diag,
        lax.ppermute(diag, "col", swap(grid_cols)),
        lax.ppermute(diag, "row", swap(grid_rows)),
        lax.ppermute(diag, ("row", "col"), both_swap),
    )

    column = spread(matrix[:, :NB], "col", grid_cols, grid_col)
    column_other = lax.ppermute(column, "col", swap(grid_cols))

    n_steps = CHUNKS + DELAY * (lines - 1)
    own, other, received = [], [], []
    for t in range(n_steps):
        if t < CHUNKS:
            send = matrix[:NB, t * width : (t + 1) * width]
            if t >= DELAY:
                send = jnp.where(grid_row < 2, send, received[t - DELAY])
        else:
            send = received[t - DELAY]
        live = [k for k in range(lines) if 0 <= t - DELAY * k < CHUNKS]
        onward = [(2 * k + e, 2 * k + 2 + e) for k in live for e in range(2) if k + 1 < lines]
        across = [(2 * k + e, 2 * k + 1 - e) for k in live for e in range(2)]
        own.append(send)
        received.append(lax.ppermute(send, "row", onward) if onward else send)
        other.append(lax.ppermute(send, "row", across))

    def ready(step):
        return own[min(step, n_steps - 1)]

    per_piece = NB // W // PIECES
    cost = 2 * 10**9
    state = factor_call(
        functools.partial(first_kernel, per_piece, 1), 3, place, blocks, [ready(FIRST_PIECE)], cost
    )
    for piece in range(1, PIECES):
        state = factor_call(
            functools.partial(next_kernel, piece * per_piece, per_piece, 1),
            3, None, state, [ready(FIRST_PIECE + piece)], cost,
        )
    packed_first, lower_first, upper_first = state
    *state, left_block, top_block = factor_call(
        functools.partial(second_kernel, per_piece, 1),
        5, place, [*blocks, lower_first, upper_first], [ready(FIRST_PIECE + PIECES)], cost,
    )
    for piece in range(1, PIECES):
        state = factor_call(
            functools.partial(next_kernel, piece * per_piece, per_piece, 1),
            3, None, state, [ready(FIRST_PIECE + PIECES + piece)], cost,
        )
    packed_second, lower_second, upper_second = state

    left = left_call(place, column, column_other, upper_first, upper_second, top_block)
    squares = (packed_first, packed_second, lower_first, lower_second)
    out = None
    for first, last in BATCHES:
        end = last + DELAY * (lines - 1)
        out = update_call(
            first, last, lines, place, matrix, left, squares, left_block,
            own[first:end], other[first:end], [ready(end)], out,
        )
    return out


def solution(mesh):
    return jax.shard_map(
        on_device, mesh=mesh, in_specs=(P("row", "col"),), out_specs=P("row", "col"), check_vma=False
    )
```

time: 2630 us -> 279 us (0.11)
  the two profiles are of different devices: /device:TPU:24 before, /device:TPU:0 now
where the time goes in v1:
time: 279 us; the launch traced here: 276 us
  Pallas kernels  155 us (56%)
  starting transfers between devices  88.8 us (32%)
  other arithmetic  12.4 us (4%)
  waiting for transfers between devices  11.8 us (4%)
  local copies, waits for them, and re-layouts  7.12 us (3%)
    pallas_call x5, Pallas kernels, update_call(): pl.pallas_call(functools.partial(update_kernel, first, count, lines, len(...  95 us
    pallas_call x8, Pallas kernels, factor_call(): pl.pallas_call(body, out_shape=[square] * 3 + [panel] * (n_out - 3), in_s...  50.7 us
    ppermute x18, starting transfers between devices, on_device(): received.append(lax.ppermute(send, 'row', onward) if onward else send)  42.7 us
    ppermute x20, starting transfers between devices, on_device(): other.append(lax.ppermute(send, 'row', across))  31.9 us
    ppermute x4, starting transfers between devices, spread(): moved = lax.ppermute(block, axis, pairs)  12 us
    pallas_call x1, Pallas kernels, left_call(): pl.pallas_call(left_kernel, grid=(4,), out_shape=jax.ShapeDtypeStruct((ro...  9.31 us
    ppermute x20, waiting for transfers between devices, on_device(): other.append(lax.ppermute(send, 'row', across))  9.24 us
    select_n x8, other arithmetic, on_device(): send = jnp.where(grid_row < 2, send, received[t - DELAY])  9.07 us
  transfers between devices with their start and end apart: 46, of which 6 were waited for; matrix products, arithmetic and copies ran while one was open for 5% of the time, Pallas kernels for 51%

profile of v1, /device:TPU:0, one launch (start us, length us, event | category | flops | bytes accessed | tf_op | source)
XLA Modules:
  0.0 276.4 jit_solution(10985092271207046892)
XLA Ops:
  1.0 4.9 %collective-permute-start.10 = (bf16[256,512]{1,0:T(8,128)(2,1)S(1)}, bf16[256,512]{1,0:T(8,128)(2,1)S(1)}, u32[]{:S(2)}, u32[]{:S(2)}) collective-permute-start(bf16[256,512]{1,0:T(8,128)(2,1)S(1)} %slice.55.refs_1_), channel_id=1, source_target_pairs={{0,8},{4,12},{1,9},{5,13},{2,10},{6,14},{3,11},{7,15}} | collective-permute-start | bytes 786440 | tf_op jit(solution)/shard_map/ppermute | solution.py:426
  6.9 3.4 %collective-permute-start.2 = (bf16[256,256]{1,0:T(8,128)(2,1)S(1)}, bf16[256,256]{1,0:T(8,128)(2,1)S(1)}, u32[]{:S(2)}, u32[]{:S(2)}) collective-permute-start(bf16[256,256]{1,0:T(8,128)(2,1)S(1)} %slice.49), channel_id=1, source_target_pairs={{0,2},{1,3},{4,6},{5,7},{8,10},{9,11},{12,14},{13,15},{16,18},{17,... | collective-permute-start | bytes 393224 | tf_op jit(solution)/shard_map/ppermute | solution.py:381
  12.5 4.4 %collective-permute-start.11 = (bf16[256,512]{1,0:T(8,128)(2,1)S(1)}, bf16[256,512]{1,0:T(8,128)(2,1)S(1)}, u32[]{:S(2)}, u32[]{:S(2)}) collective-permute-start(bf16[256,512]{1,0:T(8,128)(2,1)S(1)} %slice_select_fusion.8.refs_3_), channel_id=1, source_target_pairs={{0,8},{4,12},{8,16},{12,20},{1,9},{5,13},{9,17},{13,21},{2,10},{6,... | collective-permute-start | bytes 786440 | tf_op jit(solution)/shard_map/ppermute | solution.py:426
  16.9 1.6 slice.48
  18.5 4.6 %collective-permute-start = (bf16[3584,256]{1,0:T(8,128)(2,1)S(1)}, bf16[3584,256]{1,0:T(8,128)(2,1)}, u32[]{:S(2)}, u32[]{:S(2)}) collective-permute-start(bf16[3584,256]{1,0:T(8,128)(2,1)S(1)} %slice.48), channel_id=1, source_target_pairs={{0,2},{1,3},{4,6},{5,7},{8,10},{9,11},{12,14},{13,15},{16,18},{17,... | collective-permute-start | bytes 5505032 | tf_op jit(solution)/shard_map/ppermute | solution.py:381
  24.0 2.0 collective-permute-start.3
  27.1 2.0 collective-permute-start.8
  29.1 3.4 %collective-permute-start.43 = (bf16[256,512]{1,0:T(8,128)(2,1)S(1)}, bf16[256,512]{1,0:T(8,128)(2,1)S(1)}, u32[]{:S(2)}, u32[]{:S(2)}) collective-permute-start(bf16[256,512]{1,0:T(8,128)(2,1)S(1)} %slice.55.refs_1_), channel_id=1, source_target_pairs={{0,4},{4,0},{1,5},{5,1},{2,6},{6,2},{3,7},{7,3}} | collective-permute-start | bytes 786440 | tf_op jit(solution)/shard_map/ppermute | solution.py:427
  32.6 2.0 collective-permute-start.4
  35.6 5.1 %collective-permute-start.9 = (bf16[256,512]{1,0:T(8,128)(2,1)S(1)}, bf16[256,512]{1,0:T(8,128)(2,1)}, u32[]{:S(2)}, u32[]{:S(2)}) collective-permute-start(bf16[256,512]{1,0:T(8,128)(2,1)S(1)} %slice_select_fusion.10.refs_2_), channel_id=1, source_target_pairs={{0,8},{4,12},{8,16},{12,20},{1,9},{5,13},{9,17},{13,21},{2,10},{6,... | collective-permute-start | bytes 786440 | tf_op jit(solution)/shard_map/ppermute | solution.py:426
  41.5 2.0 collective-permute-start.6
  43.8 1.7 slice_select_fusion.11.refs_0_.refs_4_
  45.5 3.9 %collective-permute-start.45 = (bf16[256,512]{1,0:T(8,128)(2,1)S(1)}, bf16[256,512]{1,0:T(8,128)(2,1)S(1)}, u32[]{:S(2)}, u32[]{:S(2)}) collective-permute-start(bf16[256,512]{1,0:T(8,128)(2,1)S(1)} %slice_select_fusion.8.refs_3_), channel_id=1, source_target_pairs={{0,4},{4,0},{8,12},{12,8},{1,5},{5,1},{9,13},{13,9},{2,6},{6,2},{1... | collective-permute-start | bytes 786440 | tf_op jit(solution)/shard_map/ppermute | solution.py:427
  49.4 4.6 %collective-permute-start.13 = (bf16[256,512]{1,0:T(8,128)(2,1)S(1)}, bf16[256,512]{1,0:T(8,128)(2,1)S(1)}, u32[]{:S(2)}, u32[]{:S(2)}) collective-permute-start(bf16[256,512]{1,0:T(8,128)(2,1)S(1)} %get-tuple-element.65.refs_0_.refs_5_.refs_1_), channel_id=1, source_target_pairs={{0,8},{4,12},{8,16},{12,20},{16,24},{20,28},{1,9},{5,13},{9,17},{1... | collective-permute-start | bytes 786440 | tf_op jit(solution)/shard_map/ppermute | solution.py:426
  54.0 1.9 collective-permute-start.12
  56.0 6.2 %shard_map.17 = (f32[256,256]{1,0:T(8,128)}, f32[256,256]{1,0:T(8,128)}, f32[256,256]{1,0:T(8,128)}) custom-call(s32[2]{0:T(128)} %pad_add_fusion.place_ref, bf16[256,256]{1,0:T(8,128)(2,1)} %copy-done.40, bf16[256,256]{1,0:T(8,128)(2,1)} %copy-done.41, bf16[256,256]{1,0:T(8,128)(2,1)} %copy-done.42, bf16[256,256]{1,0:T(8,128)(2,1)} %copy-done.43, ...), custom_call_target="tpu_custom_call" | custom-call | flops 2000000000 | bytes 2097152 | tf_op jit(solution)/shard_map/pallas_call | solution.py:212
  62.2 6.2 %shard_map.18 = (f32[256,256]{1,0:T(8,128)}, f32[256,256]{1,0:T(8,128)}, f32[256,256]{1,0:T(8,128)}) custom-call(f32[256,256]{1,0:T(8,128)} %get-tuple-element.31.work_in, f32[256,256]{1,0:T(8,128)} %get-tuple-element.32.lower_in, f32[256,256]{1,0:T(8,128)} %get-tuple-element.33.upper_in, bf16[256,512]{1,0:T(8,128)(2,1)} %copy-done.19), custom_call_target="tpu_custom_call" | custom-call | flops 2000000000 | bytes 2097152 | tf_op jit(solution)/shard_map/pallas_call | solution.py:212
  69.5 1.9 collective-permute-start.15
  71.4 1.9 collective-permute-start.14
  73.3 1.7 broadcast_select_fusion.own
  75.1 6.7 %shard_map.19 = (f32[256,256]{1,0:T(8,128)}, f32[256,256]{1,0:T(8,128)}, f32[256,256]{1,0:T(8,128)}) custom-call(f32[256,256]{1,0:T(8,128)} %get-tuple-element.34.work_in, f32[256,256]{1,0:T(8,128)} %get-tuple-element.35.lower_in, f32[256,256]{1,0:T(8,128)} %get-tuple-element.36.upper_in, bf16[256,512]{1,0:T(8,128)(2,1)} %copy-done.20), custom_call_target="tpu_custom_call" | custom-call | flops 2000000000 | bytes 2097152 | tf_op jit(solution)/shard_map/pallas_call | solution.py:212
  83.9 4.4 %collective-permute-start.16 = (bf16[256,512]{1,0:T(8,128)(2,1)S(1)}, bf16[256,512]{1,0:T(8,128)(2,1)S(1)}, u32[]{:S(2)}, u32[]{:S(2)}) collective-permute-start(bf16[256,512]{1,0:T(8,128)(2,1)S(1)} %get-tuple-element.62.refs_0_.refs_8_.refs_4_.refs_1_), channel_id=1, source_target_pairs={{0,8},{4,12},{8,16},{12,20},{16,24},{20,28},{1,9},{5,13},{9,17},{1... | collective-permute-start | bytes 786440 | tf_op jit(solution)/shard_map/ppermute | solution.py:426
  88.4 2.2 collective-permute-start.17
  90.6 6.2 %shard_map.20 = (f32[256,256]{1,0:T(8,128)}, f32[256,256]{1,0:T(8,128)}, f32[256,256]{1,0:T(8,128)}) custom-call(f32[256,256]{1,0:T(8,128)} %get-tuple-element.37.work_in, f32[256,256]{1,0:T(8,128)} %get-tuple-element.38.lower_in, f32[256,256]{1,0:T(8,128)} %get-tuple-element.39.upper_in, bf16[256,512]{1,0:T(8,128)(2,1)} %copy-done.4), custom_call_target="tpu_custom_call" | custom-call | flops 2000000000 | bytes 2097152 | tf_op jit(solution)/shard_map/pallas_call | solution.py:212
  96.7 7.0 %shard_map.21 = (f32[256,256]{1,0:T(8,128)}, f32[256,256]{1,0:T(8,128)}, f32[256,256]{1,0:T(8,128)}, bf16[256,256]{1,0:T(8,128)(2,1)}, bf16[256,256]{1,0:T(8,128)(2,1)}) custom-call(s32[2]{0:T(128)} %pad_add_fusion.place_ref, bf16[256,256]{1,0:T(8,128)(2,1)} %copy-done.40, bf16[256,256]{1,0:T(8,128)(2,1)} %copy-done.41, bf16[256,256]{1,0:T(8,128)(2,1)} %copy-done.42, ...), custom_call_target="tpu_custom_call" | custom-call | flops 2000000000 | bytes 2097152 | tf_op jit(solution)/shard_map/pallas_call | solution.py:212
  103.7 1.9 collective-permute-start.40
  106.8 1.9 collective-permute-start.18
  108.7 2.1 collective-permute-start.19
  110.9 6.2 %shard_map.22 = (f32[256,256]{1,0:T(8,128)}, f32[256,256]{1,0:T(8,128)}, f32[256,256]{1,0:T(8,128)}) custom-call(f32[256,256]{1,0:T(8,128)} %get-tuple-element.42.work_in, f32[256,256]{1,0:T(8,128)} %get-tuple-element.43.lower_in, f32[256,256]{1,0:T(8,128)} %get-tuple-element.44.upper_in, bf16[256,512]{1,0:T(8,128)(2,1)} %copy-done.5), custom_call_target="tpu_custom_call" | custom-call | flops 2000000000 | bytes 2097152 | tf_op jit(solution)/shard_map/pallas_call | solution.py:212
  117.0 6.1 %shard_map.23 = (f32[256,256]{1,0:T(8,128)}, f32[256,256]{1,0:T(8,128)}, f32[256,256]{1,0:T(8,128)}) custom-call(f32[256,256]{1,0:T(8,128)} %get-tuple-element.45.work_in, f32[256,256]{1,0:T(8,128)} %get-tuple-element.46.lower_in, f32[256,256]{1,0:T(8,128)} %get-tuple-element.47.upper_in, bf16[256,512]{1,0:T(8,128)(2,1)} %copy-done), custom_call_target="tpu_custom_call" | custom-call | flops 2000000000 | bytes 2097152 | tf_op jit(solution)/shard_map/pallas_call | solution.py:212
  123.2 3.9 %collective-permute-start.42 = (bf16[256,512]{1,0:T(8,128)(2,1)S(1)}, bf16[256,512]{1,0:T(8,128)(2,1)S(1)}, u32[]{:S(2)}, u32[]{:S(2)}) collective-permute-start(bf16[256,512]{1,0:T(8,128)(2,1)S(1)} %get-tuple-element.66.refs_0_), channel_id=1, source_target_pairs={{0,4},{4,0},{1,5},{5,1},{2,6},{6,2},{3,7},{7,3}} | collective-permute-start | bytes 786440 | tf_op jit(solution)/shard_map/ppermute | solution.py:427
  127.1 1.9 collective-permute-start.44
  129.1 3.9 %collective-permute-start.39 = (bf16[256,512]{1,0:T(8,128)(2,1)}, bf16[256,512]{1,0:T(8,128)(2,1)S(1)}, u32[]{:S(2)}, u32[]{:S(2)}) collective-permute-start(bf16[256,512]{1,0:T(8,128)(2,1)} %slice_select_fusion.11.refs_0_.refs_4_), channel_id=1, source_target_pairs={{0,4},{4,0},{8,12},{12,8},{16,20},{20,16},{1,5},{5,1},{9,13},{13,9... | collective-permute-start | bytes 786440 | tf_op jit(solution)/shard_map/ppermute | solution.py:427
  133.1 6.1 %shard_map.24 = (f32[256,256]{1,0:T(8,128)}, f32[256,256]{1,0:T(8,128)}, f32[256,256]{1,0:T(8,128)}) custom-call(f32[256,256]{1,0:T(8,128)} %get-tuple-element.48.work_in, f32[256,256]{1,0:T(8,128)} %get-tuple-element.49.lower_in, f32[256,256]{1,0:T(8,128)} %get-tuple-element.50.upper_in, bf16[256,512]{1,0:T(8,128)(2,1)} %copy-done.7), custom_call_target="tpu_custom_call" | custom-call | flops 2000000000 | bytes 2097152 | tf_op jit(solution)/shard_map/pallas_call | solution.py:212
  140.4 2.1 collective-permute-start.41
  142.5 3.0 %collective-permute-done.39.refs_14_.refs_9_ = bf16[256,512]{1,0:T(8,128)(2,1)S(1)} collective-permute-done((bf16[256,512]{1,0:T(8,128)(2,1)}, bf16[256,512]{1,0:T(8,128)(2,1)S(1)}, u32[]{:S(2)}, u32[]{:S(2)}) %collective-permute-start.39) | collective-permute-done | bytes 262176 | tf_op jit(solution)/shard_map/ppermute | solution.py:427
  145.5 2.1 collective-permute-start.38
  147.6 3.6 %collective-permute-done.36.refs_17_.refs_12_.refs_9_ = bf16[256,512]{1,0:T(8,128)(2,1)S(1)} collective-permute-done((bf16[256,512]{1,0:T(8,128)(2,1)}, bf16[256,512]{1,0:T(8,128)(2,1)S(1)}, u32[]{:S(2)}, u32[]{:S(2)}) %collective-permute-start.36) | collective-permute-done | bytes 262176 | tf_op jit(solution)/shard_map/ppermute | solution.py:427
  152.4 1.3 collective-permute-start.21
  153.7 9.3 %shard_map.25.left_ref = bf16[3584,512]{1,0:T(8,128)(2,1)} custom-call(s32[2]{0:T(128)} %pad_add_fusion.place_ref, bf16[3584,256]{1,0:T(8,128)(2,1)} %copy-done.21, bf16[3584,256]{1,0:T(8,128)(2,1)} %collective-permute-done.1.other, f32[256,256]{1,0:T(8,128)} %get-tuple-element.40.inv_upper.inv_first, f32[256,256]{1,0:T(8,128)} %get-tuple-element.51.inv_second, ...), custom_call_target="tpu_custom_call" | custom-call | flops 3288334336 | bytes 7340032 | tf_op jit(solution)/shard_map/pallas_call | solution.py:243
  163.1 2.1 collective-permute-start.34
  165.3 2.7 collective-permute-done.38.refs_19_.refs_14_.refs_11_
  168.0 2.1 collective-permute-start.26
  171.5 25.8 %shard_map.26.refs_19_ = bf16[3584,7168]{1,0:T(8,128)(2,1)} custom-call(s32[2]{0:T(128)} %pad_add_fusion.place_ref, bf16[3584,7168]{1,0:T(8,128)(2,1)} %matrix.9, bf16[3584,512]{1,0:T(8,128)(2,1)} %shard_map.25.left_ref, f32[256,256]{1,0:T(8,128)} %get-tuple-element.53.packed_first, f32[256,256]{1,0:T(8,128)} %get-tuple-element.54.packed_second, ...), custom_call_target="tpu_custom_call" | custom-call | flops 7516192768 | bytes 29360128 | tf_op jit(solution)/shard_map/pallas_call | solution.py:350
  200.3 20.0 %shard_map.27.refs_19_ = bf16[3584,7168]{1,0:T(8,128)(2,1)} custom-call(s32[2]{0:T(128)} %pad_add_fusion.place_ref, bf16[3584,7168]{1,0:T(8,128)(2,1)} %matrix.9, bf16[3584,512]{1,0:T(8,128)(2,1)} %shard_map.25.left_ref, f32[256,256]{1,0:T(8,128)} %get-tuple-element.53.packed_first, ...), custom_call_target="tpu_custom_call", output_to_operand_aliasing={{}: (27, {})} | custom-call | flops 5637144576 | bytes 22020096 | tf_op jit(solution)/shard_map/pallas_call | solution.py:350
  224.1 19.9 %shard_map.28.refs_17_ = bf16[3584,7168]{1,0:T(8,128)(2,1)} custom-call(s32[2]{0:T(128)} %pad_add_fusion.place_ref, bf16[3584,7168]{1,0:T(8,128)(2,1)} %matrix.9, bf16[3584,512]{1,0:T(8,128)(2,1)} %shard_map.25.left_ref, f32[256,256]{1,0:T(8,128)} %get-tuple-element.53.packed_first, ...), custom_call_target="tpu_custom_call", output_to_operand_aliasing={{}: (27, {})} | custom-call | flops 5637144576 | bytes 22020096 | tf_op jit(solution)/shard_map/pallas_call | solution.py:350
  245.5 14.6 %shard_map.29.refs_17_ = bf16[3584,7168]{1,0:T(8,128)(2,1)} custom-call(s32[2]{0:T(128)} %pad_add_fusion.place_ref, bf16[3584,7168]{1,0:T(8,128)(2,1)} %matrix.9, bf16[3584,512]{1,0:T(8,128)(2,1)} %shard_map.25.left_ref, f32[256,256]{1,0:T(8,128)} %get-tuple-element.53.packed_first, ...), custom_call_target="tpu_custom_call", output_to_operand_aliasing={{}: (25, {})} | custom-call | flops 3758096384 | bytes 14680064 | tf_op jit(solution)/shard_map/pallas_call | solution.py:350
  261.5 14.6 %shard_map.30 = bf16[3584,7168]{1,0:T(8,128)(2,1)} custom-call(s32[2]{0:T(128)} %pad_add_fusion.place_ref, bf16[3584,7168]{1,0:T(8,128)(2,1)} %matrix.9, bf16[3584,512]{1,0:T(8,128)(2,1)} %shard_map.25.left_ref, f32[256,256]{1,0:T(8,128)} %get-tuple-element.53.packed_first, ...), custom_call_target="tpu_custom_call", output_to_operand_aliasing={{}: (25, {})} | custom-call | flops 3758096384 | bytes 14680064 | tf_op jit(solution)/shard_map/pallas_call | solution.py:350
  (162 shorter events, 25.9 us)
Async XLA Ops:
  1.0 170.4 %copy-start.31 = (bf16[256,512]{1,0:T(8,128)(2,1)}, bf16[256,512]{1,0:T(8,128)(2,1)S(1)}, u32[]{:S(2)}) copy-start(bf16[256,512]{1,0:T(8,128)(2,1)S(1)} %slice.55.refs_1_) | copy-start | bytes 786436
  1.0 10.5 %collective-permute-start.10 = (bf16[256,512]{1,0:T(8,128)(2,1)S(1)}, bf16[256,512]{1,0:T(8,128)(2,1)S(1)}, u32[]{:S(2)}, u32[]{:S(2)}) collective-permute-start(bf16[256,512]{1,0:T(8,128)(2,1)S(1)} %slice.55.refs_1_), channel_id=1, source_target_pairs={{0,8},{4,12},{1,9},{5,13},{2,10},{6,14},{3,11},{7,15}} | collective-permute-start | bytes 786440 | tf_op jit(solution)/shard_map/ppermute | solution.py:426
  6.9 16.3 %collective-permute-start.2 = (bf16[256,256]{1,0:T(8,128)(2,1)S(1)}, bf16[256,256]{1,0:T(8,128)(2,1)S(1)}, u32[]{:S(2)}, u32[]{:S(2)}) collective-permute-start(bf16[256,256]{1,0:T(8,128)(2,1)S(1)} %slice.49), channel_id=1, source_target_pairs={{0,2},{1,3},{4,6},{5,7},{8,10},{9,11},{12,14},{13,15},{16,18},{17,... | collective-permute-start | bytes 393224 | tf_op jit(solution)/shard_map/ppermute | solution.py:381
  12.4 159.0 %copy-start.32 = (bf16[256,512]{1,0:T(8,128)(2,1)}, bf16[256,512]{1,0:T(8,128)(2,1)S(1)}, u32[]{:S(2)}) copy-start(bf16[256,512]{1,0:T(8,128)(2,1)S(1)} %slice_select_fusion.8.refs_3_) | copy-start | bytes 786436
  12.5 13.6 %collective-permute-start.11 = (bf16[256,512]{1,0:T(8,128)(2,1)S(1)}, bf16[256,512]{1,0:T(8,128)(2,1)S(1)}, u32[]{:S(2)}, u32[]{:S(2)}) collective-permute-start(bf16[256,512]{1,0:T(8,128)(2,1)S(1)} %slice_select_fusion.8.refs_3_), channel_id=1, source_target_pairs={{0,8},{4,12},{8,16},{12,20},{1,9},{5,13},{9,17},{13,21},{2,10},{6,... | collective-permute-start | bytes 786440 | tf_op jit(solution)/shard_map/ppermute | solution.py:426
  18.5 54.8 %collective-permute-start = (bf16[3584,256]{1,0:T(8,128)(2,1)S(1)}, bf16[3584,256]{1,0:T(8,128)(2,1)}, u32[]{:S(2)}, u32[]{:S(2)}) collective-permute-start(bf16[3584,256]{1,0:T(8,128)(2,1)S(1)} %slice.48), channel_id=1, source_target_pairs={{0,2},{1,3},{4,6},{5,7},{8,10},{9,11},{12,14},{13,15},{16,18},{17,... | collective-permute-start | bytes 5505032 | tf_op jit(solution)/shard_map/ppermute | solution.py:381
  24.0 8.5 %collective-permute-start.3 = (bf16[256,256]{1,0:T(8,128)(2,1)S(1)}, bf16[256,256]{1,0:T(8,128)(2,1)}, u32[]{:S(2)}, u32[]{:S(2)}) collective-permute-start(bf16[256,256]{1,0:T(8,128)(2,1)S(1)} %broadcast_select_fusion.1), channel_id=1, source_target_pairs={{0,16},{4,20},{1,17},{5,21},{2,18},{6,22},{3,19},{7,23}} | collective-permute-start | bytes 393224 | tf_op jit(solution)/shard_map/ppermute | solution.py:381
  27.1 7.5 %collective-permute-start.8 = (bf16[256,512]{1,0:T(8,128)(2,1)S(1)}, bf16[256,512]{1,0:T(8,128)(2,1)}, u32[]{:S(2)}, u32[]{:S(2)}) collective-permute-start(bf16[256,512]{1,0:T(8,128)(2,1)S(1)} %get-tuple-element.66.refs_0_), channel_id=1, source_target_pairs={{0,8},{4,12},{1,9},{5,13},{2,10},{6,14},{3,11},{7,15}} | collective-permute-start | bytes 786440 | tf_op jit(solution)/shard_map/ppermute | solution.py:426
  29.1 79.6 %collective-permute-start.43 = (bf16[256,512]{1,0:T(8,128)(2,1)S(1)}, bf16[256,512]{1,0:T(8,128)(2,1)S(1)}, u32[]{:S(2)}, u32[]{:S(2)}) collective-permute-start(bf16[256,512]{1,0:T(8,128)(2,1)S(1)} %slice.55.refs_1_), channel_id=1, source_target_pairs={{0,4},{4,0},{1,5},{5,1},{2,6},{6,2},{3,7},{7,3}} | collective-permute-start | bytes 786440 | tf_op jit(solution)/shard_map/ppermute | solution.py:427
  32.6 8.7 %collective-permute-start.4 = (bf16[256,256]{1,0:T(8,128)(2,1)S(1)}, bf16[256,256]{1,0:T(8,128)(2,1)}, u32[]{:S(2)}, u32[]{:S(2)}) collective-permute-start(bf16[256,256]{1,0:T(8,128)(2,1)S(1)} %broadcast_select_fusion.2), channel_id=1, source_target_pairs={{0,8},{4,12},{16,24},{20,28},{1,9},{5,13},{17,25},{21,29},{2,10},{... | collective-permute-start | bytes 393224 | tf_op jit(solution)/shard_map/ppermute | solution.py:381
  35.6 8.3 %collective-permute-start.9 = (bf16[256,512]{1,0:T(8,128)(2,1)S(1)}, bf16[256,512]{1,0:T(8,128)(2,1)}, u32[]{:S(2)}, u32[]{:S(2)}) collective-permute-start(bf16[256,512]{1,0:T(8,128)(2,1)S(1)} %slice_select_fusion.10.refs_2_), channel_id=1, source_target_pairs={{0,8},{4,12},{8,16},{12,20},{1,9},{5,13},{9,17},{13,21},{2,10},{6,... | collective-permute-start | bytes 786440 | tf_op jit(solution)/shard_map/ppermute | solution.py:426
  41.4 4.1 %collective-permute-start.5 = (bf16[256,256]{1,0:T(8,128)(2,1)S(1)}, bf16[256,256]{1,0:T(8,128)(2,1)S(1)}, u32[]{:S(2)}, u32[]{:S(2)}) collective-permute-start(bf16[256,256]{1,0:T(8,128)(2,1)S(1)} %broadcast_select_fusion.3.d0), channel_id=1, source_target_pairs={{0,1},{1,0},{2,3},{3,2},{4,5},{5,4},{6,7},{7,6},{8,9},{9,8},{10,11... | collective-permute-start | bytes 393224 | tf_op jit(solution)/shard_map/ppermute | solution.py:405
  41.5 7.9 %collective-permute-start.6 = (bf16[256,256]{1,0:T(8,128)(2,1)S(1)}, bf16[256,256]{1,0:T(8,128)(2,1)S(1)}, u32[]{:S(2)}, u32[]{:S(2)}) collective-permute-start(bf16[256,256]{1,0:T(8,128)(2,1)S(1)} %broadcast_select_fusion.3.d0), channel_id=1, source_target_pairs={{0,4},{4,0},{8,12},{12,8},{16,20},{20,16},{24,28},{28,24},{1,5},{5... | collective-permute-start | bytes 393224 | tf_op jit(solution)/shard_map/ppermute | solution.py:406
  43.8 10.2 %collective-permute-start.7 = (bf16[256,256]{1,0:T(8,128)(2,1)S(1)}, bf16[256,256]{1,0:T(8,128)(2,1)S(1)}, u32[]{:S(2)}, u32[]{:S(2)}) collective-permute-start(bf16[256,256]{1,0:T(8,128)(2,1)S(1)} %broadcast_select_fusion.3.d0), channel_id=1, source_target_pairs={{0,5},{1,4},{2,7},{3,6},{4,1},{5,0},{6,3},{7,2},{8,13},{9,12},{10,... | collective-permute-start | bytes 393224 | tf_op jit(solution)/shard_map/ppermute | solution.py:407
  45.5 77.6 %collective-permute-start.45 = (bf16[256,512]{1,0:T(8,128)(2,1)S(1)}, bf16[256,512]{1,0:T(8,128)(2,1)S(1)}, u32[]{:S(2)}, u32[]{:S(2)}) collective-permute-start(bf16[256,512]{1,0:T(8,128)(2,1)S(1)} %slice_select_fusion.8.refs_3_), channel_id=1, source_target_pairs={{0,4},{4,0},{8,12},{12,8},{1,5},{5,1},{9,13},{13,9},{2,6},{6,2},{1... | collective-permute-start | bytes 786440 | tf_op jit(solution)/shard_map/ppermute | solution.py:427
  49.4 18.9 %collective-permute-start.13 = (bf16[256,512]{1,0:T(8,128)(2,1)S(1)}, bf16[256,512]{1,0:T(8,128)(2,1)S(1)}, u32[]{:S(2)}, u32[]{:S(2)}) collective-permute-start(bf16[256,512]{1,0:T(8,128)(2,1)S(1)} %get-tuple-element.65.refs_0_.refs_5_.refs_1_), channel_id=1, source_target_pairs={{0,8},{4,12},{8,16},{12,20},{16,24},{20,28},{1,9},{5,13},{9,17},{1... | collective-permute-start | bytes 786440 | tf_op jit(solution)/shard_map/ppermute | solution.py:426
  54.0 14.3 %collective-permute-start.12 = (bf16[256,512]{1,0:T(8,128)(2,1)}, bf16[256,512]{1,0:T(8,128)(2,1)S(1)}, u32[]{:S(2)}, u32[]{:S(2)}) collective-permute-start(bf16[256,512]{1,0:T(8,128)(2,1)} %slice_select_fusion.11.refs_0_.refs_4_), channel_id=1, source_target_pairs={{0,8},{4,12},{8,16},{12,20},{16,24},{20,28},{1,9},{5,13},{9,17},{1... | collective-permute-start | bytes 786440 | tf_op jit(solution)/shard_map/ppermute | solution.py:426
  69.5 12.4 %collective-permute-start.15 = (bf16[256,512]{1,0:T(8,128)(2,1)S(1)}, bf16[256,512]{1,0:T(8,128)(2,1)S(1)}, u32[]{:S(2)}, u32[]{:S(2)}) collective-permute-start(bf16[256,512]{1,0:T(8,128)(2,1)S(1)} %get-tuple-element.63.refs_0_.refs_7_.refs_3_), channel_id=1, source_target_pairs={{0,8},{4,12},{8,16},{12,20},{16,24},{20,28},{1,9},{5,13},{9,17},{1... | collective-permute-start | bytes 786440 | tf_op jit(solution)/shard_map/ppermute | solution.py:426
  71.4 11.4 %collective-permute-start.14 = (bf16[256,512]{1,0:T(8,128)(2,1)S(1)}, bf16[256,512]{1,0:T(8,128)(2,1)S(1)}, u32[]{:S(2)}, u32[]{:S(2)}) collective-permute-start(bf16[256,512]{1,0:T(8,128)(2,1)S(1)} %get-tuple-element.64.refs_0_.refs_6_.refs_2_), channel_id=1, source_target_pairs={{0,8},{4,12},{8,16},{12,20},{16,24},{20,28},{1,9},{5,13},{9,17},{1... | collective-permute-start | bytes 786440 | tf_op jit(solution)/shard_map/ppermute | solution.py:426
  75.1 77.4 %collective-permute-start.1 = (bf16[3584,256]{1,0:T(8,128)(2,1)S(1)}, bf16[3584,256]{1,0:T(8,128)(2,1)}, u32[]{:S(2)}, u32[]{:S(2)}) collective-permute-start(bf16[3584,256]{1,0:T(8,128)(2,1)S(1)} %broadcast_select_fusion.own), channel_id=1, source_target_pairs={{0,1},{1,0},{2,3},{3,2},{4,5},{5,4},{6,7},{7,6},{8,9},{9,8},{10,11... | collective-permute-start | bytes 5505032 | tf_op jit(solution)/shard_map/ppermute | solution.py:411
  83.9 19.8 %collective-permute-start.16 = (bf16[256,512]{1,0:T(8,128)(2,1)S(1)}, bf16[256,512]{1,0:T(8,128)(2,1)S(1)}, u32[]{:S(2)}, u32[]{:S(2)}) collective-permute-start(bf16[256,512]{1,0:T(8,128)(2,1)S(1)} %get-tuple-element.62.refs_0_.refs_8_.refs_4_.refs_1_), channel_id=1, source_target_pairs={{0,8},{4,12},{8,16},{12,20},{16,24},{20,28},{1,9},{5,13},{9,17},{1... | collective-permute-start | bytes 786440 | tf_op jit(solution)/shard_map/ppermute | solution.py:426
  88.4 17.3 %collective-permute-start.17 = (bf16[256,512]{1,0:T(8,128)(2,1)S(1)}, bf16[256,512]{1,0:T(8,128)(2,1)S(1)}, u32[]{:S(2)}, u32[]{:S(2)}) collective-permute-start(bf16[256,512]{1,0:T(8,128)(2,1)S(1)} %get-tuple-element.61.refs_0_.refs_9_.refs_5_.refs_2_), channel_id=1, source_target_pairs={{0,8},{4,12},{8,16},{12,20},{16,24},{20,28},{1,9},{5,13},{9,17},{1... | collective-permute-start | bytes 786440 | tf_op jit(solution)/shard_map/ppermute | solution.py:426
  103.7 23.4 %collective-permute-start.40 = (bf16[256,512]{1,0:T(8,128)(2,1)}, bf16[256,512]{1,0:T(8,128)(2,1)S(1)}, u32[]{:S(2)}, u32[]{:S(2)}) collective-permute-start(bf16[256,512]{1,0:T(8,128)(2,1)} %copy-done.19), channel_id=1, source_target_pairs={{0,4},{4,0},{8,12},{12,8},{16,20},{20,16},{1,5},{5,1},{9,13},{13,9... | collective-permute-start | bytes 786440 | tf_op jit(solution)/shard_map/ppermute | solution.py:427
  106.8 22.3 %collective-permute-start.18 = (bf16[256,512]{1,0:T(8,128)(2,1)S(1)}, bf16[256,512]{1,0:T(8,128)(2,1)S(1)}, u32[]{:S(2)}, u32[]{:S(2)}) collective-permute-start(bf16[256,512]{1,0:T(8,128)(2,1)S(1)} %get-tuple-element.60.refs_0_.refs_20_.refs_6_.refs_3_), channel_id=1, source_target_pairs={{0,8},{4,12},{8,16},{12,20},{16,24},{20,28},{1,9},{5,13},{9,17},{1... | collective-permute-start | bytes 786440 | tf_op jit(solution)/shard_map/ppermute | solution.py:426
  108.7 24.2 %collective-permute-start.19 = (bf16[256,512]{1,0:T(8,128)(2,1)S(1)}, bf16[256,512]{1,0:T(8,128)(2,1)S(1)}, u32[]{:S(2)}, u32[]{:S(2)}) collective-permute-start(bf16[256,512]{1,0:T(8,128)(2,1)S(1)} %get-tuple-element.59.refs_0_.refs_7_.refs_4_.refs_1_), channel_id=1, source_target_pairs={{0,8},{4,12},{8,16},{12,20},{16,24},{20,28},{1,9},{5,13},{9,17},{1... | collective-permute-start | bytes 786440 | tf_op jit(solution)/shard_map/ppermute | solution.py:426
  123.2 17.2 %collective-permute-start.42 = (bf16[256,512]{1,0:T(8,128)(2,1)S(1)}, bf16[256,512]{1,0:T(8,128)(2,1)S(1)}, u32[]{:S(2)}, u32[]{:S(2)}) collective-permute-start(bf16[256,512]{1,0:T(8,128)(2,1)S(1)} %get-tuple-element.66.refs_0_), channel_id=1, source_target_pairs={{0,4},{4,0},{1,5},{5,1},{2,6},{6,2},{3,7},{7,3}} | collective-permute-start | bytes 786440 | tf_op jit(solution)/shard_map/ppermute | solution.py:427
  127.1 15.3 %collective-permute-start.44 = (bf16[256,512]{1,0:T(8,128)(2,1)S(1)}, bf16[256,512]{1,0:T(8,128)(2,1)S(1)}, u32[]{:S(2)}, u32[]{:S(2)}) collective-permute-start(bf16[256,512]{1,0:T(8,128)(2,1)S(1)} %slice_select_fusion.10.refs_2_), channel_id=1, source_target_pairs={{0,4},{4,0},{8,12},{12,8},{1,5},{5,1},{9,13},{13,9},{2,6},{6,2},{1... | collective-permute-start | bytes 786440 | tf_op jit(solution)/shard_map/ppermute | solution.py:427
  129.1 16.4 %collective-permute-start.39 = (bf16[256,512]{1,0:T(8,128)(2,1)}, bf16[256,512]{1,0:T(8,128)(2,1)S(1)}, u32[]{:S(2)}, u32[]{:S(2)}) collective-permute-start(bf16[256,512]{1,0:T(8,128)(2,1)} %slice_select_fusion.11.refs_0_.refs_4_), channel_id=1, source_target_pairs={{0,4},{4,0},{8,12},{12,8},{16,20},{20,16},{1,5},{5,1},{9,13},{13,9... | collective-permute-start | bytes 786440 | tf_op jit(solution)/shard_map/ppermute | solution.py:427
  133.0 18.1 %collective-permute-start.36 = (bf16[256,512]{1,0:T(8,128)(2,1)}, bf16[256,512]{1,0:T(8,128)(2,1)S(1)}, u32[]{:S(2)}, u32[]{:S(2)}) collective-permute-start(bf16[256,512]{1,0:T(8,128)(2,1)} %copy-done.4), channel_id=1, source_target_pairs={{0,4},{4,0},{8,12},{12,8},{16,20},{20,16},{24,28},{28,24},{1,5},{5... | collective-permute-start | bytes 786440 | tf_op jit(solution)/shard_map/ppermute | solution.py:427
  140.4 22.7 %collective-permute-start.41 = (bf16[256,512]{1,0:T(8,128)(2,1)}, bf16[256,512]{1,0:T(8,128)(2,1)S(1)}, u32[]{:S(2)}, u32[]{:S(2)}) collective-permute-start(bf16[256,512]{1,0:T(8,128)(2,1)} %copy-done.20), channel_id=1, source_target_pairs={{0,4},{4,0},{8,12},{12,8},{16,20},{20,16},{24,28},{28,24},{1,5},{5... | collective-permute-start | bytes 786440 | tf_op jit(solution)/shard_map/ppermute | solution.py:427
  142.4 22.8 %collective-permute-start.37 = (bf16[256,512]{1,0:T(8,128)(2,1)}, bf16[256,512]{1,0:T(8,128)(2,1)S(1)}, u32[]{:S(2)}, u32[]{:S(2)}) collective-permute-start(bf16[256,512]{1,0:T(8,128)(2,1)} %copy-done.6), channel_id=1, source_target_pairs={{0,4},{4,0},{8,12},{12,8},{16,20},{20,16},{24,28},{28,24},{1,5},{5... | collective-permute-start | bytes 786440 | tf_op jit(solution)/shard_map/ppermute | solution.py:427
  145.5 22.5 %collective-permute-start.38 = (bf16[256,512]{1,0:T(8,128)(2,1)}, bf16[256,512]{1,0:T(8,128)(2,1)S(1)}, u32[]{:S(2)}, u32[]{:S(2)}) collective-permute-start(bf16[256,512]{1,0:T(8,128)(2,1)} %copy-done.5), channel_id=1, source_target_pairs={{0,4},{4,0},{8,12},{12,8},{16,20},{20,16},{24,28},{28,24},{1,5},{5... | collective-permute-start | bytes 786440 | tf_op jit(solution)/shard_map/ppermute | solution.py:427
  151.1 18.9 %collective-permute-start.20 = (bf16[256,512]{1,0:T(8,128)(2,1)S(1)}, bf16[256,512]{1,0:T(8,128)(2,1)S(1)}, u32[]{:S(2)}, u32[]{:S(2)}) collective-permute-start(bf16[256,512]{1,0:T(8,128)(2,1)S(1)} %get-tuple-element.58.refs_8_.refs_5_.refs_2_.refs_0_), channel_id=1, source_target_pairs={{0,8},{4,12},{8,16},{12,20},{16,24},{20,28},{1,9},{5,13},{9,17},{1... | collective-permute-start | bytes 786440 | tf_op jit(solution)/shard_map/ppermute | solution.py:426
  152.4 18.3 %collective-permute-start.21 = (bf16[256,512]{1,0:T(8,128)(2,1)S(1)}, bf16[256,512]{1,0:T(8,128)(2,1)S(1)}, u32[]{:S(2)}, u32[]{:S(2)}) collective-permute-start(bf16[256,512]{1,0:T(8,128)(2,1)S(1)} %get-tuple-element.57.refs_18_.refs_6_.refs_3_.refs_1_), channel_id=1, source_target_pairs={{0,8},{4,12},{8,16},{12,20},{16,24},{20,28},{1,9},{5,13},{9,17},{1... | collective-permute-start | bytes 786440 | tf_op jit(solution)/shard_map/ppermute | solution.py:426
  163.1 34.3 %collective-permute-start.34 = (bf16[256,512]{1,0:T(8,128)(2,1)}, bf16[256,512]{1,0:T(8,128)(2,1)S(1)}, u32[]{:S(2)}, u32[]{:S(2)}) collective-permute-start(bf16[256,512]{1,0:T(8,128)(2,1)} %copy-done), channel_id=1, source_target_pairs={{0,4},{4,0},{8,12},{12,8},{16,20},{20,16},{24,28},{28,24},{1,5},{5... | collective-permute-start | bytes 786440 | tf_op jit(solution)/shard_map/ppermute | solution.py:427
  165.2 32.2 %collective-permute-start.35 = (bf16[256,512]{1,0:T(8,128)(2,1)}, bf16[256,512]{1,0:T(8,128)(2,1)S(1)}, u32[]{:S(2)}, u32[]{:S(2)}) collective-permute-start(bf16[256,512]{1,0:T(8,128)(2,1)} %copy-done.7), channel_id=1, source_target_pairs={{0,4},{4,0},{8,12},{12,8},{16,20},{20,16},{24,28},{28,24},{1,5},{5... | collective-permute-start | bytes 786440 | tf_op jit(solution)/shard_map/ppermute | solution.py:427
  168.0 30.2 %collective-permute-start.26 = (bf16[256,512]{1,0:T(8,128)(2,1)S(1)}, bf16[256,512]{1,0:T(8,128)(2,1)S(1)}, u32[]{:S(2)}, u32[]{:S(2)}) collective-permute-start(bf16[256,512]{1,0:T(8,128)(2,1)S(1)} %get-tuple-element.58.refs_8_.refs_5_.refs_2_.refs_0_), channel_id=1, source_target_pairs={{0,4},{4,0},{8,12},{12,8},{16,20},{20,16},{24,28},{28,24},{1,5},{5... | collective-permute-start | bytes 786440 | tf_op jit(solution)/shard_map/ppermute | solution.py:427
  170.0 28.8 %collective-permute-start.22 = (bf16[256,512]{1,0:T(8,128)(2,1)S(1)}, bf16[256,512]{1,0:T(8,128)(2,1)S(1)}, u32[]{:S(2)}, u32[]{:S(2)}) collective-permute-start(bf16[256,512]{1,0:T(8,128)(2,1)S(1)} %collective-permute-done.20.refs_7_.refs_4_.refs_2_), channel_id=1, source_target_pairs={{8,16},{12,20},{16,24},{20,28},{9,17},{13,21},{17,25},{21,29},{10,... | collective-permute-start | bytes 786440 | tf_op jit(solution)/shard_map/ppermute | solution.py:426
  170.7 28.9 %collective-permute-start.23 = (bf16[256,512]{1,0:T(8,128)(2,1)S(1)}, bf16[256,512]{1,0:T(8,128)(2,1)S(1)}, u32[]{:S(2)}, u32[]{:S(2)}) collective-permute-start(bf16[256,512]{1,0:T(8,128)(2,1)S(1)} %collective-permute-done.21.refs_8_.refs_5_.refs_3_), channel_id=1, source_target_pairs={{8,16},{12,20},{16,24},{20,28},{9,17},{13,21},{17,25},{21,29},{10,... | collective-permute-start | bytes 786440 | tf_op jit(solution)/shard_map/ppermute | solution.py:426
  197.4 23.0 %collective-permute-start.27 = (bf16[256,512]{1,0:T(8,128)(2,1)S(1)}, bf16[256,512]{1,0:T(8,128)(2,1)S(1)}, u32[]{:S(2)}, u32[]{:S(2)}) collective-permute-start(bf16[256,512]{1,0:T(8,128)(2,1)S(1)} %get-tuple-element.57.refs_18_.refs_6_.refs_3_.refs_1_), channel_id=1, source_target_pairs={{0,4},{4,0},{8,12},{12,8},{16,20},{20,16},{24,28},{28,24},{1,5},{5... | collective-permute-start | bytes 786440 | tf_op jit(solution)/shard_map/ppermute | solution.py:427
  197.5 23.6 %collective-permute-start.28 = (bf16[256,512]{1,0:T(8,128)(2,1)S(1)}, bf16[256,512]{1,0:T(8,128)(2,1)S(1)}, u32[]{:S(2)}, u32[]{:S(2)}) collective-permute-start(bf16[256,512]{1,0:T(8,128)(2,1)S(1)} %collective-permute-done.20.refs_7_.refs_4_.refs_2_), channel_id=1, source_target_pairs={{8,12},{12,8},{16,20},{20,16},{24,28},{28,24},{9,13},{13,9},{17,21... | collective-permute-start | bytes 786440 | tf_op jit(solution)/shard_map/ppermute | solution.py:427
  198.2 25.2 %collective-permute-start.29 = (bf16[256,512]{1,0:T(8,128)(2,1)S(1)}, bf16[256,512]{1,0:T(8,128)(2,1)S(1)}, u32[]{:S(2)}, u32[]{:S(2)}) collective-permute-start(bf16[256,512]{1,0:T(8,128)(2,1)S(1)} %collective-permute-done.21.refs_8_.refs_5_.refs_3_), channel_id=1, source_target_pairs={{8,12},{12,8},{16,20},{20,16},{24,28},{28,24},{9,13},{13,9},{17,21... | collective-permute-start | bytes 786440 | tf_op jit(solution)/shard_map/ppermute | solution.py:427
  198.9 22.9 %collective-permute-start.24 = (bf16[256,512]{1,0:T(8,128)(2,1)S(1)}, bf16[256,512]{1,0:T(8,128)(2,1)S(1)}, u32[]{:S(2)}, u32[]{:S(2)}) collective-permute-start(bf16[256,512]{1,0:T(8,128)(2,1)S(1)} %collective-permute-done.22.refs_18_.refs_6_.refs_4_), channel_id=1, source_target_pairs={{16,24},{20,28},{17,25},{21,29},{18,26},{22,30},{19,27},{23,31}} | collective-permute-start | bytes 786440 | tf_op jit(solution)/shard_map/ppermute | solution.py:426
  199.6 22.9 %collective-permute-start.25 = (bf16[256,512]{1,0:T(8,128)(2,1)S(1)}, bf16[256,512]{1,0:T(8,128)(2,1)S(1)}, u32[]{:S(2)}, u32[]{:S(2)}) collective-permute-start(bf16[256,512]{1,0:T(8,128)(2,1)S(1)} %collective-permute-done.23.refs_7_.refs_5_), channel_id=1, source_target_pairs={{16,24},{20,28},{17,25},{21,29},{18,26},{22,30},{19,27},{23,31}} | collective-permute-start | bytes 786440 | tf_op jit(solution)/shard_map/ppermute | solution.py:426
  220.4 23.7 %collective-permute-start.30 = (bf16[256,512]{1,0:T(8,128)(2,1)S(1)}, bf16[256,512]{1,0:T(8,128)(2,1)S(1)}, u32[]{:S(2)}, u32[]{:S(2)}) collective-permute-start(bf16[256,512]{1,0:T(8,128)(2,1)S(1)} %collective-permute-done.22.refs_18_.refs_6_.refs_4_), channel_id=1, source_target_pairs={{16,20},{20,16},{24,28},{28,24},{17,21},{21,17},{25,29},{29,25},{1... | collective-permute-start | bytes 786440 | tf_op jit(solution)/shard_map/ppermute | solution.py:427
  221.1 23.0 %collective-permute-start.31 = (bf16[256,512]{1,0:T(8,128)(2,1)S(1)}, bf16[256,512]{1,0:T(8,128)(2,1)S(1)}, u32[]{:S(2)}, u32[]{:S(2)}) collective-permute-start(bf16[256,512]{1,0:T(8,128)(2,1)S(1)} %collective-permute-done.23.refs_7_.refs_5_), channel_id=1, source_target_pairs={{16,20},{20,16},{24,28},{28,24},{17,21},{21,17},{25,29},{29,25},{1... | collective-permute-start | bytes 786440 | tf_op jit(solution)/shard_map/ppermute | solution.py:427
  221.8 38.3 %collective-permute-start.32 = (bf16[256,512]{1,0:T(8,128)(2,1)S(1)}, bf16[256,512]{1,0:T(8,128)(2,1)S(1)}, u32[]{:S(2)}, u32[]{:S(2)}) collective-permute-start(bf16[256,512]{1,0:T(8,128)(2,1)S(1)} %collective-permute-done.24.refs_16_.refs_6_), channel_id=1, source_target_pairs={{24,28},{28,24},{25,29},{29,25},{26,30},{30,26},{27,31},{31,27}} | collective-permute-start | bytes 786440 | tf_op jit(solution)/shard_map/ppermute | solution.py:427
  222.5 37.6 %collective-permute-start.33 = (bf16[256,512]{1,0:T(8,128)(2,1)S(1)}, bf16[256,512]{1,0:T(8,128)(2,1)S(1)}, u32[]{:S(2)}, u32[]{:S(2)}) collective-permute-start(bf16[256,512]{1,0:T(8,128)(2,1)S(1)} %collective-permute-done.25.refs_7_.refs_16_), channel_id=1, source_target_pairs={{24,28},{28,24},{25,29},{29,25},{26,30},{30,26},{27,31},{31,27}} | collective-permute-start | bytes 786440 | tf_op jit(solution)/shard_map/ppermute | solution.py:427
  (42 other events, 1061.2 us)

commit v2 on v1

v2 whole, which is shorter than its diff:
```python
import functools

import jax
import jax.numpy as jnp
from jax import lax
from jax.experimental import pallas as pl
from jax.experimental.pallas import tpu as pltpu
from jax.sharding import PartitionSpec as P

NB = 256
W = 64
MICRO = 8
CHUNKS = 7
ROW_TILES = 7
PIECES = 4
BATCHES = ((0, 2), (2, 4), (4, 6), (6, 7))
LIMIT = 56 * 2**20


def split3(x):
    high = x.astype(jnp.bfloat16)
    rest = x - high.astype(jnp.float32)
    middle = rest.astype(jnp.bfloat16)
    low = (rest - middle.astype(jnp.float32)).astype(jnp.bfloat16)
    return high, middle, low


def dot(a, b):
    return jnp.dot(a, b, preferred_element_type=jnp.float32)


def factor_small(block):
    lane = lax.broadcasted_iota(jnp.int32, (W, 128), 1)
    row = lax.broadcasted_iota(jnp.int32, (W, 128), 0)
    work = jnp.where(lane < W, block, jnp.where(lane == row + W, 1.0, 0.0))
    upper = jnp.where(lane == row, 1.0, 0.0).astype(jnp.float32)
    packed = jnp.zeros((W, 128), jnp.float32)
    scale = jnp.ones((W, 128), jnp.float32)
    for first in range(0, W, MICRO):
        columns = [
            jnp.broadcast_to(work[:, j : j + 1], (W, 128)) for j in range(first, first + MICRO)
        ]
        for step in range(MICRO):
            j = first + step
            column = columns[step]
            inverse = 1.0 / column[j : j + 1, :]
            factor = jnp.where(row == j, 0.0, column * inverse)
            for later in range(step + 1, MICRO):
                other = columns[later]
                columns[later] = other - factor * other[j : j + 1, :]
            line = work[j : j + 1, :]
            below = jnp.where(row > j, factor, 0.0)
            above = factor - below
            packed = jnp.where((row == j) & (lane >= j), line, packed)
            packed = jnp.where((lane == j) & (row > j), factor, packed)
            scale = jnp.where(row == j, inverse, scale)
            work = work - jnp.where(lane < W, factor, below) * line
            upper = upper - above * upper[j : j + 1, :]
    return packed, work, upper * scale


def repeat_lanes(x, first):
    lane = lax.broadcasted_iota(jnp.int32, x.shape, 1)
    x = jnp.where((lane >= first) & (lane < first + W), x, 0.0)
    return x + pltpu.roll(x, W, 1)


def pack_left(x):
    lane = lax.broadcasted_iota(jnp.int32, x.shape, 1)
    high = x.astype(jnp.bfloat16)
    rest = x - high.astype(jnp.float32)
    middle = rest.astype(jnp.bfloat16).astype(jnp.float32)
    low = rest - middle
    second = jnp.where(lane < W, high.astype(jnp.float32), middle).astype(jnp.bfloat16)
    third = jnp.where(lane < W, middle, low).astype(jnp.bfloat16)
    return jnp.concatenate([high, second, third], axis=1)


def pack_right(x):
    high, middle, low = split3(x)
    return jnp.concatenate([high, middle, low, high, middle, high], axis=0)


def block_step(k, work_ref, lower_ref, upper_ref):
    active = NB - W * k
    packed, left_small, upper_small = factor_small(work_ref[:W, :128])
    small_left = pack_left(repeat_lanes(left_small, W))
    small_upper = pack_right(repeat_lanes(upper_small, 0))

    work = work_ref[...]
    lower = lower_ref[...]
    upper = upper_ref[...]
    col = lax.broadcasted_iota(jnp.int32, (W, NB), 1)
    row = lax.broadcasted_iota(jnp.int32, (NB, 128), 0)
    lane = lax.broadcasted_iota(jnp.int32, (NB, 128), 1)
    live_col = (col >= W) & (col < active)
    live_row = (row >= W) & (row < active)

    tops = dot(small_left, pack_right(jnp.concatenate([work[:W], lower[:W]], axis=1)))
    top, lower_top = tops[:, :NB], tops[:, NB:]
    sides = jnp.concatenate([work[:, :128], upper[:, :128]], axis=0)
    sides = dot(pack_left(repeat_lanes(sides, 0)), small_upper)
    left, upper_left = sides[:NB], sides[NB:]
    left_live = jnp.where(live_row, left, 0.0)
    top_live = jnp.where(live_col, top, 0.0)

    right_packed = pack_right(jnp.concatenate([top_live, lower_top], axis=1))
    change = dot(pack_left(left_live), right_packed)
    upper_change = dot(pack_left(upper_left), right_packed[:, :NB])
    work_new = work - change[:, :NB]
    lower_new = lower - change[:, NB:]
    upper_new = upper - upper_change

    left_side = jnp.where((lane < W) & live_row, left, work_new[:, :128])
    work_new = jnp.concatenate([left_side, work_new[:, 128:]], axis=1)
    packed_wide = jnp.concatenate([packed, jnp.zeros_like(packed)], axis=1)
    top_new = jnp.where(col < W, packed_wide, jnp.where(live_col, top, work[:W]))
    work_new = jnp.concatenate([work_new[W:], top_new], axis=0)
    work_ref[...] = pltpu.roll(work_new, NB - W, 1)
    lower_ref[...] = jnp.concatenate([lower_new[W:], lower_top], axis=0)
    upper_side = jnp.where(lane < W, upper_left, upper_new[:, :128])
    upper_ref[...] = pltpu.roll(
        jnp.concatenate([upper_side, upper_new[:, 128:]], axis=1), NB - W, 1
    )


def identity():
    row = lax.broadcasted_iota(jnp.int32, (NB, NB), 0)
    col = lax.broadcasted_iota(jnp.int32, (NB, NB), 1)
    return jnp.where(row == col, 1.0, 0.0).astype(jnp.float32)


def split2(x):
    high = x.astype(jnp.bfloat16)
    return high, (x - high.astype(jnp.float32)).astype(jnp.bfloat16)


def times_right(a, b):
    width = b.shape[1]
    both = dot(a, jnp.concatenate(split2(b), axis=1))
    return both[:, :width] + both[:, width:]


def times_left(a, b):
    height = a.shape[0] // 2
    both = dot(a, b)
    return both[:height] + both[height:]


def run_steps(first, count, work_ref, lower_ref, upper_ref):
    def body(k, carry):
        block_step(k, work_ref, lower_ref, upper_ref)
        return carry

    lax.fori_loop(first, first + count, body, 0)


def pick(place_ref, blocks, i, j):
    same_row = place_ref[0] % 2 == i
    same_col = place_ref[1] % 2 == j
    own, across, below, both = [block[...].astype(jnp.float32) for block in blocks]
    near = jnp.where(same_col, own, across)
    far = jnp.where(same_col, below, both)
    return jnp.where(same_row, near, far)


def first_kernel(count, n_extra, place_ref, d0, d1, d2, d3, *refs):
    work_ref, lower_ref, upper_ref = refs[n_extra:][:3]
    work_ref[...] = pick(place_ref, (d0, d1, d2, d3), 0, 0)
    lower_ref[...] = identity()
    upper_ref[...] = identity()
    run_steps(0, count, work_ref, lower_ref, upper_ref)


def second_kernel(count, n_extra, place_ref, d0, d1, d2, d3, inv_lower, inv_upper, *refs):
    work_ref, lower_ref, upper_ref, left_ref, top_ref = refs[n_extra:][:5]
    blocks = (d0, d1, d2, d3)
    left = times_right(pick(place_ref, blocks, 1, 0).astype(jnp.bfloat16), inv_upper[...])
    left = left.astype(jnp.bfloat16)
    top = times_left(jnp.concatenate(split2(inv_lower[...]), axis=0), pick(place_ref, blocks, 0, 1).astype(jnp.bfloat16))
    top = top.astype(jnp.bfloat16)
    left_ref[...] = left
    top_ref[...] = top
    block = pick(place_ref, blocks, 1, 1) - dot(left, top)
    work_ref[...] = block.astype(jnp.bfloat16).astype(jnp.float32)
    lower_ref[...] = identity()
    upper_ref[...] = identity()
    run_steps(0, count, work_ref, lower_ref, upper_ref)


def next_kernel(first, count, n_extra, work_in, lower_in, upper_in, *refs):
    work_ref, lower_ref, upper_ref = refs[n_extra:][:3]
    work_ref[...] = work_in[...]
    lower_ref[...] = lower_in[...]
    upper_ref[...] = upper_in[...]
    run_steps(first, count, work_ref, lower_ref, upper_ref)


def vmem():
    return pl.BlockSpec(memory_space=pltpu.VMEM)


def smem():
    return pl.BlockSpec(memory_space=pltpu.SMEM)


def anywhere():
    return pl.BlockSpec(memory_space=pl.ANY)


def factor_call(body, n_out, place, operands, extra, flops):
    square = jax.ShapeDtypeStruct((NB, NB), jnp.float32)
    panel = jax.ShapeDtypeStruct((NB, NB), jnp.bfloat16)
    scalars = [] if place is None else [place]
    return pl.pallas_call(
        body,
        out_shape=[square] * 3 + [panel] * (n_out - 3),
        in_specs=[smem() for _ in scalars] + [vmem() for _ in operands] + [anywhere() for _ in extra],
        out_specs=[vmem()] * n_out,
        compiler_params=pltpu.CompilerParams(vmem_limit_bytes=LIMIT),
        cost_estimate=pl.CostEstimate(flops=flops, bytes_accessed=2**21, transcendentals=0),
    )(*scalars, *operands, *extra)


def gate_kernel(column, place_ref, matrix, received, *refs):
    out, sem = refs[-2:]

    @pl.when(place_ref[0] < 2)
    def _():
        pltpu.make_async_copy(matrix.at[pl.ds(0, NB), pl.ds(column, out.shape[1])], out, sem).start()

    @pl.when(place_ref[0] >= 2)
    def _():
        pltpu.make_async_copy(received, out, sem).start()

    pltpu.make_async_copy(received, out, sem).wait()


def gate_call(column, place, matrix, received, before):
    return pl.pallas_call(
        functools.partial(gate_kernel, column),
        out_shape=jax.ShapeDtypeStruct(received.shape, received.dtype),
        in_specs=[smem()] + [anywhere() for _ in range(2 + len(before))],
        out_specs=anywhere(),
        scratch_shapes=[pltpu.SemaphoreType.DMA(())],
        compiler_params=pltpu.CompilerParams(vmem_limit_bytes=LIMIT),
    )(place, matrix, received, *before)


def left_kernel(place_ref, own, other, inv_first, inv_second, top, *refs):
    out = refs[-1]
    parity = place_ref[1] % 2
    own_value = own[...].astype(jnp.float32)
    other_value = other[...].astype(jnp.float32)
    first = jnp.where(parity == 0, own_value, other_value).astype(jnp.bfloat16)
    second = jnp.where(parity == 0, other_value, own_value)
    rows = lax.broadcasted_iota(jnp.int32, (own.shape[0], NB), 0)
    outer = (rows >= NB) | (pl.program_id(0) > 0)
    left = times_right(first, inv_first[...])
    left = jnp.where(outer | (place_ref[0] > 0), left, 0.0).astype(jnp.bfloat16)
    out[:, :NB] = left
    second = (second - dot(left, top[...])).astype(jnp.bfloat16)
    left = times_right(second, inv_second[...])
    left = jnp.where(outer | (place_ref[0] > 1), left, 0.0).astype(jnp.bfloat16)
    out[:, NB:] = left


def left_call(place, own, other, inv_first, inv_second, top, extra):
    rows = own.shape[0]
    tile = rows // 4
    whole = pl.BlockSpec((NB, NB), lambda i: (0, 0))
    return pl.pallas_call(
        left_kernel,
        grid=(4,),
        out_shape=jax.ShapeDtypeStruct((rows, 2 * NB), jnp.bfloat16),
        in_specs=[
            smem(),
            pl.BlockSpec((tile, NB), lambda i: (i, 0)),
            pl.BlockSpec((tile, NB), lambda i: (i, 0)),
            whole,
            whole,
            whole,
        ]
        + [anywhere() for _ in extra],
        out_specs=pl.BlockSpec((tile, 2 * NB), lambda i: (i, 0)),
        compiler_params=pltpu.CompilerParams(vmem_limit_bytes=LIMIT),
        cost_estimate=pl.CostEstimate(
            flops=14 * rows * NB * NB, bytes_accessed=8 * rows * NB, transcendentals=0
        ),
    )(place, own, other, inv_first, inv_second, top, *extra)


def update_kernel(first, count, lines, n_extra, place_ref, matrix, left_ref, packed_first,
                  packed_second, inv_first, inv_second, left_block, *refs):
    n_sent = count + lines - 1
    own = refs[:n_sent]
    other = refs[n_sent : 2 * n_sent]
    out, raw, top_ref, inv_ref, sems = refs[2 * n_sent + n_extra :]
    j = pl.program_id(0)
    i = pl.program_id(1)
    grid_row = place_ref[0]
    grid_col = place_ref[1]
    line = grid_row // 2
    parity = grid_row % 2
    tile, width = out.shape

    @pl.when((i == 0) & (j == 0))
    def _():
        for c in range(count):
            for k in range(lines):
                @pl.when(line == k)
                def _():
                    pltpu.make_async_copy(own[c + k], raw.at[parity, c], sems.at[0, c]).start()
                    pltpu.make_async_copy(other[c + k], raw.at[1 - parity, c], sems.at[1, c]).start()
        inv_ref[0] = jnp.concatenate(split2(inv_first[...]), axis=0)
        inv_ref[1] = jnp.concatenate(split2(inv_second[...]), axis=0)

    @pl.when(i == 0)
    def _():
        pltpu.make_async_copy(own[0], raw.at[parity, j], sems.at[0, j]).wait()
        pltpu.make_async_copy(other[0], raw.at[1 - parity, j], sems.at[1, j]).wait()
        cols = lax.broadcasted_iota(jnp.int32, (NB, width), 1)
        outer = (cols >= NB) | (first + j > 0)
        top = times_left(inv_ref[0], raw[0, j])
        top = jnp.where(outer | (grid_col > 0), -top, 0.0).astype(jnp.bfloat16)
        top_ref[:NB, :] = top
        second = raw[1, j].astype(jnp.float32) + dot(left_block[...], top)
        top = times_left(inv_ref[1], second.astype(jnp.bfloat16))
        top = jnp.where(outer | (grid_col > 1), -top, 0.0).astype(jnp.bfloat16)
        top_ref[NB:, :] = top

    for start in range(0, tile, NB):
        rows = pl.ds(pl.multiple_of(i * tile + start, NB), NB)
        here = slice(start, start + NB)
        value = matrix[here, :].astype(jnp.float32) + dot(left_ref[rows, :NB], top_ref[:NB, :])
        value = value.astype(jnp.bfloat16).astype(jnp.float32)
        value = value + dot(left_ref[rows, NB:], top_ref[NB:, :])
        out[here, :] = value.astype(jnp.bfloat16)

    rows = pl.ds(pl.multiple_of(i * tile, tile), tile)

    @pl.when((i == 0) & (grid_row == 0))
    def _():
        out[:NB, :] = -top_ref[:NB, :]

    @pl.when((i == 0) & (grid_row == 1))
    def _():
        out[:NB, :] = -top_ref[NB:, :]

    if first == 0:
        @pl.when((j == 0) & (grid_col == 0))
        def _():
            out[:, :NB] = left_ref[rows, :NB]

        @pl.when((j == 0) & (grid_col == 1))
        def _():
            out[:, :NB] = left_ref[rows, NB:]

        @pl.when((j == 0) & (i == 0) & (grid_col == 0) & (grid_row == 0))
        def _():
            out[:NB, :NB] = packed_first[...].astype(jnp.bfloat16)

        @pl.when((j == 0) & (i == 0) & (grid_col == 1) & (grid_row == 0))
        def _():
            out[:NB, :NB] = -top_ref[:NB, :NB]

        @pl.when((j == 0) & (i == 0) & (grid_col == 1) & (grid_row == 1))
        def _():
            out[:NB, :NB] = packed_second[...].astype(jnp.bfloat16)


def update_call(first, last, lines, place, matrix, left, squares, left_block, own, other, extra, before):
    rows, cols = matrix.shape
    width = cols // CHUNKS
    tile = rows // ROW_TILES
    count = last - first
    tail = list(extra) + ([] if before is None else [before])
    whole = pl.BlockSpec((NB, NB), lambda j, i: (0, 0))
    big = pl.BlockSpec((tile, width), lambda j, i: (i, j + first))
    operands = [place, matrix, left, *squares, left_block, *own, *other, *tail]
    aliases = {} if before is None else {len(operands) - 1: 0}
    return pl.pallas_call(
        functools.partial(update_kernel, first, count, lines, len(tail)),
        grid=(count, ROW_TILES),
        out_shape=jax.ShapeDtypeStruct((rows, cols), jnp.bfloat16),
        in_specs=[smem(), big, pl.BlockSpec((rows, 2 * NB), lambda j, i: (0, 0))]
        + [whole] * 5
        + [anywhere() for _ in range(len(own) + len(other) + len(tail))],
        out_specs=big,
        scratch_shapes=[
            pltpu.VMEM((2, count, NB, width), jnp.bfloat16),
            pltpu.VMEM((2 * NB, width), jnp.bfloat16),
            pltpu.VMEM((2, 2 * NB, NB), jnp.bfloat16),
            pltpu.SemaphoreType.DMA((2, count)),
        ],
        input_output_aliases=aliases,
        compiler_params=pltpu.CompilerParams(vmem_limit_bytes=LIMIT),
        cost_estimate=pl.CostEstimate(
            flops=6 * rows * NB * width * count,
            bytes_accessed=6 * rows * width * count,
            transcendentals=0,
        ),
    )(*operands)


def swap(size):
    return [(i, i ^ 1) for i in range(size)]


def spread(block, axis, size, index):
    stride = size // 2
    while stride >= 2:
        pairs = [(i, i + stride) for i in range(size) if i % (2 * stride) < 2]
        moved = lax.ppermute(block, axis, pairs)
        block = jnp.where(index % (2 * stride) >= stride, moved, block)
        stride //= 2
    return block


def on_device(matrix):
    grid_rows = lax.axis_size("row")
    grid_cols = lax.axis_size("col")
    grid_row = lax.axis_index("row")
    grid_col = lax.axis_index("col")
    place = jnp.stack([grid_row, grid_col]).astype(jnp.int32)
    lines = grid_rows // 2
    width = matrix.shape[1] // CHUNKS

    diag = spread(matrix[:NB, :NB], "col", grid_cols, grid_col)
    diag = spread(diag, "row", grid_rows, grid_row)
    both_swap = [
        (i * grid_cols + j, (i ^ 1) * grid_cols + (j ^ 1))
        for i in range(grid_rows)
        for j in range(grid_cols)
    ]
    blocks = (
        diag,
        lax.ppermute(diag, "col", swap(grid_cols)),
        lax.ppermute(diag, "row", swap(grid_rows)),
        lax.ppermute(diag, ("row", "col"), both_swap),
    )

    n_ticks = CHUNKS + lines - 1
    own, other, received = [], [], []

    def move(done, late=None):
        tick = len(own)
        if tick >= n_ticks:
            return [] if tick > n_ticks else [done]
        if tick == 0:
            send = jnp.where(grid_row < 2, matrix[:NB, :width], done)
        else:
            column = min(tick, CHUNKS - 1) * width
            send = gate_call(column, place, matrix, received[-1], [other[-1], done])
        live = [k for k in range(lines) if 0 <= tick - k < CHUNKS]
        onward = [(2 * k + e, 2 * k + 2 + e) for k in live for e in range(2) if k + 1 < lines]
        across = [(2 * k + e, 2 * k + 1 - e) for k in live for e in range(2)]
        received.append(lax.ppermute(send, "row", onward) if onward else send)
        own.append(send)
        if tick == 0:
            send = gate_call(0, place, matrix, send, late)
        other.append(lax.ppermute(send, "row", across))
        return [own[tick]]

    move(diag[:1, :1], blocks[2:])
    column = spread(matrix[:, :NB], "col", grid_cols, grid_col)
    column_other = lax.ppermute(column, "col", swap(grid_cols))

    cost = 10**9
    per_piece = NB // W // PIECES
    kept = []
    for section in range(2):
        for piece in range(PIECES):
            if piece > 0:
                extra = move(square[0])
                body = functools.partial(next_kernel, piece * per_piece, per_piece, len(extra))
                square = factor_call(body, 3, None, square, extra, cost)
            elif section == 0:
                body = functools.partial(first_kernel, per_piece, 0)
                square = factor_call(body, 3, place, blocks, [], cost)
            else:
                extra = move(square[0])
                body = functools.partial(second_kernel, per_piece, len(extra))
                *square, left_block, top_block = factor_call(
                    body, 5, place, [*blocks, *kept[0][1:]], extra, cost
                )
        kept.append(square)

    packed, lower, upper = zip(*kept)
    left = left_call(place, column, column_other, *upper, top_block, move(square[0]))
    latest = left
    out = None
    for first, last in BATCHES:
        while len(own) < min(last + lines, n_ticks):
            latest = move(latest)[0]
        sent = range(first, last + lines - 1)
        out = update_call(
            first, last, lines, place, matrix, left, (*packed, *lower), left_block,
            [own[t] for t in sent], [other[t] for t in sent], [] if latest is out else [latest], out,
        )
        latest = out
    return out


def solution(mesh):
    return jax.shard_map(
        on_device, mesh=mesh, in_specs=(P("row", "col"),), out_specs=P("row", "col"), check_vma=False
    )
```

time: 279 us -> 432 us (1.55)
  the two profiles are of different devices: /device:TPU:0 before, /device:TPU:24 now
where the time goes in v2:
time: 432 us; the launch traced here: 430 us
  Pallas kernels  305 us (71%)
  waiting for transfers between devices  65.4 us (15%)
  starting transfers between devices  37.9 us (9%)
  local copies, waits for them, and re-layouts  15.7 us (4%)
  other arithmetic  4.96 us (1%)
    pallas_call x10, Pallas kernels, gate_call(): pl.pallas_call(functools.partial(gate_kernel, column), out_shape=jax.Shap...  177 us
    pallas_call x4, Pallas kernels, update_call(): pl.pallas_call(functools.partial(update_kernel, first, count, lines, len(...  82.4 us
    ppermute x9, waiting for transfers between devices, move(): received.append(lax.ppermute(send, 'row', onward) if onward else send)  46.7 us
    pallas_call x8, Pallas kernels, factor_call(): pl.pallas_call(body, out_shape=[square] * 3 + [panel] * (n_out - 3), in_s...  38.3 us
    ppermute x10, starting transfers between devices, move(): other.append(lax.ppermute(send, 'row', across))  15.8 us
    ppermute x4, waiting for transfers between devices, spread(): moved = lax.ppermute(block, axis, pairs)  12.7 us
    unnamed x52, local copies, waits for them, and re-layouts  12.7 us
    ppermute x9, starting transfers between devices, move(): received.append(lax.ppermute(send, 'row', onward) if onward else send)  10.6 us
  transfers between devices with their start and end apart: 27, of which 12 were waited for; matrix products, arithmetic and copies ran while one was open for 1% of the time, Pallas kernels for 64%

profile of v2, /device:TPU:24, one launch (start us, length us, event | category | flops | bytes accessed | tf_op | source)
XLA Modules:
  0.0 429.6 jit_solution(968410126827134884)
XLA Ops:
  0.9 3.4 collective-permute-start.2
  4.3 2.7 collective-permute-done.2
  10.6 9.9 %collective-permute-done.4 = bf16[256,256]{1,0:T(8,128)(2,1)S(1)} collective-permute-done((bf16[256,256]{1,0:T(8,128)(2,1)S(1)}, bf16[256,256]{1,0:T(8,128)(2,1)S(1)}, u32[]{:S(2)}, u32[]{:S(2)}) %collective-permute-start.4) | collective-permute-done | bytes 131104 | tf_op jit(solution)/shard_map/ppermute | solution.py:414
  21.1 1.5 collective-permute-start.6
  22.7 1.7 slice_select_fusion.received.refs_0_
  25.1 1.5 collective-permute-done.6.d2.refs_0_
  26.6 1.9 collective-permute-done.7.d3.refs_1_
  29.1 17.7 %shard_map.18 = bf16[256,1024]{1,0:T(8,128)(2,1)} custom-call(s32[2]{0:T(128)} %pad_add_fusion.place_ref, bf16[3584,7168]{1,0:T(8,128)(2,1)} %matrix.27, bf16[256,1024]{1,0:T(8,128)(2,1)} %copy-done.7, bf16[256,256]{1,0:T(8,128)(2,1)} %copy-done.21, bf16[256,256]{1,0:T(8,128)(2,1)} %copy-done.22), custom_call_target="tpu_custom_call" | custom-call | tf_op jit(solution)/shard_map/pallas_call | solution.py:240
  47.5 1.6 slice.12
  49.1 4.5 %collective-permute-start = (bf16[3584,256]{1,0:T(8,128)(2,1)S(1)}, bf16[3584,256]{1,0:T(8,128)(2,1)S(1)}, u32[]{:S(2)}, u32[]{:S(2)}) collective-permute-start(bf16[3584,256]{1,0:T(8,128)(2,1)S(1)} %slice.12), channel_id=1, source_target_pairs={{0,2},{1,3},{4,6},{5,7},{8,10},{9,11},{12,14},{13,15},{16,18},{17,... | collective-permute-start | bytes 5505032 | tf_op jit(solution)/shard_map/ppermute | solution.py:414
  53.7 1.3 collective-permute-done.5.d1
  55.7 4.6 %shard_map.17 = (f32[256,256]{1,0:T(8,128)}, f32[256,256]{1,0:T(8,128)}, f32[256,256]{1,0:T(8,128)}) custom-call(s32[2]{0:T(128)} %pad_add_fusion.place_ref, bf16[256,256]{1,0:T(8,128)(2,1)} %copy-done.23, bf16[256,256]{1,0:T(8,128)(2,1)} %copy-done.25, bf16[256,256]{1,0:T(8,128)(2,1)} %copy-done.21, bf16[256,256]{1,0:T(8,128)(2,1)} %copy-done.22), custom_call_target="tpu_custom_call" | custom-call | flops 1000000000 | bytes 2097152 | tf_op jit(solution)/shard_map/pallas_call | solution.py:215
  61.2 17.7 %shard_map.19.refs_0_.refs_1_ = bf16[256,1024]{1,0:T(8,128)(2,1)} custom-call(s32[2]{0:T(128)} %pad_add_fusion.place_ref, bf16[3584,7168]{1,0:T(8,128)(2,1)} %matrix.27, bf16[256,1024]{1,0:T(8,128)(2,1)} %copy-done.11, bf16[256,1024]{1,0:T(8,128)(2,1)} %copy-done.8, f32[256,256]{1,0:T(8,128)} %get-tuple-element.31.refs_1_.work_in), custom_call_target="tpu_custom_call" | custom-call | tf_op jit(solution)/shard_map/pallas_call | solution.py:240
  80.3 4.6 %shard_map.20 = (f32[256,256]{1,0:T(8,128)}, f32[256,256]{1,0:T(8,128)}, f32[256,256]{1,0:T(8,128)}) custom-call(f32[256,256]{1,0:T(8,128)} %get-tuple-element.31.refs_1_.work_in, f32[256,256]{1,0:T(8,128)} %get-tuple-element.32.lower_in, f32[256,256]{1,0:T(8,128)} %get-tuple-element.33.upper_in, bf16[256,1024]{1,0:T(8,128)(2,1)} %shard_map.19.refs_0_.refs_1_), custom_call_target="tpu_custom_call" | custom-call | flops 1000000000 | bytes 2097152 | tf_op jit(solution)/shard_map/pallas_call | solution.py:215
  85.9 17.7 %shard_map.21.refs_0_.refs_2_ = bf16[256,1024]{1,0:T(8,128)(2,1)} custom-call(s32[2]{0:T(128)} %pad_add_fusion.place_ref, bf16[3584,7168]{1,0:T(8,128)(2,1)} %matrix.27, bf16[256,1024]{1,0:T(8,128)(2,1)} %copy-done.15, bf16[256,1024]{1,0:T(8,128)(2,1)} %copy-done.9, f32[256,256]{1,0:T(8,128)} %get-tuple-element.34.refs_1_.work_in), custom_call_target="tpu_custom_call" | custom-call | tf_op jit(solution)/shard_map/pallas_call | solution.py:240
  105.6 4.6 %shard_map.22 = (f32[256,256]{1,0:T(8,128)}, f32[256,256]{1,0:T(8,128)}, f32[256,256]{1,0:T(8,128)}) custom-call(f32[256,256]{1,0:T(8,128)} %get-tuple-element.34.refs_1_.work_in, f32[256,256]{1,0:T(8,128)} %get-tuple-element.35.lower_in, f32[256,256]{1,0:T(8,128)} %get-tuple-element.36.upper_in, bf16[256,1024]{1,0:T(8,128)(2,1)} %shard_map.21.refs_0_.refs_2_), custom_call_target="tpu_custom_call" | custom-call | flops 1000000000 | bytes 2097152 | tf_op jit(solution)/shard_map/pallas_call | solution.py:215
  110.2 16.5 %collective-permute-done.12.received = bf16[256,1024]{1,0:T(8,128)(2,1)S(1)} collective-permute-done((bf16[256,1024]{1,0:T(8,128)(2,1)}, bf16[256,1024]{1,0:T(8,128)(2,1)S(1)}, u32[]{:S(2)}, u32[]{:S(2)}) %collective-permute-start.12) | collective-permute-done | bytes 524320 | tf_op jit(solution)/shard_map/ppermute | solution.py:458
  127.8 17.7 %shard_map.23.refs_0_.refs_3_.refs_1_ = bf16[256,1024]{1,0:T(8,128)(2,1)} custom-call(s32[2]{0:T(128)} %pad_add_fusion.place_ref, bf16[3584,7168]{1,0:T(8,128)(2,1)} %matrix.27, bf16[256,1024]{1,0:T(8,128)(2,1)} %copy-done.16, bf16[256,1024]{1,0:T(8,128)(2,1)} %copy-done.2, f32[256,256]{1,0:T(8,128)} %get-tuple-element.37.refs_1_.work_in), custom_call_target="tpu_custom_call" | custom-call | tf_op jit(solution)/shard_map/pallas_call | solution.py:240
  146.7 1.5 collective-permute-start.15
  148.3 4.6 %shard_map.24 = (f32[256,256]{1,0:T(8,128)}, f32[256,256]{1,0:T(8,128)}, f32[256,256]{1,0:T(8,128)}) custom-call(f32[256,256]{1,0:T(8,128)} %get-tuple-element.37.refs_1_.work_in, f32[256,256]{1,0:T(8,128)} %get-tuple-element.38.lower_in, f32[256,256]{1,0:T(8,128)} %get-tuple-element.39.upper_in, bf16[256,1024]{1,0:T(8,128)(2,1)} %shard_map.23.refs_0_.refs_3_.refs_1_), custom_call_target="tpu_custom_call" | custom-call | flops 1000000000 | bytes 2097152 | tf_op jit(solution)/shard_map/pallas_call | solution.py:215
  152.9 8.6 %collective-permute-done.14.received = bf16[256,1024]{1,0:T(8,128)(2,1)S(1)} collective-permute-done((bf16[256,1024]{1,0:T(8,128)(2,1)}, bf16[256,1024]{1,0:T(8,128)(2,1)S(1)}, u32[]{:S(2)}, u32[]{:S(2)}) %collective-permute-start.14) | collective-permute-done | bytes 524320 | tf_op jit(solution)/shard_map/ppermute | solution.py:458
  162.5 17.7 %shard_map.25.refs_0_.refs_4_.refs_2_ = bf16[256,1024]{1,0:T(8,128)(2,1)} custom-call(s32[2]{0:T(128)} %pad_add_fusion.place_ref, bf16[3584,7168]{1,0:T(8,128)(2,1)} %matrix.27, bf16[256,1024]{1,0:T(8,128)(2,1)} %copy-done.17, bf16[256,1024]{1,0:T(8,128)(2,1)} %copy-done.3, f32[256,256]{1,0:T(8,128)} %get-tuple-element.42.refs_1_.packed_first), custom_call_target="tpu_custom_call" | custom-call | tf_op jit(solution)/shard_map/pallas_call | solution.py:240
  180.2 1.5 collective-permute-start.16
  181.7 1.7 collective-permute-start.17
  183.3 1.7 broadcast_select_fusion.own
  185.1 5.9 %shard_map.26 = (f32[256,256]{1,0:T(8,128)}, f32[256,256]{1,0:T(8,128)}, f32[256,256]{1,0:T(8,128)}, bf16[256,256]{1,0:T(8,128)(2,1)}, bf16[256,256]{1,0:T(8,128)(2,1)}) custom-call(s32[2]{0:T(128)} %pad_add_fusion.place_ref, bf16[256,256]{1,0:T(8,128)(2,1)} %copy-done.23, bf16[256,256]{1,0:T(8,128)(2,1)} %copy-done.25, bf16[256,256]{1,0:T(8,128)(2,1)} %copy-done.21, ...), custom_call_target="tpu_custom_call" | custom-call | flops 1000000000 | bytes 2097152 | tf_op jit(solution)/shard_map/pallas_call | solution.py:215
  191.1 3.6 collective-permute-done.16.received
  195.7 17.7 %shard_map.27.refs_0_.refs_3_.refs_1_ = bf16[256,1024]{1,0:T(8,128)(2,1)} custom-call(s32[2]{0:T(128)} %pad_add_fusion.place_ref, bf16[3584,7168]{1,0:T(8,128)(2,1)} %matrix.27, bf16[256,1024]{1,0:T(8,128)(2,1)} %copy-done.12, bf16[256,1024]{1,0:T(8,128)(2,1)} %copy-done, f32[256,256]{1,0:T(8,128)} %get-tuple-element.43.refs_1_.work_in), custom_call_target="tpu_custom_call" | custom-call | tf_op jit(solution)/shard_map/pallas_call | solution.py:240
  214.6 1.8 collective-permute-start.19
  216.5 4.6 %shard_map.28 = (f32[256,256]{1,0:T(8,128)}, f32[256,256]{1,0:T(8,128)}, f32[256,256]{1,0:T(8,128)}) custom-call(f32[256,256]{1,0:T(8,128)} %get-tuple-element.43.refs_1_.work_in, f32[256,256]{1,0:T(8,128)} %get-tuple-element.44.lower_in, f32[256,256]{1,0:T(8,128)} %get-tuple-element.45.upper_in, bf16[256,1024]{1,0:T(8,128)(2,1)} %shard_map.27.refs_0_.refs_3_.refs_1_), custom_call_target="tpu_custom_call" | custom-call | flops 1000000000 | bytes 2097152 | tf_op jit(solution)/shard_map/pallas_call | solution.py:215
  221.1 6.2 %collective-permute-done.18.received = bf16[256,1024]{1,0:T(8,128)(2,1)S(1)} collective-permute-done((bf16[256,1024]{1,0:T(8,128)(2,1)}, bf16[256,1024]{1,0:T(8,128)(2,1)S(1)}, u32[]{:S(2)}, u32[]{:S(2)}) %collective-permute-start.18) | collective-permute-done | bytes 524320 | tf_op jit(solution)/shard_map/ppermute | solution.py:458
  228.3 17.7 %shard_map.29.refs_0_.refs_4_.refs_2_ = bf16[256,1024]{1,0:T(8,128)(2,1)} custom-call(s32[2]{0:T(128)} %pad_add_fusion.place_ref, bf16[3584,7168]{1,0:T(8,128)(2,1)} %matrix.27, bf16[256,1024]{1,0:T(8,128)(2,1)} %copy-done.20, bf16[256,1024]{1,0:T(8,128)(2,1)} %copy-done.4, f32[256,256]{1,0:T(8,128)} %get-tuple-element.46.refs_1_.work_in), custom_call_target="tpu_custom_call" | custom-call | tf_op jit(solution)/shard_map/pallas_call | solution.py:240
  248.0 4.6 %shard_map.30 = (f32[256,256]{1,0:T(8,128)}, f32[256,256]{1,0:T(8,128)}, f32[256,256]{1,0:T(8,128)}) custom-call(f32[256,256]{1,0:T(8,128)} %get-tuple-element.46.refs_1_.work_in, f32[256,256]{1,0:T(8,128)} %get-tuple-element.47.lower_in, f32[256,256]{1,0:T(8,128)} %get-tuple-element.48.upper_in, bf16[256,1024]{1,0:T(8,128)(2,1)} %shard_map.29.refs_0_.refs_4_.refs_2_), custom_call_target="tpu_custom_call" | custom-call | flops 1000000000 | bytes 2097152 | tf_op jit(solution)/shard_map/pallas_call | solution.py:215
  252.6 6.9 %collective-permute-done.20.received = bf16[256,1024]{1,0:T(8,128)(2,1)S(1)} collective-permute-done((bf16[256,1024]{1,0:T(8,128)(2,1)}, bf16[256,1024]{1,0:T(8,128)(2,1)S(1)}, u32[]{:S(2)}, u32[]{:S(2)}) %collective-permute-start.20) | collective-permute-done | bytes 524320 | tf_op jit(solution)/shard_map/ppermute | solution.py:458
  260.6 17.7 %shard_map.31.refs_0_.refs_3_.refs_1_ = bf16[256,1024]{1,0:T(8,128)(2,1)} custom-call(s32[2]{0:T(128)} %pad_add_fusion.place_ref, bf16[3584,7168]{1,0:T(8,128)(2,1)} %matrix.27, bf16[256,1024]{1,0:T(8,128)(2,1)} %copy-done.18, bf16[256,1024]{1,0:T(8,128)(2,1)} %copy-done.1, f32[256,256]{1,0:T(8,128)} %get-tuple-element.49.refs_1_.work_in), custom_call_target="tpu_custom_call" | custom-call | tf_op jit(solution)/shard_map/pallas_call | solution.py:240
  279.6 1.9 collective-permute-start.23
  281.5 4.6 %shard_map.32 = (f32[256,256]{1,0:T(8,128)}, f32[256,256]{1,0:T(8,128)}, f32[256,256]{1,0:T(8,128)}) custom-call(f32[256,256]{1,0:T(8,128)} %get-tuple-element.49.refs_1_.work_in, f32[256,256]{1,0:T(8,128)} %get-tuple-element.50.lower_in, f32[256,256]{1,0:T(8,128)} %get-tuple-element.51.upper_in, bf16[256,1024]{1,0:T(8,128)(2,1)} %shard_map.31.refs_0_.refs_3_.refs_1_), custom_call_target="tpu_custom_call" | custom-call | flops 1000000000 | bytes 2097152 | tf_op jit(solution)/shard_map/pallas_call | solution.py:215
  286.1 4.8 %collective-permute-done.22.received = bf16[256,1024]{1,0:T(8,128)(2,1)S(1)} collective-permute-done((bf16[256,1024]{1,0:T(8,128)(2,1)}, bf16[256,1024]{1,0:T(8,128)(2,1)S(1)}, u32[]{:S(2)}, u32[]{:S(2)}) %collective-permute-start.22) | collective-permute-done | bytes 524320 | tf_op jit(solution)/shard_map/ppermute | solution.py:458
  290.9 1.3 collective-permute-done.23.refs_0_.refs_8_.refs_5_
  293.0 17.7 %shard_map.33.refs_0_.refs_4_.refs_2_ = bf16[256,1024]{1,0:T(8,128)(2,1)} custom-call(s32[2]{0:T(128)} %pad_add_fusion.place_ref, bf16[3584,7168]{1,0:T(8,128)(2,1)} %matrix.27, bf16[256,1024]{1,0:T(8,128)(2,1)} %copy-done.19, bf16[256,1024]{1,0:T(8,128)(2,1)} %copy-done.5, f32[256,256]{1,0:T(8,128)} %get-tuple-element.54.refs_1_.packed_second), custom_call_target="tpu_custom_call" | custom-call | tf_op jit(solution)/shard_map/pallas_call | solution.py:240
  312.0 2.4 collective-permute-start.25
  315.6 7.6 %shard_map.34.left_ref.refs_10_ = bf16[3584,512]{1,0:T(8,128)(2,1)} custom-call(s32[2]{0:T(128)} %pad_add_fusion.place_ref, bf16[3584,256]{1,0:T(8,128)(2,1)} %copy-done.10, bf16[3584,256]{1,0:T(8,128)(2,1)} %copy-done.24, f32[256,256]{1,0:T(8,128)} %get-tuple-element.40.inv_upper.inv_first, f32[256,256]{1,0:T(8,128)} %get-tuple-element.52.inv_second, ...), custom_call_target="tpu_custom_call" | custom-call | flops 3288334336 | bytes 7340032 | tf_op jit(solution)/shard_map/pallas_call | solution.py:272
  323.3 23.1 %shard_map.35.refs_10_ = bf16[3584,7168]{1,0:T(8,128)(2,1)} custom-call(s32[2]{0:T(128)} %pad_add_fusion.place_ref, bf16[3584,7168]{1,0:T(8,128)(2,1)} %matrix.27, bf16[3584,512]{1,0:T(8,128)(2,1)} %shard_map.34.left_ref.refs_10_, f32[256,256]{1,0:T(8,128)} %get-tuple-element.42.refs_1_.packed_first, f32[256,256]{1,0:T(8,128)} %get-tuple-element.54.refs_1_.packed_second, ...), custom_call_target="tpu_custom_call" | custom-call | flops 11274289152 | bytes 44040192 | tf_op jit(solution)/shard_map/pallas_call | solution.py:382
  346.4 22.8 %shard_map.36.refs_1_.refs_11_ = bf16[3584,7168]{1,0:T(8,128)(2,1)} custom-call(s32[2]{0:T(128)} %pad_add_fusion.place_ref, bf16[3584,7168]{1,0:T(8,128)(2,1)} %matrix.27, bf16[3584,512]{1,0:T(8,128)(2,1)} %shard_map.34.left_ref.refs_10_, f32[256,256]{1,0:T(8,128)} %get-tuple-element.42.refs_1_.packed_first, ...), custom_call_target="tpu_custom_call", output_to_operand_aliasing={{}: (18, {})} | custom-call | flops 11274289152 | bytes 44040192 | tf_op jit(solution)/shard_map/pallas_call | solution.py:382
  370.8 17.7 %shard_map.37.refs_10_.refs_3_ = bf16[256,1024]{1,0:T(8,128)(2,1)} custom-call(s32[2]{0:T(128)} %pad_add_fusion.place_ref, bf16[3584,7168]{1,0:T(8,128)(2,1)} %matrix.27, bf16[256,1024]{1,0:T(8,128)(2,1)} %copy-done.13, bf16[256,1024]{1,0:T(8,128)(2,1)} %copy-done.6, bf16[3584,7168]{1,0:T(8,128)(2,1)} %shard_map.36.refs_1_.refs_11_), custom_call_target="tpu_custom_call" | custom-call | tf_op jit(solution)/shard_map/pallas_call | solution.py:240
  388.5 3.6 collective-permute-start.26
  392.1 22.8 %shard_map.38.refs_8_ = bf16[3584,7168]{1,0:T(8,128)(2,1)} custom-call(s32[2]{0:T(128)} %pad_add_fusion.place_ref, bf16[3584,7168]{1,0:T(8,128)(2,1)} %matrix.27, bf16[3584,512]{1,0:T(8,128)(2,1)} %shard_map.34.left_ref.refs_10_, f32[256,256]{1,0:T(8,128)} %get-tuple-element.42.refs_1_.packed_first, ...), custom_call_target="tpu_custom_call", output_to_operand_aliasing={{}: (19, {})} | custom-call | flops 11274289152 | bytes 44040192 | tf_op jit(solution)/shard_map/pallas_call | solution.py:382
  415.8 13.7 %shard_map.39 = bf16[3584,7168]{1,0:T(8,128)(2,1)} custom-call(s32[2]{0:T(128)} %pad_add_fusion.place_ref, bf16[3584,7168]{1,0:T(8,128)(2,1)} %matrix.27, bf16[3584,512]{1,0:T(8,128)(2,1)} %shard_map.34.left_ref.refs_10_, f32[256,256]{1,0:T(8,128)} %get-tuple-element.42.refs_1_.packed_first, ...), custom_call_target="tpu_custom_call", output_to_operand_aliasing={{}: (16, {})} | custom-call | flops 5637144576 | bytes 22020096 | tf_op jit(solution)/shard_map/pallas_call | solution.py:382
  (90 shorter events, 29.7 us)
Async XLA Ops:
  0.9 6.1 %collective-permute-start.2 = (bf16[256,256]{1,0:T(8,128)(2,1)S(1)}, bf16[256,256]{1,0:T(8,128)(2,1)S(1)}, u32[]{:S(2)}, u32[]{:S(2)}) collective-permute-start(bf16[256,256]{1,0:T(8,128)(2,1)S(1)} %slice.13), channel_id=1, source_target_pairs={{0,2},{1,3},{4,6},{5,7},{8,10},{9,11},{12,14},{13,15},{16,18},{17,... | collective-permute-start | bytes 393224 | tf_op jit(solution)/shard_map/ppermute | solution.py:414
  8.0 0.7 collective-permute-start.3
  8.7 11.9 %collective-permute-start.4 = (bf16[256,256]{1,0:T(8,128)(2,1)S(1)}, bf16[256,256]{1,0:T(8,128)(2,1)S(1)}, u32[]{:S(2)}, u32[]{:S(2)}) collective-permute-start(bf16[256,256]{1,0:T(8,128)(2,1)S(1)} %broadcast_select_fusion.2), channel_id=1, source_target_pairs={{0,8},{4,12},{16,24},{20,28},{1,9},{5,13},{17,25},{21,29},{2,10},{... | collective-permute-start | bytes 393224 | tf_op jit(solution)/shard_map/ppermute | solution.py:414
  20.6 34.4 %copy-start.23 = (bf16[256,256]{1,0:T(8,128)(2,1)}, bf16[256,256]{1,0:T(8,128)(2,1)S(1)}, u32[]{:S(2)}) copy-start(bf16[256,256]{1,0:T(8,128)(2,1)S(1)} %broadcast_select_fusion.3.d0) | copy-start | bytes 393220
  21.1 5.4 %collective-permute-start.6 = (bf16[256,256]{1,0:T(8,128)(2,1)S(1)}, bf16[256,256]{1,0:T(8,128)(2,1)S(1)}, u32[]{:S(2)}, u32[]{:S(2)}) collective-permute-start(bf16[256,256]{1,0:T(8,128)(2,1)S(1)} %broadcast_select_fusion.3.d0), channel_id=1, source_target_pairs={{0,4},{4,0},{8,12},{12,8},{16,20},{20,16},{24,28},{28,24},{1,5},{5... | collective-permute-start | bytes 393224 | tf_op jit(solution)/shard_map/ppermute | solution.py:439
  22.7 5.8 %collective-permute-start.7 = (bf16[256,256]{1,0:T(8,128)(2,1)S(1)}, bf16[256,256]{1,0:T(8,128)(2,1)S(1)}, u32[]{:S(2)}, u32[]{:S(2)}) collective-permute-start(bf16[256,256]{1,0:T(8,128)(2,1)S(1)} %broadcast_select_fusion.3.d0), channel_id=1, source_target_pairs={{0,5},{1,4},{2,7},{3,6},{4,1},{5,0},{6,3},{7,2},{8,13},{9,12},{10,... | collective-permute-start | bytes 393224 | tf_op jit(solution)/shard_map/ppermute | solution.py:440
  24.4 4.1 copy-start.7
  24.4 35.9 %collective-permute-start.8 = (bf16[256,1024]{1,0:T(8,128)(2,1)S(1)}, bf16[256,1024]{1,0:T(8,128)(2,1)S(1)}, u32[]{:S(2)}, u32[]{:S(2)}) collective-permute-start(bf16[256,1024]{1,0:T(8,128)(2,1)S(1)} %slice_select_fusion.received.refs_0_), channel_id=1, source_target_pairs={{0,8},{4,12},{1,9},{5,13},{2,10},{6,14},{3,11},{7,15}} | collective-permute-start | bytes 1572872 | tf_op jit(solution)/shard_map/ppermute | solution.py:458
  26.6 1.9 copy-start.21
  46.8 13.5 %collective-permute-start.9 = (bf16[256,1024]{1,0:T(8,128)(2,1)}, bf16[256,1024]{1,0:T(8,128)(2,1)S(1)}, u32[]{:S(2)}, u32[]{:S(2)}) collective-permute-start(bf16[256,1024]{1,0:T(8,128)(2,1)} %shard_map.18), channel_id=1, source_target_pairs={{0,4},{4,0},{1,5},{5,1},{2,6},{6,2},{3,7},{7,3}} | collective-permute-start | bytes 1572872 | tf_op jit(solution)/shard_map/ppermute | solution.py:462
  49.1 134.3 %collective-permute-start = (bf16[3584,256]{1,0:T(8,128)(2,1)S(1)}, bf16[3584,256]{1,0:T(8,128)(2,1)S(1)}, u32[]{:S(2)}, u32[]{:S(2)}) collective-permute-start(bf16[3584,256]{1,0:T(8,128)(2,1)S(1)} %slice.12), channel_id=1, source_target_pairs={{0,2},{1,3},{4,6},{5,7},{8,10},{9,11},{12,14},{13,15},{16,18},{17,... | collective-permute-start | bytes 5505032 | tf_op jit(solution)/shard_map/ppermute | solution.py:414
  53.6 1.4 collective-permute-start.5
  60.3 0.8 copy-start.11
  60.3 1.0 copy-start.8
  78.9 6.0 %collective-permute-start.10 = (bf16[256,1024]{1,0:T(8,128)(2,1)}, bf16[256,1024]{1,0:T(8,128)(2,1)S(1)}, u32[]{:S(2)}, u32[]{:S(2)}) collective-permute-start(bf16[256,1024]{1,0:T(8,128)(2,1)} %shard_map.19.refs_0_.refs_1_), channel_id=1, source_target_pairs={{0,8},{4,12},{8,16},{12,20},{1,9},{5,13},{9,17},{13,21},{2,10},{6,... | collective-permute-start | bytes 1572872 | tf_op jit(solution)/shard_map/ppermute | solution.py:458
  79.6 5.3 %collective-permute-start.11 = (bf16[256,1024]{1,0:T(8,128)(2,1)}, bf16[256,1024]{1,0:T(8,128)(2,1)S(1)}, u32[]{:S(2)}, u32[]{:S(2)}) collective-permute-start(bf16[256,1024]{1,0:T(8,128)(2,1)} %shard_map.19.refs_0_.refs_1_), channel_id=1, source_target_pairs={{0,4},{4,0},{8,12},{12,8},{1,5},{5,1},{9,13},{13,9},{2,6},{6,2},{1... | collective-permute-start | bytes 1572872 | tf_op jit(solution)/shard_map/ppermute | solution.py:462
  84.9 0.8 copy-start.15
  84.9 1.0 copy-start.9
  103.6 23.2 %collective-permute-start.12 = (bf16[256,1024]{1,0:T(8,128)(2,1)}, bf16[256,1024]{1,0:T(8,128)(2,1)S(1)}, u32[]{:S(2)}, u32[]{:S(2)}) collective-permute-start(bf16[256,1024]{1,0:T(8,128)(2,1)} %shard_map.21.refs_0_.refs_2_), channel_id=1, source_target_pairs={{0,8},{4,12},{8,16},{12,20},{16,24},{20,28},{1,9},{5,13},{9,17},{1... | collective-permute-start | bytes 1572872 | tf_op jit(solution)/shard_map/ppermute | solution.py:458
  104.9 21.9 %collective-permute-start.13 = (bf16[256,1024]{1,0:T(8,128)(2,1)}, bf16[256,1024]{1,0:T(8,128)(2,1)S(1)}, u32[]{:S(2)}, u32[]{:S(2)}) collective-permute-start(bf16[256,1024]{1,0:T(8,128)(2,1)} %shard_map.21.refs_0_.refs_2_), channel_id=1, source_target_pairs={{0,4},{4,0},{8,12},{12,8},{16,20},{20,16},{1,5},{5,1},{9,13},{13,9... | collective-permute-start | bytes 1572872 | tf_op jit(solution)/shard_map/ppermute | solution.py:462
  126.8 1.0 copy-start.2
  145.4 16.1 %collective-permute-start.14 = (bf16[256,1024]{1,0:T(8,128)(2,1)}, bf16[256,1024]{1,0:T(8,128)(2,1)S(1)}, u32[]{:S(2)}, u32[]{:S(2)}) collective-permute-start(bf16[256,1024]{1,0:T(8,128)(2,1)} %shard_map.23.refs_0_.refs_3_.refs_1_), channel_id=1, source_target_pairs={{0,8},{4,12},{8,16},{12,20},{16,24},{20,28},{1,9},{5,13},{9,17},{1... | collective-permute-start | bytes 1572872 | tf_op jit(solution)/shard_map/ppermute | solution.py:458
  146.7 14.8 %collective-permute-start.15 = (bf16[256,1024]{1,0:T(8,128)(2,1)}, bf16[256,1024]{1,0:T(8,128)(2,1)S(1)}, u32[]{:S(2)}, u32[]{:S(2)}) collective-permute-start(bf16[256,1024]{1,0:T(8,128)(2,1)} %shard_map.23.refs_0_.refs_3_.refs_1_), channel_id=1, source_target_pairs={{0,4},{4,0},{8,12},{12,8},{16,20},{20,16},{24,28},{28,24},{1,5},{5... | collective-permute-start | bytes 1572872 | tf_op jit(solution)/shard_map/ppermute | solution.py:462
  161.5 1.0 copy-start.3
  180.2 14.5 %collective-permute-start.16 = (bf16[256,1024]{1,0:T(8,128)(2,1)}, bf16[256,1024]{1,0:T(8,128)(2,1)S(1)}, u32[]{:S(2)}, u32[]{:S(2)}) collective-permute-start(bf16[256,1024]{1,0:T(8,128)(2,1)} %shard_map.25.refs_0_.refs_4_.refs_2_), channel_id=1, source_target_pairs={{0,8},{4,12},{8,16},{12,20},{16,24},{20,28},{1,9},{5,13},{9,17},{1... | collective-permute-start | bytes 1572872 | tf_op jit(solution)/shard_map/ppermute | solution.py:458
  181.7 13.0 %collective-permute-start.17 = (bf16[256,1024]{1,0:T(8,128)(2,1)}, bf16[256,1024]{1,0:T(8,128)(2,1)S(1)}, u32[]{:S(2)}, u32[]{:S(2)}) collective-permute-start(bf16[256,1024]{1,0:T(8,128)(2,1)} %shard_map.25.refs_0_.refs_4_.refs_2_), channel_id=1, source_target_pairs={{0,4},{4,0},{8,12},{12,8},{16,20},{20,16},{24,28},{28,24},{1,5},{5... | collective-permute-start | bytes 1572872 | tf_op jit(solution)/shard_map/ppermute | solution.py:462
  185.0 61.0 %copy-start.10 = (bf16[3584,256]{1,0:T(8,128)(2,1)}, bf16[3584,256]{1,0:T(8,128)(2,1)S(1)}, u32[]{:S(2)}) copy-start(bf16[3584,256]{1,0:T(8,128)(2,1)S(1)} %broadcast_select_fusion.own) | copy-start | bytes 5505028
  185.0 129.3 %collective-permute-start.1 = (bf16[3584,256]{1,0:T(8,128)(2,1)S(1)}, bf16[3584,256]{1,0:T(8,128)(2,1)S(1)}, u32[]{:S(2)}, u32[]{:S(2)}) collective-permute-start(bf16[3584,256]{1,0:T(8,128)(2,1)S(1)} %broadcast_select_fusion.own), channel_id=1, source_target_pairs={{0,1},{1,0},{2,3},{3,2},{4,5},{5,4},{6,7},{7,6},{8,9},{9,8},{10,11... | collective-permute-start | bytes 5505032 | tf_op jit(solution)/shard_map/ppermute | solution.py:467
  194.7 0.8 copy-start.12
  194.7 1.0 copy-start
  213.3 14.0 %collective-permute-start.18 = (bf16[256,1024]{1,0:T(8,128)(2,1)}, bf16[256,1024]{1,0:T(8,128)(2,1)S(1)}, u32[]{:S(2)}, u32[]{:S(2)}) collective-permute-start(bf16[256,1024]{1,0:T(8,128)(2,1)} %shard_map.27.refs_0_.refs_3_.refs_1_), channel_id=1, source_target_pairs={{0,8},{4,12},{8,16},{12,20},{16,24},{20,28},{1,9},{5,13},{9,17},{1... | collective-permute-start | bytes 1572872 | tf_op jit(solution)/shard_map/ppermute | solution.py:458
  214.6 12.7 %collective-permute-start.19 = (bf16[256,1024]{1,0:T(8,128)(2,1)}, bf16[256,1024]{1,0:T(8,128)(2,1)S(1)}, u32[]{:S(2)}, u32[]{:S(2)}) collective-permute-start(bf16[256,1024]{1,0:T(8,128)(2,1)} %shard_map.27.refs_0_.refs_3_.refs_1_), channel_id=1, source_target_pairs={{0,4},{4,0},{8,12},{12,8},{16,20},{20,16},{24,28},{28,24},{1,5},{5... | collective-permute-start | bytes 1572872 | tf_op jit(solution)/shard_map/ppermute | solution.py:462
  227.3 0.8 copy-start.20
  227.3 1.0 copy-start.4
  246.0 13.6 %collective-permute-start.20 = (bf16[256,1024]{1,0:T(8,128)(2,1)}, bf16[256,1024]{1,0:T(8,128)(2,1)S(1)}, u32[]{:S(2)}, u32[]{:S(2)}) collective-permute-start(bf16[256,1024]{1,0:T(8,128)(2,1)} %shard_map.29.refs_0_.refs_4_.refs_2_), channel_id=1, source_target_pairs={{0,8},{4,12},{8,16},{12,20},{16,24},{20,28},{1,9},{5,13},{9,17},{1... | collective-permute-start | bytes 1572872 | tf_op jit(solution)/shard_map/ppermute | solution.py:458
  247.3 12.3 %collective-permute-start.21 = (bf16[256,1024]{1,0:T(8,128)(2,1)}, bf16[256,1024]{1,0:T(8,128)(2,1)S(1)}, u32[]{:S(2)}, u32[]{:S(2)}) collective-permute-start(bf16[256,1024]{1,0:T(8,128)(2,1)} %shard_map.29.refs_0_.refs_4_.refs_2_), channel_id=1, source_target_pairs={{0,4},{4,0},{8,12},{12,8},{16,20},{20,16},{24,28},{28,24},{1,5},{5... | collective-permute-start | bytes 1572872 | tf_op jit(solution)/shard_map/ppermute | solution.py:462
  259.6 0.8 copy-start.18
  259.6 1.0 copy-start.1
  278.3 12.6 %collective-permute-start.22 = (bf16[256,1024]{1,0:T(8,128)(2,1)}, bf16[256,1024]{1,0:T(8,128)(2,1)S(1)}, u32[]{:S(2)}, u32[]{:S(2)}) collective-permute-start(bf16[256,1024]{1,0:T(8,128)(2,1)} %shard_map.31.refs_0_.refs_3_.refs_1_), channel_id=1, source_target_pairs={{8,16},{12,20},{16,24},{20,28},{9,17},{13,21},{17,25},{21,29},{10,... | collective-permute-start | bytes 1572872 | tf_op jit(solution)/shard_map/ppermute | solution.py:458
  279.6 12.6 %collective-permute-start.23 = (bf16[256,1024]{1,0:T(8,128)(2,1)}, bf16[256,1024]{1,0:T(8,128)(2,1)S(1)}, u32[]{:S(2)}, u32[]{:S(2)}) collective-permute-start(bf16[256,1024]{1,0:T(8,128)(2,1)} %shard_map.31.refs_0_.refs_3_.refs_1_), channel_id=1, source_target_pairs={{8,12},{12,8},{16,20},{20,16},{24,28},{28,24},{9,13},{13,9},{17,21... | collective-permute-start | bytes 1572872 | tf_op jit(solution)/shard_map/ppermute | solution.py:462
  290.9 1.3 copy-start.19
  310.7 58.5 %collective-permute-start.24 = (bf16[256,1024]{1,0:T(8,128)(2,1)}, bf16[256,1024]{1,0:T(8,128)(2,1)S(1)}, u32[]{:S(2)}, u32[]{:S(2)}) collective-permute-start(bf16[256,1024]{1,0:T(8,128)(2,1)} %shard_map.33.refs_0_.refs_4_.refs_2_), channel_id=1, source_target_pairs={{16,24},{20,28},{17,25},{21,29},{18,26},{22,30},{19,27},{23,31}} | collective-permute-start | bytes 1572872 | tf_op jit(solution)/shard_map/ppermute | solution.py:458
  312.0 57.2 %collective-permute-start.25 = (bf16[256,1024]{1,0:T(8,128)(2,1)}, bf16[256,1024]{1,0:T(8,128)(2,1)S(1)}, u32[]{:S(2)}, u32[]{:S(2)}) collective-permute-start(bf16[256,1024]{1,0:T(8,128)(2,1)} %shard_map.33.refs_0_.refs_4_.refs_2_), channel_id=1, source_target_pairs={{16,20},{20,16},{24,28},{28,24},{17,21},{21,17},{25,29},{29,25},{1... | collective-permute-start | bytes 1572872 | tf_op jit(solution)/shard_map/ppermute | solution.py:462
  314.4 1.2 copy-start.24
  369.2 0.8 copy-start.13
  370.0 0.8 copy-start.6
  388.5 26.5 %collective-permute-start.26 = (bf16[256,1024]{1,0:T(8,128)(2,1)}, bf16[256,1024]{1,0:T(8,128)(2,1)S(1)}, u32[]{:S(2)}, u32[]{:S(2)}) collective-permute-start(bf16[256,1024]{1,0:T(8,128)(2,1)} %shard_map.37.refs_10_.refs_3_), channel_id=1, source_target_pairs={{24,28},{28,24},{25,29},{29,25},{26,30},{30,26},{27,31},{31,27}} | collective-permute-start | bytes 1572872 | tf_op jit(solution)/shard_map/ppermute | solution.py:462
  414.9 0.8 copy-start.14
  (5 other events, 3.7 us)

commit v3 on v2

--- a/solution.py
+++ b/solution.py
@@ -12,8 +12,10 @@
 MICRO = 8
 CHUNKS = 7
 ROW_TILES = 7
-PIECES = 4
-BATCHES = ((0, 2), (2, 4), (4, 6), (6, 7))
+PIECES = 2
+SLOTS = 4
+SPLIT = 4
+BATCHES = ((0, 1), (1, 2), (2, 3), (3, 4), (4, 5), (5, 6), (6, 7))
 LIMIT = 56 * 2**20
 
 
@@ -222,29 +224,46 @@
     )(*scalars, *operands, *extra)
 
 
-def gate_kernel(column, place_ref, matrix, received, *refs):
+def gate_kernel(column, place_ref, received, matrix, *refs):
     out, sem = refs[-2:]
 
     @pl.when(place_ref[0] < 2)
     def _():
-        pltpu.make_async_copy(matrix.at[pl.ds(0, NB), pl.ds(column, out.shape[1])], out, sem).start()
+        copy = pltpu.make_async_copy(
+            matrix.at[pl.ds(0, NB), pl.ds(column, out.shape[1])], out, sem
+        )
+        copy.start()
+        copy.wait()
 
     @pl.when(place_ref[0] >= 2)
     def _():
-        pltpu.make_async_copy(received, out, sem).start()
-
-    pltpu.make_async_copy(received, out, sem).wait()
+        out[...] = received[...]
 
 
 def gate_call(column, place, matrix, received, before):
     return pl.pallas_call(
         functools.partial(gate_kernel, column),
         out_shape=jax.ShapeDtypeStruct(received.shape, received.dtype),
-        in_specs=[smem()] + [anywhere() for _ in range(2 + len(before))],
-        out_specs=anywhere(),
+        in_specs=[smem(), vmem()] + [anywhere() for _ in range(1 + len(before))],
+        out_specs=vmem(),
         scratch_shapes=[pltpu.SemaphoreType.DMA(())],
         compiler_params=pltpu.CompilerParams(vmem_limit_bytes=LIMIT),
-    )(place, matrix, received, *before)
+    )(place, received, matrix, *before)
+
+
+def hold_kernel(*refs):
+    pass
+
+
+def hold_call(value, before):
+    return pl.pallas_call(
+        hold_kernel,
+        out_shape=jax.ShapeDtypeStruct(value.shape, value.dtype),
+        in_specs=[anywhere() for _ in range(1 + len(before))],
+        out_specs=anywhere(),
+        input_output_aliases={0: 0},
+        compiler_params=pltpu.CompilerParams(vmem_limit_bytes=LIMIT),
+    )(value, *before)
 
 
 def left_kernel(place_ref, own, other, inv_first, inv_second, top, *refs):
@@ -290,35 +309,65 @@
     )(place, own, other, inv_first, inv_second, top, *extra)
 
 
-def update_kernel(first, count, lines, n_extra, place_ref, matrix, left_ref, packed_first,
-                  packed_second, inv_first, inv_second, left_block, *refs):
+def update_kernel(first, count, lines, n_extra, place_ref, left_ref, packed_first, packed_second,
+                  inv_first, inv_second, left_block, matrix, *refs):
     n_sent = count + lines - 1
     own = refs[:n_sent]
     other = refs[n_sent : 2 * n_sent]
-    out, raw, top_ref, inv_ref, sems = refs[2 * n_sent + n_extra :]
-    j = pl.program_id(0)
-    i = pl.program_id(1)
+    out, raw, top_ref, inv_ref, reads, writes, raw_sems, read_sems, write_sems = refs[2 * n_sent + n_extra :]
     grid_row = place_ref[0]
     grid_col = place_ref[1]
     line = grid_row // 2
     parity = grid_row % 2
-    tile, width = out.shape
-
-    @pl.when((i == 0) & (j == 0))
-    def _():
-        for c in range(count):
-            for k in range(lines):
-                @pl.when(line == k)
-                def _():
-                    pltpu.make_async_copy(own[c + k], raw.at[parity, c], sems.at[0, c]).start()
-                    pltpu.make_async_copy(other[c + k], raw.at[1 - parity, c], sems.at[1, c]).start()
-        inv_ref[0] = jnp.concatenate(split2(inv_first[...]), axis=0)
-        inv_ref[1] = jnp.concatenate(split2(inv_second[...]), axis=0)
-
-    @pl.when(i == 0)
-    def _():
-        pltpu.make_async_copy(own[0], raw.at[parity, j], sems.at[0, j]).wait()
-        pltpu.make_async_copy(other[0], raw.at[1 - parity, j], sems.at[1, j]).wait()
+    tile, width = reads.shape[1:]
+    steps = count * ROW_TILES
+    part = tile // SPLIT
+
+    def window(step, begin, size):
+        top = pl.multiple_of(step % ROW_TILES * tile + begin, 16)
+        side = pl.multiple_of((first + step // ROW_TILES) * width, 128)
+        return pl.ds(top, size), pl.ds(side, width)
+
+    def read(step):
+        slot = step % SLOTS
+        for n in range(SPLIT):
+            pltpu.make_async_copy(
+                matrix.at[window(step, n * part, part)],
+                reads.at[slot, pl.ds(n * part, part)],
+                read_sems.at[slot],
+            ).start()
+
+    def wait_read(step):
+        slot = step % SLOTS
+        pltpu.make_async_copy(matrix.at[window(step, 0, tile)], reads.at[slot], read_sems.at[slot]).wait()
+
+    def write(step):
+        slot = step % SLOTS
+        for n in range(SPLIT):
+            pltpu.make_async_copy(
+                writes.at[slot, pl.ds(n * part, part)],
+                out.at[window(step, n * part, part)],
+                write_sems.at[slot],
+            ).start()
+
+    def wait_write(step):
+        slot = step % SLOTS
+        pltpu.make_async_copy(writes.at[slot], out.at[window(step, 0, tile)], write_sems.at[slot]).wait()
+
+    for c in range(count):
+        for k in range(lines):
+            @pl.when(line == k)
+            def _():
+                pltpu.make_async_copy(own[c + k], raw.at[parity, c], raw_sems.at[0, c]).start()
+                pltpu.make_async_copy(other[c + k], raw.at[1 - parity, c], raw_sems.at[1, c]).start()
+    for step in range(SLOTS - 1):
+        read(step)
+    inv_ref[0] = jnp.concatenate(split2(inv_first[...]), axis=0)
+    inv_ref[1] = jnp.concatenate(split2(inv_second[...]), axis=0)
+
+    def solve_top(j):
+        pltpu.make_async_copy(own[0], raw.at[parity, j], raw_sems.at[0, j]).wait()
+        pltpu.make_async_copy(other[0], raw.at[1 - parity, j], raw_sems.at[1, j]).wait()
         cols = lax.broadcasted_iota(jnp.int32, (NB, width), 1)
         outer = (cols >= NB) | (first + j > 0)
         top = times_left(inv_ref[0], raw[0, j])
@@ -329,44 +378,77 @@
         top = jnp.where(outer | (grid_col > 1), -top, 0.0).astype(jnp.bfloat16)
         top_ref[NB:, :] = top
 
-    for start in range(0, tile, NB):
-        rows = pl.ds(pl.multiple_of(i * tile + start, NB), NB)
-        here = slice(start, start + NB)
-        value = matrix[here, :].astype(jnp.float32) + dot(left_ref[rows, :NB], top_ref[:NB, :])
-        value = value.astype(jnp.bfloat16).astype(jnp.float32)
-        value = value + dot(left_ref[rows, NB:], top_ref[NB:, :])
-        out[here, :] = value.astype(jnp.bfloat16)
-
-    rows = pl.ds(pl.multiple_of(i * tile, tile), tile)
-
-    @pl.when((i == 0) & (grid_row == 0))
-    def _():
-        out[:NB, :] = -top_ref[:NB, :]
-
-    @pl.when((i == 0) & (grid_row == 1))
-    def _():
-        out[:NB, :] = -top_ref[NB:, :]
-
-    if first == 0:
-        @pl.when((j == 0) & (grid_col == 0))
+    def body(step, carry):
+        i = step % ROW_TILES
+        j = step // ROW_TILES
+        slot = step % SLOTS
+
+        @pl.when(step + SLOTS - 1 < steps)
         def _():
-            out[:, :NB] = left_ref[rows, :NB]
-
-        @pl.when((j == 0) & (grid_col == 1))
+            read(step + SLOTS - 1)
+
+        @pl.when(i == 0)
         def _():
-            out[:, :NB] = left_ref[rows, NB:]
-
-        @pl.when((j == 0) & (i == 0) & (grid_col == 0) & (grid_row == 0))
+            solve_top(j)
+
+        wait_read(step)
+
+        @pl.when(step >= SLOTS)
         def _():
-            out[:NB, :NB] = packed_first[...].astype(jnp.bfloat16)
-
-        @pl.when((j == 0) & (i == 0) & (grid_col == 1) & (grid_row == 0))
+            wait_write(step - SLOTS)
+
+        rows = pl.ds(pl.multiple_of(i * tile, NB), tile)
+        left = left_ref[rows, :]
+
+        def products(start):
+            cols = slice(start, min(start + NB, width))
+            return dot(left[:, :NB], top_ref[:NB, cols]), dot(left[:, NB:], top_ref[NB:, cols])
+
+        ahead = products(0)
+        for start in range(0, width, NB):
+            cols = slice(start, min(start + NB, width))
+            first_change, second_change = ahead
+            if start + NB < width:
+                ahead = products(start + NB)
+            value = reads[slot, :, cols].astype(jnp.float32) + first_change
+            value = value.astype(jnp.bfloat16).astype(jnp.float32) + second_change
+            writes[slot, :, cols] = value.astype(jnp.bfloat16)
+
+        @pl.when((i == 0) & (grid_row == 0))
         def _():
-            out[:NB, :NB] = -top_ref[:NB, :NB]
-
-        @pl.when((j == 0) & (i == 0) & (grid_col == 1) & (grid_row == 1))
+            writes[slot, :NB, :] = -top_ref[:NB, :]
+
+        @pl.when((i == 0) & (grid_row == 1))
         def _():
-            out[:NB, :NB] = packed_second[...].astype(jnp.bfloat16)
+            writes[slot, :NB, :] = -top_ref[NB:, :]
+
+        if first == 0:
+            @pl.when((j == 0) & (grid_col == 0))
+            def _():
+                writes[slot, :, :NB] = left_ref[rows, :NB]
+
+            @pl.when((j == 0) & (grid_col == 1))
+            def _():
+                writes[slot, :, :NB] = left_ref[rows, NB:]
+
+            @pl.when((j == 0) & (i == 0) & (grid_col == 0) & (grid_row == 0))
+            def _():
+                writes[slot, :NB, :NB] = packed_first[...].astype(jnp.bfloat16)
+
+            @pl.when((j == 0) & (i == 0) & (grid_col == 1) & (grid_row == 0))
+            def _():
+                writes[slot, :NB, :NB] = -top_ref[:NB, :NB]
+
+            @pl.when((j == 0) & (i == 0) & (grid_col == 1) & (grid_row == 1))
+            def _():
+                writes[slot, :NB, :NB] = packed_second[...].astype(jnp.bfloat16)
+
+        write(step)
+        return carry
+
+    lax.fori_loop(0, steps, body, 0)
+    for step in range(steps - SLOTS, steps):
+        wait_write(step)
 
 
 def update_call(first, last, lines, place, matrix, left, squares, left_block, own, other, extra, before):
@@ -375,23 +457,24 @@
     tile = rows // ROW_TILES
     count = last - first
     tail = list(extra) + ([] if before is None else [before])
-    whole = pl.BlockSpec((NB, NB), lambda j, i: (0, 0))
-    big = pl.BlockSpec((tile, width), lambda j, i: (i, j + first))
-    operands = [place, matrix, left, *squares, left_block, *own, *other, *tail]
+    operands = [place, left, *squares, left_block, matrix, *own, *other, *tail]
     aliases = {} if before is None else {len(operands) - 1: 0}
     return pl.pallas_call(
         functools.partial(update_kernel, first, count, lines, len(tail)),
-        grid=(count, ROW_TILES),
         out_shape=jax.ShapeDtypeStruct((rows, cols), jnp.bfloat16),
-        in_specs=[smem(), big, pl.BlockSpec((rows, 2 * NB), lambda j, i: (0, 0))]
-        + [whole] * 5
-        + [anywhere() for _ in range(len(own) + len(other) + len(tail))],
-        out_specs=big,
+        in_specs=[smem()]
+        + [vmem()] * 6
+        + [anywhere() for _ in range(1 + len(own) + len(other) + len(tail))],
+        out_specs=anywhere(),
         scratch_shapes=[
             pltpu.VMEM((2, count, NB, width), jnp.bfloat16),
             pltpu.VMEM((2 * NB, width), jnp.bfloat16),
             pltpu.VMEM((2, 2 * NB, NB), jnp.bfloat16),
+            pltpu.VMEM((SLOTS, tile, width), jnp.bfloat16),
+            pltpu.VMEM((SLOTS, tile, width), jnp.bfloat16),
             pltpu.SemaphoreType.DMA((2, count)),
+            pltpu.SemaphoreType.DMA((SLOTS,)),
+            pltpu.SemaphoreType.DMA((SLOTS,)),
         ],
         input_output_aliases=aliases,
         compiler_params=pltpu.CompilerParams(vmem_limit_bytes=LIMIT),
@@ -407,8 +490,8 @@
     return [(i, i ^ 1) for i in range(size)]
 
 
-def spread(block, axis, size, index):
-    stride = size // 2
+def spread(block, axis, reach, index, size):
+    stride = reach // 2
     while stride >= 2:
         pairs = [(i, i + stride) for i in range(size) if i % (2 * stride) < 2]
         moved = lax.ppermute(block, axis, pairs)
@@ -426,8 +509,8 @@
     lines = grid_rows // 2
     width = matrix.shape[1] // CHUNKS
 
-    diag = spread(matrix[:NB, :NB], "col", grid_cols, grid_col)
-    diag = spread(diag, "row", grid_rows, grid_row)
+    diag = spread(matrix[:NB, :NB], "col", grid_cols, grid_col, grid_cols)
+    diag = spread(diag, "row", grid_rows, grid_row, grid_rows)
     both_swap = [
         (i * grid_cols + j, (i ^ 1) * grid_cols + (j ^ 1))
         for i in range(grid_rows)
@@ -443,43 +526,49 @@
     n_ticks = CHUNKS + lines - 1
     own, other, received = [], [], []
 
-    def move(done, late=None):
+    def move(done):
         tick = len(own)
         if tick >= n_ticks:
-            return [] if tick > n_ticks else [done]
+            return done[:1]
         if tick == 0:
-            send = jnp.where(grid_row < 2, matrix[:NB, :width], done)
+            send = jnp.where(grid_row < 2, matrix[:NB, :width], diag[:1, :1])
         else:
             column = min(tick, CHUNKS - 1) * width
-            send = gate_call(column, place, matrix, received[-1], [other[-1], done])
+            send = gate_call(column, place, matrix, received[-1], [*other[-2:-1], *done])
         live = [k for k in range(lines) if 0 <= tick - k < CHUNKS]
         onward = [(2 * k + e, 2 * k + 2 + e) for k in live for e in range(2) if k + 1 < lines]
         across = [(2 * k + e, 2 * k + 1 - e) for k in live for e in range(2)]
         received.append(lax.ppermute(send, "row", onward) if onward else send)
         own.append(send)
         if tick == 0:
-            send = gate_call(0, place, matrix, send, late)
+            send = gate_call(0, place, matrix, send, done)
         other.append(lax.ppermute(send, "row", across))
-        return [own[tick]]
-
-    move(diag[:1, :1], blocks[2:])
-    column = spread(matrix[:, :NB], "col", grid_cols, grid_col)
-    column_other = lax.ppermute(column, "col", swap(grid_cols))
+        return [send]
+
+    move(blocks[2:])
+    extra = []
+    stride = grid_cols // 2
+    column = matrix[:, :NB]
+    pairs = [(i, i + stride) for i in range(grid_cols) if i % (2 * stride) < 2]
+    moved = lax.ppermute(column, "col", pairs)
 
     cost = 10**9
     per_piece = NB // W // PIECES
     kept = []
     for section in range(2):
         for piece in range(PIECES):
+            if section + piece > 0:
+                extra = move(square[:1])
+            if section > 0 and piece == 0:
+                moved = hold_call(moved, extra)
+                extra = [*extra, moved]
             if piece > 0:
-                extra = move(square[0])
                 body = functools.partial(next_kernel, piece * per_piece, per_piece, len(extra))
                 square = factor_call(body, 3, None, square, extra, cost)
             elif section == 0:
-                body = functools.partial(first_kernel, per_piece, 0)
-                square = factor_call(body, 3, place, blocks, [], cost)
+                body = functools.partial(first_kernel, per_piece, len(extra))
+                square = factor_call(body, 3, place, blocks, extra, cost)
             else:
-                extra = move(square[0])
                 body = functools.partial(second_kernel, per_piece, len(extra))
                 *square, left_block, top_block = factor_call(
                     body, 5, place, [*blocks, *kept[0][1:]], extra, cost
@@ -487,12 +576,15 @@
         kept.append(square)
 
     packed, lower, upper = zip(*kept)
-    left = left_call(place, column, column_other, *upper, top_block, move(square[0]))
+    column = jnp.where(grid_col % (2 * stride) >= stride, moved, column)
+    column = spread(column, "col", stride, grid_col, grid_cols)
+    column_other = lax.ppermute(column, "col", swap(grid_cols))
+    left = left_call(place, column, column_other, *upper, top_block, move(square[:1]))
     latest = left
     out = None
     for first, last in BATCHES:
         while len(own) < min(last + lines, n_ticks):
-            latest = move(latest)[0]
+            latest = move([latest])[0]
         sent = range(first, last + lines - 1)
         out = update_call(
             first, last, lines, place, matrix, left, (*packed, *lower), left_block,

time: 432 us -> 248 us (0.57)
  Pallas kernels: 305 us -> 140 us
  waiting for transfers between devices: 65.4 us -> 41.8 us
  local copies, waits for them, and re-layouts: 15.7 us -> 21.1 us
    pallas_call x10, Pallas kernels: 177 us -> 19.1 us  [gate_call(): pl.pallas_call(functools.partial(gate_kernel, column), out_shape=jax.Shap...]
    ppermute x9, waiting for transfers between devices: 46.7 us -> 27.4 us  [move(): received.append(lax.ppermute(send, 'row', onward) if onward else send)]
    pallas_call x8 -> x4, Pallas kernels: 38.3 us -> 30.8 us  [factor_call(): pl.pallas_call(body, out_shape=[square] * 3 + [panel] * (n_out - 3), in_s...]
    ppermute x4 -> x3, starting transfers between devices: 9.87 us -> 5.36 us  [spread(): moved = lax.ppermute(block, axis, pairs)]
    ppermute x0 -> x1, starting transfers between devices: none -> 4.49 us  [on_device(): moved = lax.ppermute(column, 'col', pairs)]
    ppermute x4 -> x3, waiting for transfers between devices: 12.7 us -> 8.26 us  [spread(): moved = lax.ppermute(block, axis, pairs)]
    unnamed x52 -> x56, local copies, waits for them, and re-layouts: 12.7 us -> 16.8 us
    pallas_call x4 -> x7, Pallas kernels: 82.4 us -> 83 us  [update_call(): pl.pallas_call(functools.partial(update_kernel, first, count, lines, len(...]
  transfers between devices with their start and end apart: 27 -> 27, of which waited for: 12 -> 9; matrix products, arithmetic and copies ran while one was open for 1% -> 2% of each run, Pallas kernels for 64% -> 52%
where the time goes in v3:
time: 248 us; the launch traced here: 246 us
  Pallas kernels  140 us (56%)
  waiting for transfers between devices  41.8 us (17%)
  starting transfers between devices  37 us (15%)
  local copies, waits for them, and re-layouts  21.1 us (9%)
  other arithmetic  4.97 us (2%)
    pallas_call x7, Pallas kernels, update_call(): pl.pallas_call(functools.partial(update_kernel, first, count, lines, len(...  83 us
    pallas_call x4, Pallas kernels, factor_call(): pl.pallas_call(body, out_shape=[square] * 3 + [panel] * (n_out - 3), in_s...  30.8 us
    ppermute x9, waiting for transfers between devices, move(): received.append(lax.ppermute(send, 'row', onward) if onward else send)  27.4 us
    pallas_call x10, Pallas kernels, gate_call(): pl.pallas_call(functools.partial(gate_kernel, column), out_shape=jax.Shap...  19.1 us
    unnamed x56, local copies, waits for them, and re-layouts  16.8 us
    ppermute x10, starting transfers between devices, move(): other.append(lax.ppermute(send, 'row', across))  14.2 us
    ppermute x9, starting transfers between devices, move(): received.append(lax.ppermute(send, 'row', onward) if onward else send)  10.9 us
    ppermute x3, waiting for transfers between devices, spread(): moved = lax.ppermute(block, axis, pairs)  8.26 us
  transfers between devices with their start and end apart: 27, of which 9 were waited for; matrix products, arithmetic and copies ran while one was open for 2% of the time, Pallas kernels for 52%

profile of v3, /device:TPU:24, one launch (start us, length us, event | category | flops | bytes accessed | tf_op | source)
XLA Modules:
  0.0 246.2 jit_solution(12404862201078589527)
XLA Ops:
  0.9 3.4 %collective-permute-start.1 = (bf16[256,256]{1,0:T(8,128)(2,1)S(1)}, bf16[256,256]{1,0:T(8,128)(2,1)S(1)}, u32[]{:S(2)}, u32[]{:S(2)}) collective-permute-start(bf16[256,256]{1,0:T(8,128)(2,1)S(1)} %slice.14), channel_id=1, source_target_pairs={{0,2},{1,3},{4,6},{5,7},{8,10},{9,11},{12,14},{13,15},{16,18},{17,... | collective-permute-start | bytes 393224 | tf_op jit(solution)/shard_map/ppermute | solution.py:497
  4.3 2.7 %collective-permute-done.1 = bf16[256,256]{1,0:T(8,128)(2,1)S(1)} collective-permute-done((bf16[256,256]{1,0:T(8,128)(2,1)S(1)}, bf16[256,256]{1,0:T(8,128)(2,1)S(1)}, u32[]{:S(2)}, u32[]{:S(2)}) %collective-permute-start.1) | collective-permute-done | bytes 131104 | tf_op jit(solution)/shard_map/ppermute | solution.py:497
  8.7 2.8 %slice.12 = bf16[3584,256]{1,0:T(8,128)(2,1)} slice(bf16[3584,7168]{1,0:T(8,128)(2,1)} %matrix.33), slice={[0:3584], [0:256]} | slice | bytes 3670016 | tf_op jit(solution)/shard_map/slice | solution.py:551
  11.5 4.5 %collective-permute-start = (bf16[3584,256]{1,0:T(8,128)(2,1)}, bf16[3584,256]{1,0:T(8,128)(2,1)S(1)}, u32[]{:S(2)}, u32[]{:S(2)}) collective-permute-start(bf16[3584,256]{1,0:T(8,128)(2,1)} %slice.12), channel_id=1, source_target_pairs={{0,2},{1,3},{4,6},{5,7},{8,10},{9,11},{12,14},{13,15},{16,18},{17,... | collective-permute-start | bytes 5505032 | tf_op jit(solution)/shard_map/ppermute | solution.py:553
  16.1 1.3 collective-permute-start.3
  17.4 5.5 %collective-permute-done.3 = bf16[256,256]{1,0:T(8,128)(2,1)S(1)} collective-permute-done((bf16[256,256]{1,0:T(8,128)(2,1)S(1)}, bf16[256,256]{1,0:T(8,128)(2,1)S(1)}, u32[]{:S(2)}, u32[]{:S(2)}) %collective-permute-start.3) | collective-permute-done | bytes 131104 | tf_op jit(solution)/shard_map/ppermute | solution.py:497
  23.5 1.7 slice_select_fusion.received.refs_0_
  26.0 1.6 collective-permute-start.6
  28.5 3.2 %collective-permute-done.7.d3.refs_1_ = bf16[256,256]{1,0:T(8,128)(2,1)S(1)} collective-permute-done((bf16[256,256]{1,0:T(8,128)(2,1)S(1)}, bf16[256,256]{1,0:T(8,128)(2,1)S(1)}, u32[]{:S(2)}, u32[]{:S(2)}) %collective-permute-start.7) | collective-permute-done | bytes 131104 | tf_op jit(solution)/shard_map/ppermute | solution.py:523
  31.7 2.9 %collective-permute-done.6.d2.refs_0_ = bf16[256,256]{1,0:T(8,128)(2,1)S(1)} collective-permute-done((bf16[256,256]{1,0:T(8,128)(2,1)S(1)}, bf16[256,256]{1,0:T(8,128)(2,1)S(1)}, u32[]{:S(2)}, u32[]{:S(2)}) %collective-permute-start.6) | collective-permute-done | bytes 131104 | tf_op jit(solution)/shard_map/ppermute | solution.py:522
  35.3 1.9 shard_map.19
  38.6 7.5 %shard_map.17 = (f32[256,256]{1,0:T(8,128)}, f32[256,256]{1,0:T(8,128)}, f32[256,256]{1,0:T(8,128)}) custom-call(s32[2]{0:T(128)} %pad_add_fusion.place_ref, bf16[256,256]{1,0:T(8,128)(2,1)} %copy-done.25, bf16[256,256]{1,0:T(8,128)(2,1)} %copy-done.27, bf16[256,256]{1,0:T(8,128)(2,1)} %copy-done.24, bf16[256,256]{1,0:T(8,128)(2,1)} %copy-done.23), custom_call_target="tpu_custom_call" | custom-call | flops 1000000000 | bytes 2097152 | tf_op jit(solution)/shard_map/pallas_call | solution.py:217
  46.9 1.9 shard_map.18.refs_0_.refs_1_
  49.6 7.5 %shard_map.20 = (f32[256,256]{1,0:T(8,128)}, f32[256,256]{1,0:T(8,128)}, f32[256,256]{1,0:T(8,128)}) custom-call(f32[256,256]{1,0:T(8,128)} %get-tuple-element.19.refs_0_.work_in, f32[256,256]{1,0:T(8,128)} %get-tuple-element.20.lower_in, f32[256,256]{1,0:T(8,128)} %get-tuple-element.21.upper_in, bf16[256,1024]{1,0:T(8,128)(2,1)} %shard_map.18.refs_0_.refs_1_), custom_call_target="tpu_custom_call" | custom-call | flops 1000000000 | bytes 2097152 | tf_op jit(solution)/shard_map/pallas_call | solution.py:217
  58.1 1.9 shard_map.21.refs_1_.refs_0_.refs_2_
  60.1 1.2 copy-done.6
  61.3 1.7 broadcast_select_fusion.own
  63.8 1.3 collective-permute-start.11
  65.8 8.3 %shard_map.23 = (f32[256,256]{1,0:T(8,128)}, f32[256,256]{1,0:T(8,128)}, f32[256,256]{1,0:T(8,128)}, bf16[256,256]{1,0:T(8,128)(2,1)}, bf16[256,256]{1,0:T(8,128)(2,1)}) custom-call(s32[2]{0:T(128)} %pad_add_fusion.place_ref, bf16[256,256]{1,0:T(8,128)(2,1)} %copy-done.25, bf16[256,256]{1,0:T(8,128)(2,1)} %copy-done.27, bf16[256,256]{1,0:T(8,128)(2,1)} %copy-done.24, ...), custom_call_target="tpu_custom_call" | custom-call | flops 1000000000 | bytes 2097152 | tf_op jit(solution)/shard_map/pallas_call | solution.py:217
  74.1 13.3 %collective-permute-done.11.received = bf16[256,1024]{1,0:T(8,128)(2,1)S(1)} collective-permute-done((bf16[256,1024]{1,0:T(8,128)(2,1)}, bf16[256,1024]{1,0:T(8,128)(2,1)S(1)}, u32[]{:S(2)}, u32[]{:S(2)}) %collective-permute-start.11) | collective-permute-done | bytes 524320 | tf_op jit(solution)/shard_map/ppermute | solution.py:541
  88.2 1.9 shard_map.24.refs_0_.refs_3_.refs_2_.refs_1_
  90.1 1.5 collective-permute-start.13
  91.7 7.4 %shard_map.25 = (f32[256,256]{1,0:T(8,128)}, f32[256,256]{1,0:T(8,128)}, f32[256,256]{1,0:T(8,128)}) custom-call(f32[256,256]{1,0:T(8,128)} %get-tuple-element.25.refs_1_.work_in, f32[256,256]{1,0:T(8,128)} %get-tuple-element.26.lower_in, f32[256,256]{1,0:T(8,128)} %get-tuple-element.27.upper_in, bf16[256,1024]{1,0:T(8,128)(2,1)} %shard_map.24.refs_0_.refs_3_.refs_2_.refs_1_), custom_call_target="tpu_custom_call" | custom-call | flops 1000000000 | bytes 2097152 | tf_op jit(solution)/shard_map/pallas_call | solution.py:217
  99.2 12.8 %collective-permute-done.13.received = bf16[256,1024]{1,0:T(8,128)(2,1)S(1)} collective-permute-done((bf16[256,1024]{1,0:T(8,128)(2,1)}, bf16[256,1024]{1,0:T(8,128)(2,1)S(1)}, u32[]{:S(2)}, u32[]{:S(2)}) %collective-permute-start.13) | collective-permute-done | bytes 524320 | tf_op jit(solution)/shard_map/ppermute | solution.py:541
  112.8 1.9 shard_map.26.refs_0_.refs_3_.refs_2_.refs_1_
  115.2 1.3 collective-permute-start.15
  116.5 1.2 copy-done.26
  117.7 7.7 %shard_map.27.left_ref.refs_8_ = bf16[3584,512]{1,0:T(8,128)(2,1)} custom-call(s32[2]{0:T(128)} %pad_add_fusion.place_ref, bf16[3584,256]{1,0:T(8,128)(2,1)} %copy-done.12, bf16[3584,256]{1,0:T(8,128)(2,1)} %copy-done.26, f32[256,256]{1,0:T(8,128)} %get-tuple-element.23.inv_upper.inv_first, f32[256,256]{1,0:T(8,128)} %get-tuple-element.28.inv_second, ...), custom_call_target="tpu_custom_call" | custom-call | flops 3288334336 | bytes 7340032 | tf_op jit(solution)/shard_map/pallas_call | solution.py:291
  126.1 12.1 %shard_map.28.refs_1_.refs_9_ = bf16[3584,7168]{1,0:T(8,128)(2,1)} custom-call(s32[2]{0:T(128)} %pad_add_fusion.place_ref, bf16[3584,512]{1,0:T(8,128)(2,1)} %shard_map.27.left_ref.refs_8_, f32[256,256]{1,0:T(8,128)} %get-tuple-element.22.refs_1_.packed_first, f32[256,256]{1,0:T(8,128)} %get-tuple-element.30.refs_1_.packed_second, ...), custom_call_target="tpu_custom_call" | custom-call | flops 5637144576 | bytes 22020096 | tf_op jit(solution)/shard_map/pallas_call | solution.py:462
  139.1 1.9 shard_map.29.refs_8_.refs_3_.refs_2_.refs_1_.refs_0_
  141.0 1.7 collective-permute-start.20
  142.7 1.3 collective-permute-start.17
  144.8 11.8 %shard_map.30.refs_1_.refs_9_ = bf16[3584,7168]{1,0:T(8,128)(2,1)} custom-call(s32[2]{0:T(128)} %pad_add_fusion.place_ref, bf16[3584,512]{1,0:T(8,128)(2,1)} %shard_map.27.left_ref.refs_8_, f32[256,256]{1,0:T(8,128)} %get-tuple-element.22.refs_1_.packed_first, f32[256,256]{1,0:T(8,128)} %get-tuple-element.30.refs_1_.packed_second, ...), custom_call_target="tpu_custom_call", output_to_operand_aliasing={{}: (17, {})} | custom-call | flops 5637144576 | bytes 22020096 | tf_op jit(solution)/shard_map/pallas_call | solution.py:462
  158.5 1.9 shard_map.31.refs_8_.refs_3_.refs_2_.refs_1_.refs_0_
  160.8 1.3 collective-permute-start.19
  162.9 11.8 %shard_map.32.refs_1_.refs_9_ = bf16[3584,7168]{1,0:T(8,128)(2,1)} custom-call(s32[2]{0:T(128)} %pad_add_fusion.place_ref, bf16[3584,512]{1,0:T(8,128)(2,1)} %shard_map.27.left_ref.refs_8_, f32[256,256]{1,0:T(8,128)} %get-tuple-element.22.refs_1_.packed_first, f32[256,256]{1,0:T(8,128)} %get-tuple-element.30.refs_1_.packed_second, ...), custom_call_target="tpu_custom_call", output_to_operand_aliasing={{}: (17, {})} | custom-call | flops 5637144576 | bytes 22020096 | tf_op jit(solution)/shard_map/pallas_call | solution.py:462
  175.6 1.9 shard_map.33.refs_8_.refs_3_.refs_2_.refs_1_
  177.5 3.6 %collective-permute-start.24 = (bf16[256,1024]{1,0:T(8,128)(2,1)}, bf16[256,1024]{1,0:T(8,128)(2,1)S(1)}, u32[]{:S(2)}, u32[]{:S(2)}) collective-permute-start(bf16[256,1024]{1,0:T(8,128)(2,1)} %shard_map.33.refs_8_.refs_3_.refs_2_.refs_1_), channel_id=1, source_target_pairs={{8,12},{12,8},{16,20},{20,16},{24,28},{28,24},{9,13},{13,9},{17,21... | collective-permute-start | bytes 1572872 | tf_op jit(solution)/shard_map/ppermute | solution.py:545
  181.1 1.3 collective-permute-start.21
  183.2 11.8 %shard_map.34.refs_1_.refs_9_ = bf16[3584,7168]{1,0:T(8,128)(2,1)} custom-call(s32[2]{0:T(128)} %pad_add_fusion.place_ref, bf16[3584,512]{1,0:T(8,128)(2,1)} %shard_map.27.left_ref.refs_8_, f32[256,256]{1,0:T(8,128)} %get-tuple-element.22.refs_1_.packed_first, f32[256,256]{1,0:T(8,128)} %get-tuple-element.30.refs_1_.packed_second, ...), custom_call_target="tpu_custom_call", output_to_operand_aliasing={{}: (17, {})} | custom-call | flops 5637144576 | bytes 22020096 | tf_op jit(solution)/shard_map/pallas_call | solution.py:462
  196.0 1.9 shard_map.35.refs_8_.refs_3_.refs_2_
  197.9 2.3 collective-permute-start.25
  200.1 1.5 collective-permute-start.23
  202.5 11.8 %shard_map.36.refs_1_.refs_9_ = bf16[3584,7168]{1,0:T(8,128)(2,1)} custom-call(s32[2]{0:T(128)} %pad_add_fusion.place_ref, bf16[3584,512]{1,0:T(8,128)(2,1)} %shard_map.27.left_ref.refs_8_, f32[256,256]{1,0:T(8,128)} %get-tuple-element.22.refs_1_.packed_first, f32[256,256]{1,0:T(8,128)} %get-tuple-element.30.refs_1_.packed_second, ...), custom_call_target="tpu_custom_call", output_to_operand_aliasing={{}: (17, {})} | custom-call | flops 5637144576 | bytes 22020096 | tf_op jit(solution)/shard_map/pallas_call | solution.py:462
  215.1 1.9 shard_map.37.refs_8_.refs_3_
  217.1 3.6 %collective-permute-start.26 = (bf16[256,1024]{1,0:T(8,128)(2,1)}, bf16[256,1024]{1,0:T(8,128)(2,1)S(1)}, u32[]{:S(2)}, u32[]{:S(2)}) collective-permute-start(bf16[256,1024]{1,0:T(8,128)(2,1)} %shard_map.37.refs_8_.refs_3_), channel_id=1, source_target_pairs={{24,28},{28,24},{25,29},{29,25},{26,30},{30,26},{27,31},{31,27}} | collective-permute-start | bytes 1572872 | tf_op jit(solution)/shard_map/ppermute | solution.py:545
  221.5 11.8 %shard_map.38.refs_8_ = bf16[3584,7168]{1,0:T(8,128)(2,1)} custom-call(s32[2]{0:T(128)} %pad_add_fusion.place_ref, bf16[3584,512]{1,0:T(8,128)(2,1)} %shard_map.27.left_ref.refs_8_, f32[256,256]{1,0:T(8,128)} %get-tuple-element.22.refs_1_.packed_first, f32[256,256]{1,0:T(8,128)} %get-tuple-element.30.refs_1_.packed_second, ...), custom_call_target="tpu_custom_call", output_to_operand_aliasing={{}: (17, {})} | custom-call | flops 5637144576 | bytes 22020096 | tf_op jit(solution)/shard_map/pallas_call | solution.py:462
  234.1 11.9 %shard_map.39 = bf16[3584,7168]{1,0:T(8,128)(2,1)} custom-call(s32[2]{0:T(128)} %pad_add_fusion.place_ref, bf16[3584,512]{1,0:T(8,128)(2,1)} %shard_map.27.left_ref.refs_8_, f32[256,256]{1,0:T(8,128)} %get-tuple-element.22.refs_1_.packed_first, f32[256,256]{1,0:T(8,128)} %get-tuple-element.30.refs_1_.packed_second, ...), custom_call_target="tpu_custom_call", output_to_operand_aliasing={{}: (16, {})} | custom-call | flops 5637144576 | bytes 22020096 | tf_op jit(solution)/shard_map/pallas_call | solution.py:462
  (94 shorter events, 24.3 us)
Async XLA Ops:
  0.9 6.1 %collective-permute-start.1 = (bf16[256,256]{1,0:T(8,128)(2,1)S(1)}, bf16[256,256]{1,0:T(8,128)(2,1)S(1)}, u32[]{:S(2)}, u32[]{:S(2)}) collective-permute-start(bf16[256,256]{1,0:T(8,128)(2,1)S(1)} %slice.14), channel_id=1, source_target_pairs={{0,2},{1,3},{4,6},{5,7},{8,10},{9,11},{12,14},{13,15},{16,18},{17,... | collective-permute-start | bytes 393224 | tf_op jit(solution)/shard_map/ppermute | solution.py:497
  8.0 8.0 %collective-permute-start.2 = (bf16[256,256]{1,0:T(8,128)(2,1)S(1)}, bf16[256,256]{1,0:T(8,128)(2,1)S(1)}, u32[]{:S(2)}, u32[]{:S(2)}) collective-permute-start(bf16[256,256]{1,0:T(8,128)(2,1)S(1)} %broadcast_select_fusion.1), channel_id=1, source_target_pairs={{0,16},{4,20},{1,17},{5,21},{2,18},{6,22},{3,19},{7,23}} | collective-permute-start | bytes 393224 | tf_op jit(solution)/shard_map/ppermute | solution.py:497
  11.5 48.6 %collective-permute-start = (bf16[3584,256]{1,0:T(8,128)(2,1)}, bf16[3584,256]{1,0:T(8,128)(2,1)S(1)}, u32[]{:S(2)}, u32[]{:S(2)}) collective-permute-start(bf16[3584,256]{1,0:T(8,128)(2,1)} %slice.12), channel_id=1, source_target_pairs={{0,2},{1,3},{4,6},{5,7},{8,10},{9,11},{12,14},{13,15},{16,18},{17,... | collective-permute-start | bytes 5505032 | tf_op jit(solution)/shard_map/ppermute | solution.py:553
  16.1 6.9 %collective-permute-start.3 = (bf16[256,256]{1,0:T(8,128)(2,1)S(1)}, bf16[256,256]{1,0:T(8,128)(2,1)S(1)}, u32[]{:S(2)}, u32[]{:S(2)}) collective-permute-start(bf16[256,256]{1,0:T(8,128)(2,1)S(1)} %broadcast_select_fusion.2), channel_id=1, source_target_pairs={{0,8},{4,12},{16,24},{20,28},{1,9},{5,13},{17,25},{21,29},{2,10},{... | collective-permute-start | bytes 393224 | tf_op jit(solution)/shard_map/ppermute | solution.py:497
  22.9 15.0 %copy-start.25 = (bf16[256,256]{1,0:T(8,128)(2,1)}, bf16[256,256]{1,0:T(8,128)(2,1)S(1)}, u32[]{:S(2)}) copy-start(bf16[256,256]{1,0:T(8,128)(2,1)S(1)} %broadcast_select_fusion.3.d0) | copy-start | bytes 393220
  25.2 9.4 %copy-start.9 = (bf16[256,1024]{1,0:T(8,128)(2,1)}, bf16[256,1024]{1,0:T(8,128)(2,1)S(1)}, u32[]{:S(2)}) copy-start(bf16[256,1024]{1,0:T(8,128)(2,1)S(1)} %slice_select_fusion.received.refs_0_) | copy-start | bytes 1572868
  25.3 20.8 %collective-permute-start.4 = (bf16[256,1024]{1,0:T(8,128)(2,1)S(1)}, bf16[256,1024]{1,0:T(8,128)(2,1)S(1)}, u32[]{:S(2)}, u32[]{:S(2)}) collective-permute-start(bf16[256,1024]{1,0:T(8,128)(2,1)S(1)} %slice_select_fusion.received.refs_0_), channel_id=1, source_target_pairs={{0,8},{4,12},{1,9},{5,13},{2,10},{6,14},{3,11},{7,15}} | collective-permute-start | bytes 1572872 | tf_op jit(solution)/shard_map/ppermute | solution.py:541
  26.0 5.8 %collective-permute-start.7 = (bf16[256,256]{1,0:T(8,128)(2,1)S(1)}, bf16[256,256]{1,0:T(8,128)(2,1)S(1)}, u32[]{:S(2)}, u32[]{:S(2)}) collective-permute-start(bf16[256,256]{1,0:T(8,128)(2,1)S(1)} %broadcast_select_fusion.3.d0), channel_id=1, source_target_pairs={{0,5},{1,4},{2,7},{3,6},{4,1},{5,0},{6,3},{7,2},{8,13},{9,12},{10,... | collective-permute-start | bytes 393224 | tf_op jit(solution)/shard_map/ppermute | solution.py:523
  26.0 8.6 %collective-permute-start.6 = (bf16[256,256]{1,0:T(8,128)(2,1)S(1)}, bf16[256,256]{1,0:T(8,128)(2,1)S(1)}, u32[]{:S(2)}, u32[]{:S(2)}) collective-permute-start(bf16[256,256]{1,0:T(8,128)(2,1)S(1)} %broadcast_select_fusion.3.d0), channel_id=1, source_target_pairs={{0,4},{4,0},{8,12},{12,8},{16,20},{20,16},{24,28},{28,24},{1,5},{5... | collective-permute-start | bytes 393224 | tf_op jit(solution)/shard_map/ppermute | solution.py:522
  27.6 10.3 %collective-permute-start.5 = (bf16[256,256]{1,0:T(8,128)(2,1)S(1)}, bf16[256,256]{1,0:T(8,128)(2,1)S(1)}, u32[]{:S(2)}, u32[]{:S(2)}) collective-permute-start(bf16[256,256]{1,0:T(8,128)(2,1)S(1)} %broadcast_select_fusion.3.d0), channel_id=1, source_target_pairs={{0,1},{1,0},{2,3},{3,2},{4,5},{5,4},{6,7},{7,6},{8,9},{9,8},{10,11... | collective-permute-start | bytes 393224 | tf_op jit(solution)/shard_map/ppermute | solution.py:521
  31.7 2.9 %copy-start.23 = (bf16[256,256]{1,0:T(8,128)(2,1)}, bf16[256,256]{1,0:T(8,128)(2,1)S(1)}, u32[]{:S(2)}) copy-start(bf16[256,256]{1,0:T(8,128)(2,1)S(1)} %collective-permute-done.7.d3.refs_1_) | copy-start | bytes 393220
  37.2 19.9 %collective-permute-start.9 = (bf16[256,1024]{1,0:T(8,128)(2,1)}, bf16[256,1024]{1,0:T(8,128)(2,1)S(1)}, u32[]{:S(2)}, u32[]{:S(2)}) collective-permute-start(bf16[256,1024]{1,0:T(8,128)(2,1)} %shard_map.19), channel_id=1, source_target_pairs={{0,4},{4,0},{1,5},{5,1},{2,6},{6,2},{3,7},{7,3}} | collective-permute-start | bytes 1572872 | tf_op jit(solution)/shard_map/ppermute | solution.py:545
  46.1 0.8 copy-start.13
  48.8 14.3 %copy-start.7 = (bf16[256,1024]{1,0:T(8,128)(2,1)S(1)}, bf16[256,1024]{1,0:T(8,128)(2,1)}, u32[]{:S(2)}) copy-start(bf16[256,1024]{1,0:T(8,128)(2,1)} %shard_map.18.refs_0_.refs_1_) | copy-start | bytes 1572868
  48.8 8.3 %collective-permute-start.8 = (bf16[256,1024]{1,0:T(8,128)(2,1)}, bf16[256,1024]{1,0:T(8,128)(2,1)S(1)}, u32[]{:S(2)}, u32[]{:S(2)}) collective-permute-start(bf16[256,1024]{1,0:T(8,128)(2,1)} %shard_map.18.refs_0_.refs_1_), channel_id=1, source_target_pairs={{0,8},{4,12},{8,16},{12,20},{1,9},{5,13},{9,17},{13,21},{2,10},{6,... | collective-permute-start | bytes 1572872 | tf_op jit(solution)/shard_map/ppermute | solution.py:541
  57.2 0.8 copy-start.10
  57.2 1.0 copy-start.18
  60.1 1.2 copy-start.6
  63.0 51.7 %copy-start.12 = (bf16[3584,256]{1,0:T(8,128)(2,1)}, bf16[3584,256]{1,0:T(8,128)(2,1)S(1)}, u32[]{:S(2)}) copy-start(bf16[3584,256]{1,0:T(8,128)(2,1)S(1)} %broadcast_select_fusion.own) | copy-start | bytes 5505028
  63.0 53.4 %collective-permute-start.10 = (bf16[3584,256]{1,0:T(8,128)(2,1)S(1)}, bf16[3584,256]{1,0:T(8,128)(2,1)S(1)}, u32[]{:S(2)}, u32[]{:S(2)}) collective-permute-start(bf16[3584,256]{1,0:T(8,128)(2,1)S(1)} %broadcast_select_fusion.own), channel_id=1, source_target_pairs={{0,1},{1,0},{2,3},{3,2},{4,5},{5,4},{6,7},{7,6},{8,9},{9,8},{10,11... | collective-permute-start | bytes 5505032 | tf_op jit(solution)/shard_map/ppermute | solution.py:581
  63.1 11.0 %collective-permute-start.12 = (bf16[256,1024]{1,0:T(8,128)(2,1)S(1)}, bf16[256,1024]{1,0:T(8,128)(2,1)S(1)}, u32[]{:S(2)}, u32[]{:S(2)}) collective-permute-start(bf16[256,1024]{1,0:T(8,128)(2,1)S(1)} %copy-done.7), channel_id=1, source_target_pairs={{0,4},{4,0},{8,12},{12,8},{1,5},{5,1},{9,13},{13,9},{2,6},{6,2},{1... | collective-permute-start | bytes 1572872 | tf_op jit(solution)/shard_map/ppermute | solution.py:545
  63.8 23.6 %collective-permute-start.11 = (bf16[256,1024]{1,0:T(8,128)(2,1)}, bf16[256,1024]{1,0:T(8,128)(2,1)S(1)}, u32[]{:S(2)}, u32[]{:S(2)}) collective-permute-start(bf16[256,1024]{1,0:T(8,128)(2,1)} %shard_map.21.refs_1_.refs_0_.refs_2_), channel_id=1, source_target_pairs={{0,8},{4,12},{8,16},{12,20},{16,24},{20,28},{1,9},{5,13},{9,17},{1... | collective-permute-start | bytes 1572872 | tf_op jit(solution)/shard_map/ppermute | solution.py:541
  65.1 34.0 %collective-permute-start.14 = (bf16[256,1024]{1,0:T(8,128)(2,1)}, bf16[256,1024]{1,0:T(8,128)(2,1)S(1)}, u32[]{:S(2)}, u32[]{:S(2)}) collective-permute-start(bf16[256,1024]{1,0:T(8,128)(2,1)} %shard_map.21.refs_1_.refs_0_.refs_2_), channel_id=1, source_target_pairs={{0,4},{4,0},{8,12},{12,8},{16,20},{20,16},{1,5},{5,1},{9,13},{13,9... | collective-permute-start | bytes 1572872 | tf_op jit(solution)/shard_map/ppermute | solution.py:545
  74.1 13.3 %copy-start.8 = (bf16[256,1024]{1,0:T(8,128)(2,1)}, bf16[256,1024]{1,0:T(8,128)(2,1)S(1)}, u32[]{:S(2)}) copy-start(bf16[256,1024]{1,0:T(8,128)(2,1)S(1)} %collective-permute-done.12.refs_0_.refs_5_.refs_4_) | copy-start | bytes 1572868
  90.1 21.8 %collective-permute-start.13 = (bf16[256,1024]{1,0:T(8,128)(2,1)}, bf16[256,1024]{1,0:T(8,128)(2,1)S(1)}, u32[]{:S(2)}, u32[]{:S(2)}) collective-permute-start(bf16[256,1024]{1,0:T(8,128)(2,1)} %shard_map.24.refs_0_.refs_3_.refs_2_.refs_1_), channel_id=1, source_target_pairs={{0,8},{4,12},{8,16},{12,20},{16,24},{20,28},{1,9},{5,13},{9,17},{1... | collective-permute-start | bytes 1572872 | tf_op jit(solution)/shard_map/ppermute | solution.py:541
  91.6 33.7 %collective-permute-start.16 = (bf16[256,1024]{1,0:T(8,128)(2,1)}, bf16[256,1024]{1,0:T(8,128)(2,1)S(1)}, u32[]{:S(2)}, u32[]{:S(2)}) collective-permute-start(bf16[256,1024]{1,0:T(8,128)(2,1)} %shard_map.24.refs_0_.refs_3_.refs_2_.refs_1_), channel_id=1, source_target_pairs={{0,4},{4,0},{8,12},{12,8},{16,20},{20,16},{24,28},{28,24},{1,5},{5... | collective-permute-start | bytes 1572872 | tf_op jit(solution)/shard_map/ppermute | solution.py:545
  99.2 12.8 %copy-start.4 = (bf16[256,1024]{1,0:T(8,128)(2,1)}, bf16[256,1024]{1,0:T(8,128)(2,1)S(1)}, u32[]{:S(2)}) copy-start(bf16[256,1024]{1,0:T(8,128)(2,1)S(1)} %collective-permute-done.14.refs_0_.refs_6_.refs_5_.refs_4_) | copy-start | bytes 1572868
  114.7 29.3 %collective-permute-start.18 = (bf16[256,1024]{1,0:T(8,128)(2,1)}, bf16[256,1024]{1,0:T(8,128)(2,1)S(1)}, u32[]{:S(2)}, u32[]{:S(2)}) collective-permute-start(bf16[256,1024]{1,0:T(8,128)(2,1)} %shard_map.26.refs_0_.refs_3_.refs_2_.refs_1_), channel_id=1, source_target_pairs={{0,4},{4,0},{8,12},{12,8},{16,20},{20,16},{24,28},{28,24},{1,5},{5... | collective-permute-start | bytes 1572872 | tf_op jit(solution)/shard_map/ppermute | solution.py:545
  115.2 23.1 %collective-permute-start.15 = (bf16[256,1024]{1,0:T(8,128)(2,1)}, bf16[256,1024]{1,0:T(8,128)(2,1)S(1)}, u32[]{:S(2)}, u32[]{:S(2)}) collective-permute-start(bf16[256,1024]{1,0:T(8,128)(2,1)} %shard_map.26.refs_0_.refs_3_.refs_2_.refs_1_), channel_id=1, source_target_pairs={{0,8},{4,12},{8,16},{12,20},{16,24},{20,28},{1,9},{5,13},{9,17},{1... | collective-permute-start | bytes 1572872 | tf_op jit(solution)/shard_map/ppermute | solution.py:541
  116.4 1.2 copy-start.26
  125.3 0.8 copy-start.1
  141.0 21.1 %collective-permute-start.20 = (bf16[256,1024]{1,0:T(8,128)(2,1)}, bf16[256,1024]{1,0:T(8,128)(2,1)S(1)}, u32[]{:S(2)}, u32[]{:S(2)}) collective-permute-start(bf16[256,1024]{1,0:T(8,128)(2,1)} %shard_map.29.refs_8_.refs_3_.refs_2_.refs_1_.refs_0_), channel_id=1, source_target_pairs={{0,4},{4,0},{8,12},{12,8},{16,20},{20,16},{24,28},{28,24},{1,5},{5... | collective-permute-start | bytes 1572872 | tf_op jit(solution)/shard_map/ppermute | solution.py:545
  142.7 14.9 %collective-permute-start.17 = (bf16[256,1024]{1,0:T(8,128)(2,1)}, bf16[256,1024]{1,0:T(8,128)(2,1)S(1)}, u32[]{:S(2)}, u32[]{:S(2)}) collective-permute-start(bf16[256,1024]{1,0:T(8,128)(2,1)} %shard_map.29.refs_8_.refs_3_.refs_2_.refs_1_.refs_0_), channel_id=1, source_target_pairs={{0,8},{4,12},{8,16},{12,20},{16,24},{20,28},{1,9},{5,13},{9,17},{1... | collective-permute-start | bytes 1572872 | tf_op jit(solution)/shard_map/ppermute | solution.py:541
  144.0 0.8 copy-start
  160.4 22.1 %collective-permute-start.22 = (bf16[256,1024]{1,0:T(8,128)(2,1)}, bf16[256,1024]{1,0:T(8,128)(2,1)S(1)}, u32[]{:S(2)}, u32[]{:S(2)}) collective-permute-start(bf16[256,1024]{1,0:T(8,128)(2,1)} %shard_map.31.refs_8_.refs_3_.refs_2_.refs_1_.refs_0_), channel_id=1, source_target_pairs={{0,4},{4,0},{8,12},{12,8},{16,20},{20,16},{24,28},{28,24},{1,5},{5... | collective-permute-start | bytes 1572872 | tf_op jit(solution)/shard_map/ppermute | solution.py:545
  160.8 14.0 %collective-permute-start.19 = (bf16[256,1024]{1,0:T(8,128)(2,1)}, bf16[256,1024]{1,0:T(8,128)(2,1)S(1)}, u32[]{:S(2)}, u32[]{:S(2)}) collective-permute-start(bf16[256,1024]{1,0:T(8,128)(2,1)} %shard_map.31.refs_8_.refs_3_.refs_2_.refs_1_.refs_0_), channel_id=1, source_target_pairs={{0,8},{4,12},{8,16},{12,20},{16,24},{20,28},{1,9},{5,13},{9,17},{1... | collective-permute-start | bytes 1572872 | tf_op jit(solution)/shard_map/ppermute | solution.py:541
  174.8 0.8 copy-start.20
  177.5 24.1 %collective-permute-start.24 = (bf16[256,1024]{1,0:T(8,128)(2,1)}, bf16[256,1024]{1,0:T(8,128)(2,1)S(1)}, u32[]{:S(2)}, u32[]{:S(2)}) collective-permute-start(bf16[256,1024]{1,0:T(8,128)(2,1)} %shard_map.33.refs_8_.refs_3_.refs_2_.refs_1_), channel_id=1, source_target_pairs={{8,12},{12,8},{16,20},{20,16},{24,28},{28,24},{9,13},{13,9},{17,21... | collective-permute-start | bytes 1572872 | tf_op jit(solution)/shard_map/ppermute | solution.py:545
  181.1 14.0 %collective-permute-start.21 = (bf16[256,1024]{1,0:T(8,128)(2,1)}, bf16[256,1024]{1,0:T(8,128)(2,1)S(1)}, u32[]{:S(2)}, u32[]{:S(2)}) collective-permute-start(bf16[256,1024]{1,0:T(8,128)(2,1)} %shard_map.33.refs_8_.refs_3_.refs_2_.refs_1_), channel_id=1, source_target_pairs={{8,16},{12,20},{16,24},{20,28},{9,17},{13,21},{17,25},{21,29},{10,... | collective-permute-start | bytes 1572872 | tf_op jit(solution)/shard_map/ppermute | solution.py:541
  182.4 0.8 copy-start.3
  195.2 0.8 copy-start.21
  197.9 22.8 %collective-permute-start.25 = (bf16[256,1024]{1,0:T(8,128)(2,1)}, bf16[256,1024]{1,0:T(8,128)(2,1)S(1)}, u32[]{:S(2)}, u32[]{:S(2)}) collective-permute-start(bf16[256,1024]{1,0:T(8,128)(2,1)} %shard_map.35.refs_8_.refs_3_.refs_2_), channel_id=1, source_target_pairs={{16,20},{20,16},{24,28},{28,24},{17,21},{21,17},{25,29},{29,25},{1... | collective-permute-start | bytes 1572872 | tf_op jit(solution)/shard_map/ppermute | solution.py:545
  200.1 14.2 %collective-permute-start.23 = (bf16[256,1024]{1,0:T(8,128)(2,1)}, bf16[256,1024]{1,0:T(8,128)(2,1)S(1)}, u32[]{:S(2)}, u32[]{:S(2)}) collective-permute-start(bf16[256,1024]{1,0:T(8,128)(2,1)} %shard_map.35.refs_8_.refs_3_.refs_2_), channel_id=1, source_target_pairs={{16,24},{20,28},{17,25},{21,29},{18,26},{22,30},{19,27},{23,31}} | collective-permute-start | bytes 1572872 | tf_op jit(solution)/shard_map/ppermute | solution.py:541
  201.7 0.8 copy-start.5
  214.3 0.8 copy-start.22
  217.1 16.2 %collective-permute-start.26 = (bf16[256,1024]{1,0:T(8,128)(2,1)}, bf16[256,1024]{1,0:T(8,128)(2,1)S(1)}, u32[]{:S(2)}, u32[]{:S(2)}) collective-permute-start(bf16[256,1024]{1,0:T(8,128)(2,1)} %shard_map.37.refs_8_.refs_3_), channel_id=1, source_target_pairs={{24,28},{28,24},{25,29},{29,25},{26,30},{30,26},{27,31},{31,27}} | collective-permute-start | bytes 1572872 | tf_op jit(solution)/shard_map/ppermute | solution.py:545
  220.7 0.8 copy-start.11
  233.3 0.8 copy-start.14
  (7 other events, 5.3 us)

commit v4 on v3

--- a/solution.py
+++ b/solution.py
@@ -16,7 +16,7 @@
 SLOTS = 4
 SPLIT = 4
 BATCHES = ((0, 1), (1, 2), (2, 3), (3, 4), (4, 5), (5, 6), (6, 7))
-LIMIT = 56 * 2**20
+MIB = 2**20
 
 
 def split3(x):
@@ -138,15 +138,11 @@
 
 
 def times_right(a, b):
-    width = b.shape[1]
-    both = dot(a, jnp.concatenate(split2(b), axis=1))
-    return both[:, :width] + both[:, width:]
+    return dot(jnp.concatenate([a, a], axis=1), jnp.concatenate(split2(b), axis=0))
 
 
 def times_left(a, b):
-    height = a.shape[0] // 2
-    both = dot(a, b)
-    return both[:height] + both[height:]
+    return dot(a, jnp.concatenate([b, b], axis=0))
 
 
 def run_steps(first, count, work_ref, lower_ref, upper_ref):
@@ -179,7 +175,7 @@
     blocks = (d0, d1, d2, d3)
     left = times_right(pick(place_ref, blocks, 1, 0).astype(jnp.bfloat16), inv_upper[...])
     left = left.astype(jnp.bfloat16)
-    top = times_left(jnp.concatenate(split2(inv_lower[...]), axis=0), pick(place_ref, blocks, 0, 1).astype(jnp.bfloat16))
+    top = times_left(jnp.concatenate(split2(inv_lower[...]), axis=1), pick(place_ref, blocks, 0, 1).astype(jnp.bfloat16))
     top = top.astype(jnp.bfloat16)
     left_ref[...] = left
     top_ref[...] = top
@@ -204,6 +200,10 @@
 
 def smem():
     return pl.BlockSpec(memory_space=pltpu.SMEM)
+
+
+def hbm():
+    return pl.BlockSpec(memory_space=pltpu.HBM)
 
 
 def anywhere():
@@ -219,7 +219,7 @@
         out_shape=[square] * 3 + [panel] * (n_out - 3),
         in_specs=[smem() for _ in scalars] + [vmem() for _ in operands] + [anywhere() for _ in extra],
         out_specs=[vmem()] * n_out,
-        compiler_params=pltpu.CompilerParams(vmem_limit_bytes=LIMIT),
+        compiler_params=pltpu.CompilerParams(vmem_limit_bytes=10 * MIB),
         cost_estimate=pl.CostEstimate(flops=flops, bytes_accessed=2**21, transcendentals=0),
     )(*scalars, *operands, *extra)
 
@@ -244,10 +244,10 @@
     return pl.pallas_call(
         functools.partial(gate_kernel, column),
         out_shape=jax.ShapeDtypeStruct(received.shape, received.dtype),
-        in_specs=[smem(), vmem()] + [anywhere() for _ in range(1 + len(before))],
+        in_specs=[smem(), vmem(), hbm()] + [anywhere() for _ in before],
         out_specs=vmem(),
         scratch_shapes=[pltpu.SemaphoreType.DMA(())],
-        compiler_params=pltpu.CompilerParams(vmem_limit_bytes=LIMIT),
+        compiler_params=pltpu.CompilerParams(vmem_limit_bytes=24 * MIB),
     )(place, received, matrix, *before)
 
 
@@ -262,7 +262,7 @@
         in_specs=[anywhere() for _ in range(1 + len(before))],
         out_specs=anywhere(),
         input_output_aliases={0: 0},
-        compiler_params=pltpu.CompilerParams(vmem_limit_bytes=LIMIT),
+        compiler_params=pltpu.CompilerParams(vmem_limit_bytes=MIB),
     )(value, *before)
 
 
@@ -302,7 +302,7 @@
         ]
         + [anywhere() for _ in extra],
         out_specs=pl.BlockSpec((tile, 2 * NB), lambda i: (i, 0)),
-        compiler_params=pltpu.CompilerParams(vmem_limit_bytes=LIMIT),
+        compiler_params=pltpu.CompilerParams(vmem_limit_bytes=12 * MIB),
         cost_estimate=pl.CostEstimate(
             flops=14 * rows * NB * NB, bytes_accessed=8 * rows * NB, transcendentals=0
         ),
@@ -362,8 +362,8 @@
                 pltpu.make_async_copy(other[c + k], raw.at[1 - parity, c], raw_sems.at[1, c]).start()
     for step in range(SLOTS - 1):
         read(step)
-    inv_ref[0] = jnp.concatenate(split2(inv_first[...]), axis=0)
-    inv_ref[1] = jnp.concatenate(split2(inv_second[...]), axis=0)
+    inv_ref[0] = jnp.concatenate(split2(inv_first[...]), axis=1)
+    inv_ref[1] = jnp.concatenate(split2(inv_second[...]), axis=1)
 
     def solve_top(j):
         pltpu.make_async_copy(own[0], raw.at[parity, j], raw_sems.at[0, j]).wait()
@@ -464,12 +464,14 @@
         out_shape=jax.ShapeDtypeStruct((rows, cols), jnp.bfloat16),
         in_specs=[smem()]
         + [vmem()] * 6
-        + [anywhere() for _ in range(1 + len(own) + len(other) + len(tail))],
-        out_specs=anywhere(),
+        + [hbm()]
+        + [anywhere() for _ in range(len(own) + len(other) + len(extra))]
+        + [hbm() for _ in tail[len(extra) :]],
+        out_specs=hbm(),
         scratch_shapes=[
             pltpu.VMEM((2, count, NB, width), jnp.bfloat16),
             pltpu.VMEM((2 * NB, width), jnp.bfloat16),
-            pltpu.VMEM((2, 2 * NB, NB), jnp.bfloat16),
+            pltpu.VMEM((2, NB, 2 * NB), jnp.bfloat16),
             pltpu.VMEM((SLOTS, tile, width), jnp.bfloat16),
             pltpu.VMEM((SLOTS, tile, width), jnp.bfloat16),
             pltpu.SemaphoreType.DMA((2, count)),
@@ -477,7 +479,7 @@
             pltpu.SemaphoreType.DMA((SLOTS,)),
         ],
         input_output_aliases=aliases,
-        compiler_params=pltpu.CompilerParams(vmem_limit_bytes=LIMIT),
+        compiler_params=pltpu.CompilerParams(vmem_limit_bytes=26 * MIB),
         cost_estimate=pl.CostEstimate(
             flops=6 * rows * NB * width * count,
             bytes_accessed=6 * rows * width * count,
@@ -540,15 +542,13 @@
         across = [(2 * k + e, 2 * k + 1 - e) for k in live for e in range(2)]
         received.append(lax.ppermute(send, "row", onward) if onward else send)
         own.append(send)
-        if tick == 0:
-            send = gate_call(0, place, matrix, send, done)
         other.append(lax.ppermute(send, "row", across))
         return [send]
 
     move(blocks[2:])
     extra = []
     stride = grid_cols // 2
-    column = matrix[:, :NB]
+    column = jnp.where(grid_col < 2, matrix[:, :NB], diag[:1, :1])
     pairs = [(i, i + stride) for i in range(grid_cols) if i % (2 * stride) < 2]
     moved = lax.ppermute(column, "col", pairs)
 

time: 248 us -> 201 us (0.81)
  Pallas kernels: 140 us -> 94.2 us
  local copies, waits for them, and re-layouts: 21.1 us -> 1.42 us
  waiting for transfers between devices: 41.8 us -> 56.2 us
  other arithmetic: 4.97 us -> 8.49 us
    pallas_call x7, Pallas kernels: 83 us -> 58.9 us  [update_call(): pl.pallas_call(functools.partial(update_kernel, first, count, lines, len(...]
    unnamed x56 -> x0, local copies, waits for them, and re-layouts: 16.8 us -> none
    pallas_call x10 -> x9, Pallas kernels: 19.1 us -> 5.34 us  [gate_call(): pl.pallas_call(functools.partial(gate_kernel, column), out_shape=jax.Shap...]
    ppermute x1, waiting for transfers between devices: 0.01 us -> 11.6 us  [on_device(): moved = lax.ppermute(column, 'col', pairs)]
    pallas_call x4, Pallas kernels: 30.8 us -> 24.3 us  [factor_call(): pl.pallas_call(body, out_shape=[square] * 3 + [panel] * (n_out - 3), in_s...]
    ppermute x3, waiting for transfers between devices: 8.26 us -> 13.2 us  [spread(): moved = lax.ppermute(block, axis, pairs)]
    select_n x0 -> x1, other arithmetic: none -> 3.42 us  [on_device(): column = jnp.where(grid_col < 2, matrix[:, :NB], diag[:1, :1])]
    slice x2 -> x1, local copies, waits for them, and re-layouts: 3.43 us -> 0.5 us  [on_device(): column = jnp.where(grid_col < 2, matrix[:, :NB], diag[:1, :1])]
  transfers between devices with their start and end apart: 27 -> 27, of which waited for: 9 -> 12; matrix products, arithmetic and copies ran while one was open for 2% -> 1% of each run, Pallas kernels for 52% -> 43%
where the time goes in v4:
time: 201 us; the launch traced here: 199 us
  Pallas kernels  94.2 us (47%)
  waiting for transfers between devices  56.2 us (28%)
  starting transfers between devices  38.3 us (19%)
  other arithmetic  8.49 us (4%)
    pallas_call x7, Pallas kernels, update_call(): pl.pallas_call(functools.partial(update_kernel, first, count, lines, len(...  58.9 us
    ppermute x9, waiting for transfers between devices, move(): received.append(lax.ppermute(send, 'row', onward) if onward else send)  25.1 us
    pallas_call x4, Pallas kernels, factor_call(): pl.pallas_call(body, out_shape=[square] * 3 + [panel] * (n_out - 3), in_s...  24.3 us
    ppermute x10, starting transfers between devices, move(): other.append(lax.ppermute(send, 'row', across))  15.7 us
    ppermute x3, waiting for transfers between devices, spread(): moved = lax.ppermute(block, axis, pairs)  13.2 us
    ppermute x1, waiting for transfers between devices, on_device(): moved = lax.ppermute(column, 'col', pairs)  11.6 us
    ppermute x9, starting transfers between devices, move(): received.append(lax.ppermute(send, 'row', onward) if onward else send)  10.8 us
    pallas_call x1, Pallas kernels, left_call(): pl.pallas_call(left_kernel, grid=(4,), out_shape=jax.ShapeDtypeStruct((ro...  5.63 us
  transfers between devices with their start and end apart: 27, of which 12 were waited for; matrix products, arithmetic and copies ran while one was open for 1% of the time, Pallas kernels for 43%

profile of v4, /device:TPU:24, one launch (start us, length us, event | category | flops | bytes accessed | tf_op | source)
XLA Modules:
  0.0 199.3 jit_solution(11884818460406518692)
XLA Ops:
  0.0 0.9 slice.14
  0.9 3.4 %collective-permute-start = (bf16[256,256]{1,0:T(8,128)(2,1)S(1)}, bf16[256,256]{1,0:T(8,128)(2,1)S(1)}, u32[]{:S(2)}, u32[]{:S(2)}) collective-permute-start(bf16[256,256]{1,0:T(8,128)(2,1)S(1)} %slice.14), channel_id=1, source_target_pairs={{0,2},{1,3},{4,6},{5,7},{8,10},{9,11},{12,14},{13,15},{16,18},{17,... | collective-permute-start | bytes 393224 | tf_op jit(solution)/shard_map/ppermute | solution.py:499
  4.3 2.7 %collective-permute-done = bf16[256,256]{1,0:T(8,128)(2,1)S(1)} collective-permute-done((bf16[256,256]{1,0:T(8,128)(2,1)S(1)}, bf16[256,256]{1,0:T(8,128)(2,1)S(1)}, u32[]{:S(2)}, u32[]{:S(2)}) %collective-permute-start) | collective-permute-done | bytes 131104 | tf_op jit(solution)/shard_map/ppermute | solution.py:499
  7.1 0.9 broadcast_select_fusion.1
  8.7 1.3 collective-permute-start.2
  10.0 10.5 %collective-permute-done.2 = bf16[256,256]{1,0:T(8,128)(2,1)S(1)} collective-permute-done((bf16[256,256]{1,0:T(8,128)(2,1)S(1)}, bf16[256,256]{1,0:T(8,128)(2,1)S(1)}, u32[]{:S(2)}, u32[]{:S(2)}) %collective-permute-start.2) | collective-permute-done | bytes 131104 | tf_op jit(solution)/shard_map/ppermute | solution.py:499
  21.1 3.4 %slice_select_fusion = bf16[3584,256]{1,0:T(8,128)(2,1)} fusion(bf16[3584,7168]{1,0:T(8,128)(2,1)} %matrix.31, pred[]{:T(512)S(6)} %lt.23, bf16[]{:T(256)} %bitcast.2), kind=kLoop, calls=%fused_computation | loop fusion | flops 917504 | bytes 3670019 | tf_op jit(solution)/shard_map/jit(_where)/select_n | solution.py:551
  24.5 4.5 %collective-permute-start.3 = (bf16[3584,256]{1,0:T(8,128)(2,1)}, bf16[3584,256]{1,0:T(8,128)(2,1)S(1)}, u32[]{:S(2)}, u32[]{:S(2)}) collective-permute-start(bf16[3584,256]{1,0:T(8,128)(2,1)} %slice_select_fusion), channel_id=1, source_target_pairs={{0,2},{1,3},{4,6},{5,7},{8,10},{9,11},{12,14},{13,15},{16,18},{17,... | collective-permute-start | bytes 5505032 | tf_op jit(solution)/shard_map/ppermute | solution.py:553
  29.0 1.6 slice_select_fusion.1.refs_0_
  30.7 0.7 collective-permute-start.4
  31.4 1.6 collective-permute-start.6
  33.4 3.8 %collective-permute-done.7.d3 = bf16[256,256]{1,0:T(8,128)(2,1)S(1)} collective-permute-done((bf16[256,256]{1,0:T(8,128)(2,1)S(1)}, bf16[256,256]{1,0:T(8,128)(2,1)S(1)}, u32[]{:S(2)}, u32[]{:S(2)}) %collective-permute-start.7) | collective-permute-done | bytes 131104 | tf_op jit(solution)/shard_map/ppermute | solution.py:525
  37.8 2.2 %collective-permute-done.6.d2 = bf16[256,256]{1,0:T(8,128)(2,1)S(1)} collective-permute-done((bf16[256,256]{1,0:T(8,128)(2,1)S(1)}, bf16[256,256]{1,0:T(8,128)(2,1)S(1)}, u32[]{:S(2)}, u32[]{:S(2)}) %collective-permute-start.6) | collective-permute-done | bytes 131104 | tf_op jit(solution)/shard_map/ppermute | solution.py:524
  40.0 6.2 %shard_map.17 = (f32[256,256]{1,0:T(8,128)S(1)}, f32[256,256]{1,0:T(8,128)S(1)}, f32[256,256]{1,0:T(8,128)S(1)}) custom-call(s32[2]{0:T(128)S(1)} %pad_add_fusion.place_ref, bf16[256,256]{1,0:T(8,128)(2,1)S(1)} %broadcast_select_fusion.3.d0, bf16[256,256]{1,0:T(8,128)(2,1)S(1)} %collective-permute-done.5.d1, bf16[256,256]{1,0:T(8,128)(2,1)S(1)} %collective-permute-done.6.d2, ...), custom_call_target="tpu_custom_call" | custom-call | flops 1000000000 | bytes 2097152 | tf_op jit(solution)/shard_map/pallas_call | solution.py:217
  46.9 0.7 collective-permute-start.8
  47.6 5.7 %shard_map.19 = (f32[256,256]{1,0:T(8,128)S(1)}, f32[256,256]{1,0:T(8,128)S(1)}, f32[256,256]{1,0:T(8,128)S(1)}) custom-call(f32[256,256]{1,0:T(8,128)S(1)} %get-tuple-element.19.refs_0_.work_in, f32[256,256]{1,0:T(8,128)S(1)} %get-tuple-element.20.lower_in, f32[256,256]{1,0:T(8,128)S(1)} %get-tuple-element.21.upper_in, ...), custom_call_target="tpu_custom_call" | custom-call | flops 1000000000 | bytes 2097152 | tf_op jit(solution)/shard_map/pallas_call | solution.py:217
  53.9 11.6 %collective-permute-done.3.refs_0_ = bf16[3584,256]{1,0:T(8,128)(2,1)S(1)} collective-permute-done((bf16[3584,256]{1,0:T(8,128)(2,1)}, bf16[3584,256]{1,0:T(8,128)(2,1)S(1)}, u32[]{:S(2)}, u32[]{:S(2)}) %collective-permute-start.3) | collective-permute-done | bytes 1835040 | tf_op jit(solution)/shard_map/ppermute | solution.py:553
  65.4 2.4 %broadcast_select_fusion.own = bf16[3584,256]{1,0:T(8,128)(2,1)S(1)} fusion(bf16[3584,256]{1,0:T(8,128)(2,1)S(1)} %shard_map.21.refs_1_, pred[]{:T(512)S(6)} %ge.10, bf16[]{:T(256)} %bitcast.2, bf16[3584,7168]{1,0:T(8,128)(2,1)} %matrix.31, pred[]{:T(512)S(6)} %lt.23), kind=kLoop, calls=%fused_computation.1 | loop fusion | flops 1835008 | bytes 5505028 | tf_op jit(solution)/shard_map/jit(_where)/select_n | solution.py:579
  68.6 1.3 collective-permute-start.11
  69.9 0.7 collective-permute-start.14
  70.6 6.8 %shard_map.22 = (f32[256,256]{1,0:T(8,128)S(1)}, f32[256,256]{1,0:T(8,128)S(1)}, f32[256,256]{1,0:T(8,128)S(1)}, bf16[256,256]{1,0:T(8,128)(2,1)S(1)}, bf16[256,256]{1,0:T(8,128)(2,1)S(1)}) custom-call(s32[2]{0:T(128)S(1)} %pad_add_fusion.place_ref, bf16[256,256]{1,0:T(8,128)(2,1)S(1)} %broadcast_select_fusion.3.d0, ...), custom_call_target="tpu_custom_call" | custom-call | flops 1000000000 | bytes 2097152 | tf_op jit(solution)/shard_map/pallas_call | solution.py:217
  77.4 7.4 %collective-permute-done.11.received = bf16[256,1024]{1,0:T(8,128)(2,1)S(1)} collective-permute-done((bf16[256,1024]{1,0:T(8,128)(2,1)S(1)}, bf16[256,1024]{1,0:T(8,128)(2,1)S(1)}, u32[]{:S(2)}, u32[]{:S(2)}) %collective-permute-start.11) | collective-permute-done | bytes 524320 | tf_op jit(solution)/shard_map/ppermute | solution.py:543
  85.4 1.5 collective-permute-start.13
  86.9 1.6 collective-permute-start.16
  88.5 5.6 %shard_map.24 = (f32[256,256]{1,0:T(8,128)S(1)}, f32[256,256]{1,0:T(8,128)S(1)}, f32[256,256]{1,0:T(8,128)S(1)}) custom-call(f32[256,256]{1,0:T(8,128)S(1)} %get-tuple-element.25.refs_1_.work_in, f32[256,256]{1,0:T(8,128)S(1)} %get-tuple-element.26.lower_in, f32[256,256]{1,0:T(8,128)S(1)} %get-tuple-element.27.upper_in, ...), custom_call_target="tpu_custom_call" | custom-call | flops 1000000000 | bytes 2097152 | tf_op jit(solution)/shard_map/pallas_call | solution.py:217
  94.1 6.7 %collective-permute-done.13.received = bf16[256,1024]{1,0:T(8,128)(2,1)S(1)} collective-permute-done((bf16[256,1024]{1,0:T(8,128)(2,1)S(1)}, bf16[256,1024]{1,0:T(8,128)(2,1)S(1)}, u32[]{:S(2)}, u32[]{:S(2)}) %collective-permute-start.13) | collective-permute-done | bytes 524320 | tf_op jit(solution)/shard_map/ppermute | solution.py:543
  101.4 1.6 collective-permute-start.18
  103.0 1.3 collective-permute-start.15
  104.3 5.6 %shard_map.26.left_ref.refs_8_ = bf16[3584,512]{1,0:T(8,128)(2,1)S(1)} custom-call(s32[2]{0:T(128)S(1)} %pad_add_fusion.place_ref, bf16[3584,256]{1,0:T(8,128)(2,1)S(1)} %broadcast_select_fusion.own, bf16[3584,256]{1,0:T(8,128)(2,1)S(1)} %collective-permute-done.10.other, f32[256,256]{1,0:T(8,128)S(1)} %get-tuple-element.23.inv_upper.inv_first, ...), custom_call_target="tpu_custom_call" | custom-call | flops 3288334336 | bytes 7340032 | tf_op jit(solution)/shard_map/pallas_call | solution.py:291
  110.0 8.7 %shard_map.27.refs_1_.refs_9_ = bf16[3584,7168]{1,0:T(8,128)(2,1)} custom-call(s32[2]{0:T(128)S(1)} %pad_add_fusion.place_ref, bf16[3584,512]{1,0:T(8,128)(2,1)S(1)} %shard_map.26.left_ref.refs_8_, f32[256,256]{1,0:T(8,128)S(1)} %get-tuple-element.22.refs_1_.packed_first, f32[256,256]{1,0:T(8,128)S(1)} %get-tuple-element.30.refs_1_.packed_second, ...), custom_call_target="tpu_custom_call" | custom-call | flops 5637144576 | bytes 22020096 | tf_op jit(solution)/shard_map/pallas_call | solution.py:462
  119.9 1.3 collective-permute-start.17
  121.2 8.4 %shard_map.29.refs_1_.refs_9_ = bf16[3584,7168]{1,0:T(8,128)(2,1)} custom-call(s32[2]{0:T(128)S(1)} %pad_add_fusion.place_ref, bf16[3584,512]{1,0:T(8,128)(2,1)S(1)} %shard_map.26.left_ref.refs_8_, f32[256,256]{1,0:T(8,128)S(1)} %get-tuple-element.22.refs_1_.packed_first, ...), custom_call_target="tpu_custom_call", output_to_operand_aliasing={{}: (17, {})} | custom-call | flops 5637144576 | bytes 22020096 | tf_op jit(solution)/shard_map/pallas_call | solution.py:462
  129.6 4.9 %collective-permute-done.17.received = bf16[256,1024]{1,0:T(8,128)(2,1)S(1)} collective-permute-done((bf16[256,1024]{1,0:T(8,128)(2,1)S(1)}, bf16[256,1024]{1,0:T(8,128)(2,1)S(1)}, u32[]{:S(2)}, u32[]{:S(2)}) %collective-permute-start.17) | collective-permute-done | bytes 524320 | tf_op jit(solution)/shard_map/ppermute | solution.py:543
  135.1 1.6 collective-permute-start.22
  136.7 1.3 collective-permute-start.19
  138.0 8.4 %shard_map.31.refs_1_.refs_9_ = bf16[3584,7168]{1,0:T(8,128)(2,1)} custom-call(s32[2]{0:T(128)S(1)} %pad_add_fusion.place_ref, bf16[3584,512]{1,0:T(8,128)(2,1)S(1)} %shard_map.26.left_ref.refs_8_, f32[256,256]{1,0:T(8,128)S(1)} %get-tuple-element.22.refs_1_.packed_first, ...), custom_call_target="tpu_custom_call", output_to_operand_aliasing={{}: (17, {})} | custom-call | flops 5637144576 | bytes 22020096 | tf_op jit(solution)/shard_map/pallas_call | solution.py:462
  146.3 3.1 %collective-permute-done.19.received = bf16[256,1024]{1,0:T(8,128)(2,1)S(1)} collective-permute-done((bf16[256,1024]{1,0:T(8,128)(2,1)S(1)}, bf16[256,1024]{1,0:T(8,128)(2,1)S(1)}, u32[]{:S(2)}, u32[]{:S(2)}) %collective-permute-start.19) | collective-permute-done | bytes 524320 | tf_op jit(solution)/shard_map/ppermute | solution.py:543
  150.0 2.4 %collective-permute-start.24 = (bf16[256,1024]{1,0:T(8,128)(2,1)S(1)}, bf16[256,1024]{1,0:T(8,128)(2,1)S(1)}, u32[]{:S(2)}, u32[]{:S(2)}) collective-permute-start(bf16[256,1024]{1,0:T(8,128)(2,1)S(1)} %shard_map.32.refs_8_.refs_3_.refs_2_.refs_1_), channel_id=1, source_target_pairs={{8,12},{12,8},{16,20},{20,16},{24,28},{28,24},{9,13},{13,9},{17,21... | collective-permute-start | bytes 1572872 | tf_op jit(solution)/shard_map/ppermute | solution.py:545
  152.4 1.3 collective-permute-start.21
  153.7 8.4 %shard_map.33.refs_1_.refs_9_ = bf16[3584,7168]{1,0:T(8,128)(2,1)} custom-call(s32[2]{0:T(128)S(1)} %pad_add_fusion.place_ref, bf16[3584,512]{1,0:T(8,128)(2,1)S(1)} %shard_map.26.left_ref.refs_8_, f32[256,256]{1,0:T(8,128)S(1)} %get-tuple-element.22.refs_1_.packed_first, ...), custom_call_target="tpu_custom_call", output_to_operand_aliasing={{}: (17, {})} | custom-call | flops 5637144576 | bytes 22020096 | tf_op jit(solution)/shard_map/pallas_call | solution.py:462
  162.1 1.9 collective-permute-done.21.received
  164.6 3.4 %collective-permute-start.25 = (bf16[256,1024]{1,0:T(8,128)(2,1)S(1)}, bf16[256,1024]{1,0:T(8,128)(2,1)S(1)}, u32[]{:S(2)}, u32[]{:S(2)}) collective-permute-start(bf16[256,1024]{1,0:T(8,128)(2,1)S(1)} %shard_map.34.refs_8_.refs_3_.refs_2_), channel_id=1, source_target_pairs={{16,20},{20,16},{24,28},{28,24},{17,21},{21,17},{25,29},{29,25},{1... | collective-permute-start | bytes 1572872 | tf_op jit(solution)/shard_map/ppermute | solution.py:545
  168.0 1.5 collective-permute-start.23
  169.5 8.4 %shard_map.35.refs_1_.refs_9_ = bf16[3584,7168]{1,0:T(8,128)(2,1)} custom-call(s32[2]{0:T(128)S(1)} %pad_add_fusion.place_ref, bf16[3584,512]{1,0:T(8,128)(2,1)S(1)} %shard_map.26.left_ref.refs_8_, f32[256,256]{1,0:T(8,128)S(1)} %get-tuple-element.22.refs_1_.packed_first, ...), custom_call_target="tpu_custom_call", output_to_operand_aliasing={{}: (17, {})} | custom-call | flops 5637144576 | bytes 22020096 | tf_op jit(solution)/shard_map/pallas_call | solution.py:462
  177.9 1.2 collective-permute-done.23.received
  179.7 2.4 %collective-permute-start.26 = (bf16[256,1024]{1,0:T(8,128)(2,1)S(1)}, bf16[256,1024]{1,0:T(8,128)(2,1)S(1)}, u32[]{:S(2)}, u32[]{:S(2)}) collective-permute-start(bf16[256,1024]{1,0:T(8,128)(2,1)S(1)} %shard_map.36.refs_8_.refs_3_), channel_id=1, source_target_pairs={{24,28},{28,24},{25,29},{29,25},{26,30},{30,26},{27,31},{31,27}} | collective-permute-start | bytes 1572872 | tf_op jit(solution)/shard_map/ppermute | solution.py:545
  182.1 8.4 %shard_map.37.refs_8_ = bf16[3584,7168]{1,0:T(8,128)(2,1)} custom-call(s32[2]{0:T(128)S(1)} %pad_add_fusion.place_ref, bf16[3584,512]{1,0:T(8,128)(2,1)S(1)} %shard_map.26.left_ref.refs_8_, f32[256,256]{1,0:T(8,128)S(1)} %get-tuple-element.22.refs_1_.packed_first, ...), custom_call_target="tpu_custom_call", output_to_operand_aliasing={{}: (17, {})} | custom-call | flops 5637144576 | bytes 22020096 | tf_op jit(solution)/shard_map/pallas_call | solution.py:462
  190.8 8.4 %shard_map.38 = bf16[3584,7168]{1,0:T(8,128)(2,1)} custom-call(s32[2]{0:T(128)S(1)} %pad_add_fusion.place_ref, bf16[3584,512]{1,0:T(8,128)(2,1)S(1)} %shard_map.26.left_ref.refs_8_, f32[256,256]{1,0:T(8,128)S(1)} %get-tuple-element.22.refs_1_.packed_first, f32[256,256]{1,0:T(8,128)S(1)} %get-tuple-element.30.refs_1_.packed_second, ...), custom_call_target="tpu_custom_call", output_to_operand_aliasing={{}: (16, {})} | custom-call | flops 5637144576 | bytes 22020096 | tf_op jit(solution)/shard_map/pallas_call | solution.py:462
  (37 shorter events, 9.3 us)
Async XLA Ops:
  0.9 6.1 %collective-permute-start = (bf16[256,256]{1,0:T(8,128)(2,1)S(1)}, bf16[256,256]{1,0:T(8,128)(2,1)S(1)}, u32[]{:S(2)}, u32[]{:S(2)}) collective-permute-start(bf16[256,256]{1,0:T(8,128)(2,1)S(1)} %slice.14), channel_id=1, source_target_pairs={{0,2},{1,3},{4,6},{5,7},{8,10},{9,11},{12,14},{13,15},{16,18},{17,... | collective-permute-start | bytes 393224 | tf_op jit(solution)/shard_map/ppermute | solution.py:499
  8.0 0.7 collective-permute-start.1
  8.7 11.9 %collective-permute-start.2 = (bf16[256,256]{1,0:T(8,128)(2,1)S(1)}, bf16[256,256]{1,0:T(8,128)(2,1)S(1)}, u32[]{:S(2)}, u32[]{:S(2)}) collective-permute-start(bf16[256,256]{1,0:T(8,128)(2,1)S(1)} %broadcast_select_fusion.2), channel_id=1, source_target_pairs={{0,8},{4,12},{16,24},{20,28},{1,9},{5,13},{17,25},{21,29},{2,10},{... | collective-permute-start | bytes 393224 | tf_op jit(solution)/shard_map/ppermute | solution.py:499
  24.5 40.9 %collective-permute-start.3 = (bf16[3584,256]{1,0:T(8,128)(2,1)}, bf16[3584,256]{1,0:T(8,128)(2,1)S(1)}, u32[]{:S(2)}, u32[]{:S(2)}) collective-permute-start(bf16[3584,256]{1,0:T(8,128)(2,1)} %slice_select_fusion), channel_id=1, source_target_pairs={{0,2},{1,3},{4,6},{5,7},{8,10},{9,11},{12,14},{13,15},{16,18},{17,... | collective-permute-start | bytes 5505032 | tf_op jit(solution)/shard_map/ppermute | solution.py:553
  30.7 15.6 %collective-permute-start.4 = (bf16[256,1024]{1,0:T(8,128)(2,1)S(1)}, bf16[256,1024]{1,0:T(8,128)(2,1)S(1)}, u32[]{:S(2)}, u32[]{:S(2)}) collective-permute-start(bf16[256,1024]{1,0:T(8,128)(2,1)S(1)} %slice_select_fusion.1.refs_0_), channel_id=1, source_target_pairs={{0,8},{4,12},{1,9},{5,13},{2,10},{6,14},{3,11},{7,15}} | collective-permute-start | bytes 1572872 | tf_op jit(solution)/shard_map/ppermute | solution.py:543
  31.4 5.8 %collective-permute-start.7 = (bf16[256,256]{1,0:T(8,128)(2,1)S(1)}, bf16[256,256]{1,0:T(8,128)(2,1)S(1)}, u32[]{:S(2)}, u32[]{:S(2)}) collective-permute-start(bf16[256,256]{1,0:T(8,128)(2,1)S(1)} %broadcast_select_fusion.3.d0), channel_id=1, source_target_pairs={{0,5},{1,4},{2,7},{3,6},{4,1},{5,0},{6,3},{7,2},{8,13},{9,12},{10,... | collective-permute-start | bytes 393224 | tf_op jit(solution)/shard_map/ppermute | solution.py:525
  31.4 8.6 %collective-permute-start.6 = (bf16[256,256]{1,0:T(8,128)(2,1)S(1)}, bf16[256,256]{1,0:T(8,128)(2,1)S(1)}, u32[]{:S(2)}, u32[]{:S(2)}) collective-permute-start(bf16[256,256]{1,0:T(8,128)(2,1)S(1)} %broadcast_select_fusion.3.d0), channel_id=1, source_target_pairs={{0,4},{4,0},{8,12},{12,8},{16,20},{20,16},{24,28},{28,24},{1,5},{5... | collective-permute-start | bytes 393224 | tf_op jit(solution)/shard_map/ppermute | solution.py:524
  33.0 7.0 %collective-permute-start.5 = (bf16[256,256]{1,0:T(8,128)(2,1)S(1)}, bf16[256,256]{1,0:T(8,128)(2,1)S(1)}, u32[]{:S(2)}, u32[]{:S(2)}) collective-permute-start(bf16[256,256]{1,0:T(8,128)(2,1)S(1)} %broadcast_select_fusion.3.d0), channel_id=1, source_target_pairs={{0,1},{1,0},{2,3},{3,2},{4,5},{5,4},{6,7},{7,6},{8,9},{9,8},{10,11... | collective-permute-start | bytes 393224 | tf_op jit(solution)/shard_map/ppermute | solution.py:523
  37.1 16.1 %collective-permute-start.9 = (bf16[256,1024]{1,0:T(8,128)(2,1)S(1)}, bf16[256,1024]{1,0:T(8,128)(2,1)S(1)}, u32[]{:S(2)}, u32[]{:S(2)}) collective-permute-start(bf16[256,1024]{1,0:T(8,128)(2,1)S(1)} %slice_select_fusion.1.refs_0_), channel_id=1, source_target_pairs={{0,4},{4,0},{1,5},{5,1},{2,6},{6,2},{3,7},{7,3}} | collective-permute-start | bytes 1572872 | tf_op jit(solution)/shard_map/ppermute | solution.py:545
  46.9 6.4 %collective-permute-start.8 = (bf16[256,1024]{1,0:T(8,128)(2,1)S(1)}, bf16[256,1024]{1,0:T(8,128)(2,1)S(1)}, u32[]{:S(2)}, u32[]{:S(2)}) collective-permute-start(bf16[256,1024]{1,0:T(8,128)(2,1)S(1)} %shard_map.18.refs_0_.refs_1_), channel_id=1, source_target_pairs={{0,8},{4,12},{8,16},{12,20},{1,9},{5,13},{9,17},{13,21},{2,10},{6,... | collective-permute-start | bytes 1572872 | tf_op jit(solution)/shard_map/ppermute | solution.py:543
  67.8 36.5 %collective-permute-start.10 = (bf16[3584,256]{1,0:T(8,128)(2,1)S(1)}, bf16[3584,256]{1,0:T(8,128)(2,1)S(1)}, u32[]{:S(2)}, u32[]{:S(2)}) collective-permute-start(bf16[3584,256]{1,0:T(8,128)(2,1)S(1)} %broadcast_select_fusion.own), channel_id=1, source_target_pairs={{0,1},{1,0},{2,3},{3,2},{4,5},{5,4},{6,7},{7,6},{8,9},{9,8},{10,11... | collective-permute-start | bytes 5505032 | tf_op jit(solution)/shard_map/ppermute | solution.py:581
  67.9 9.5 %collective-permute-start.12 = (bf16[256,1024]{1,0:T(8,128)(2,1)S(1)}, bf16[256,1024]{1,0:T(8,128)(2,1)S(1)}, u32[]{:S(2)}, u32[]{:S(2)}) collective-permute-start(bf16[256,1024]{1,0:T(8,128)(2,1)S(1)} %shard_map.18.refs_0_.refs_1_), channel_id=1, source_target_pairs={{0,4},{4,0},{8,12},{12,8},{1,5},{5,1},{9,13},{13,9},{2,6},{6,2},{1... | collective-permute-start | bytes 1572872 | tf_op jit(solution)/shard_map/ppermute | solution.py:545
  68.6 16.2 %collective-permute-start.11 = (bf16[256,1024]{1,0:T(8,128)(2,1)S(1)}, bf16[256,1024]{1,0:T(8,128)(2,1)S(1)}, u32[]{:S(2)}, u32[]{:S(2)}) collective-permute-start(bf16[256,1024]{1,0:T(8,128)(2,1)S(1)} %shard_map.20.refs_1_.refs_0_.refs_2_), channel_id=1, source_target_pairs={{0,8},{4,12},{8,16},{12,20},{16,24},{20,28},{1,9},{5,13},{9,17},{1... | collective-permute-start | bytes 1572872 | tf_op jit(solution)/shard_map/ppermute | solution.py:543
  69.9 24.2 %collective-permute-start.14 = (bf16[256,1024]{1,0:T(8,128)(2,1)S(1)}, bf16[256,1024]{1,0:T(8,128)(2,1)S(1)}, u32[]{:S(2)}, u32[]{:S(2)}) collective-permute-start(bf16[256,1024]{1,0:T(8,128)(2,1)S(1)} %shard_map.20.refs_1_.refs_0_.refs_2_), channel_id=1, source_target_pairs={{0,4},{4,0},{8,12},{12,8},{16,20},{20,16},{1,5},{5,1},{9,13},{13,9... | collective-permute-start | bytes 1572872 | tf_op jit(solution)/shard_map/ppermute | solution.py:545
  85.4 15.4 %collective-permute-start.13 = (bf16[256,1024]{1,0:T(8,128)(2,1)S(1)}, bf16[256,1024]{1,0:T(8,128)(2,1)S(1)}, u32[]{:S(2)}, u32[]{:S(2)}) collective-permute-start(bf16[256,1024]{1,0:T(8,128)(2,1)S(1)} %shard_map.23.refs_0_.refs_3_.refs_2_.refs_1_), channel_id=1, source_target_pairs={{0,8},{4,12},{8,16},{12,20},{16,24},{20,28},{1,9},{5,13},{9,17},{1... | collective-permute-start | bytes 1572872 | tf_op jit(solution)/shard_map/ppermute | solution.py:543
  86.9 23.1 %collective-permute-start.16 = (bf16[256,1024]{1,0:T(8,128)(2,1)S(1)}, bf16[256,1024]{1,0:T(8,128)(2,1)S(1)}, u32[]{:S(2)}, u32[]{:S(2)}) collective-permute-start(bf16[256,1024]{1,0:T(8,128)(2,1)S(1)} %shard_map.23.refs_0_.refs_3_.refs_2_.refs_1_), channel_id=1, source_target_pairs={{0,4},{4,0},{8,12},{12,8},{16,20},{20,16},{24,28},{28,24},{1,5},{5... | collective-permute-start | bytes 1572872 | tf_op jit(solution)/shard_map/ppermute | solution.py:545
  101.4 19.7 %collective-permute-start.18 = (bf16[256,1024]{1,0:T(8,128)(2,1)S(1)}, bf16[256,1024]{1,0:T(8,128)(2,1)S(1)}, u32[]{:S(2)}, u32[]{:S(2)}) collective-permute-start(bf16[256,1024]{1,0:T(8,128)(2,1)S(1)} %shard_map.25.refs_0_.refs_3_.refs_2_.refs_1_), channel_id=1, source_target_pairs={{0,4},{4,0},{8,12},{12,8},{16,20},{20,16},{24,28},{28,24},{1,5},{5... | collective-permute-start | bytes 1572872 | tf_op jit(solution)/shard_map/ppermute | solution.py:545
  103.0 15.7 %collective-permute-start.15 = (bf16[256,1024]{1,0:T(8,128)(2,1)S(1)}, bf16[256,1024]{1,0:T(8,128)(2,1)S(1)}, u32[]{:S(2)}, u32[]{:S(2)}) collective-permute-start(bf16[256,1024]{1,0:T(8,128)(2,1)S(1)} %shard_map.25.refs_0_.refs_3_.refs_2_.refs_1_), channel_id=1, source_target_pairs={{0,8},{4,12},{8,16},{12,20},{16,24},{20,28},{1,9},{5,13},{9,17},{1... | collective-permute-start | bytes 1572872 | tf_op jit(solution)/shard_map/ppermute | solution.py:543
  119.3 18.6 %collective-permute-start.20 = (bf16[256,1024]{1,0:T(8,128)(2,1)S(1)}, bf16[256,1024]{1,0:T(8,128)(2,1)S(1)}, u32[]{:S(2)}, u32[]{:S(2)}) collective-permute-start(bf16[256,1024]{1,0:T(8,128)(2,1)S(1)} %shard_map.28.refs_8_.refs_3_.refs_2_.refs_1_.refs_0_), channel_id=1, source_target_pairs={{0,4},{4,0},{8,12},{12,8},{16,20},{20,16},{24,28},{28,24},{1,5},{5... | collective-permute-start | bytes 1572872 | tf_op jit(solution)/shard_map/ppermute | solution.py:545
  119.9 14.6 %collective-permute-start.17 = (bf16[256,1024]{1,0:T(8,128)(2,1)S(1)}, bf16[256,1024]{1,0:T(8,128)(2,1)S(1)}, u32[]{:S(2)}, u32[]{:S(2)}) collective-permute-start(bf16[256,1024]{1,0:T(8,128)(2,1)S(1)} %shard_map.28.refs_8_.refs_3_.refs_2_.refs_1_.refs_0_), channel_id=1, source_target_pairs={{0,8},{4,12},{8,16},{12,20},{16,24},{20,28},{1,9},{5,13},{9,17},{1... | collective-permute-start | bytes 1572872 | tf_op jit(solution)/shard_map/ppermute | solution.py:543
  135.1 18.6 %collective-permute-start.22 = (bf16[256,1024]{1,0:T(8,128)(2,1)S(1)}, bf16[256,1024]{1,0:T(8,128)(2,1)S(1)}, u32[]{:S(2)}, u32[]{:S(2)}) collective-permute-start(bf16[256,1024]{1,0:T(8,128)(2,1)S(1)} %shard_map.30.refs_8_.refs_3_.refs_2_.refs_1_.refs_0_), channel_id=1, source_target_pairs={{0,4},{4,0},{8,12},{12,8},{16,20},{20,16},{24,28},{28,24},{1,5},{5... | collective-permute-start | bytes 1572872 | tf_op jit(solution)/shard_map/ppermute | solution.py:545
  136.7 12.7 %collective-permute-start.19 = (bf16[256,1024]{1,0:T(8,128)(2,1)S(1)}, bf16[256,1024]{1,0:T(8,128)(2,1)S(1)}, u32[]{:S(2)}, u32[]{:S(2)}) collective-permute-start(bf16[256,1024]{1,0:T(8,128)(2,1)S(1)} %shard_map.30.refs_8_.refs_3_.refs_2_.refs_1_.refs_0_), channel_id=1, source_target_pairs={{0,8},{4,12},{8,16},{12,20},{16,24},{20,28},{1,9},{5,13},{9,17},{1... | collective-permute-start | bytes 1572872 | tf_op jit(solution)/shard_map/ppermute | solution.py:543
  150.0 19.5 %collective-permute-start.24 = (bf16[256,1024]{1,0:T(8,128)(2,1)S(1)}, bf16[256,1024]{1,0:T(8,128)(2,1)S(1)}, u32[]{:S(2)}, u32[]{:S(2)}) collective-permute-start(bf16[256,1024]{1,0:T(8,128)(2,1)S(1)} %shard_map.32.refs_8_.refs_3_.refs_2_.refs_1_), channel_id=1, source_target_pairs={{8,12},{12,8},{16,20},{20,16},{24,28},{28,24},{9,13},{13,9},{17,21... | collective-permute-start | bytes 1572872 | tf_op jit(solution)/shard_map/ppermute | solution.py:545
  152.4 11.5 %collective-permute-start.21 = (bf16[256,1024]{1,0:T(8,128)(2,1)S(1)}, bf16[256,1024]{1,0:T(8,128)(2,1)S(1)}, u32[]{:S(2)}, u32[]{:S(2)}) collective-permute-start(bf16[256,1024]{1,0:T(8,128)(2,1)S(1)} %shard_map.32.refs_8_.refs_3_.refs_2_.refs_1_), channel_id=1, source_target_pairs={{8,16},{12,20},{16,24},{20,28},{9,17},{13,21},{17,25},{21,29},{10,... | collective-permute-start | bytes 1572872 | tf_op jit(solution)/shard_map/ppermute | solution.py:543
  164.6 17.5 %collective-permute-start.25 = (bf16[256,1024]{1,0:T(8,128)(2,1)S(1)}, bf16[256,1024]{1,0:T(8,128)(2,1)S(1)}, u32[]{:S(2)}, u32[]{:S(2)}) collective-permute-start(bf16[256,1024]{1,0:T(8,128)(2,1)S(1)} %shard_map.34.refs_8_.refs_3_.refs_2_), channel_id=1, source_target_pairs={{16,20},{20,16},{24,28},{28,24},{17,21},{21,17},{25,29},{29,25},{1... | collective-permute-start | bytes 1572872 | tf_op jit(solution)/shard_map/ppermute | solution.py:545
  168.0 11.1 %collective-permute-start.23 = (bf16[256,1024]{1,0:T(8,128)(2,1)S(1)}, bf16[256,1024]{1,0:T(8,128)(2,1)S(1)}, u32[]{:S(2)}, u32[]{:S(2)}) collective-permute-start(bf16[256,1024]{1,0:T(8,128)(2,1)S(1)} %shard_map.34.refs_8_.refs_3_.refs_2_), channel_id=1, source_target_pairs={{16,24},{20,28},{17,25},{21,29},{18,26},{22,30},{19,27},{23,31}} | collective-permute-start | bytes 1572872 | tf_op jit(solution)/shard_map/ppermute | solution.py:543
  179.7 11.1 %collective-permute-start.26 = (bf16[256,1024]{1,0:T(8,128)(2,1)S(1)}, bf16[256,1024]{1,0:T(8,128)(2,1)S(1)}, u32[]{:S(2)}, u32[]{:S(2)}) collective-permute-start(bf16[256,1024]{1,0:T(8,128)(2,1)S(1)} %shard_map.36.refs_8_.refs_3_), channel_id=1, source_target_pairs={{24,28},{28,24},{25,29},{29,25},{26,30},{30,26},{27,31},{31,27}} | collective-permute-start | bytes 1572872 | tf_op jit(solution)/shard_map/ppermute | solution.py:545

commit v5 on v4

--- a/solution.py
+++ b/solution.py
@@ -512,7 +512,11 @@
     width = matrix.shape[1] // CHUNKS
 
     diag = spread(matrix[:NB, :NB], "col", grid_cols, grid_col, grid_cols)
-    diag = spread(diag, "row", grid_rows, grid_row, grid_rows)
+    half = grid_rows // 2
+    pairs = [(i, i + half) for i in range(2)]
+    diag = jnp.where(grid_row >= half, lax.ppermute(diag, "row", pairs), diag)
+    near = diag[:1, :1]
+    diag = spread(diag, "row", half, grid_row, grid_rows)
     both_swap = [
         (i * grid_cols + j, (i ^ 1) * grid_cols + (j ^ 1))
         for i in range(grid_rows)
@@ -533,7 +537,7 @@
         if tick >= n_ticks:
             return done[:1]
         if tick == 0:
-            send = jnp.where(grid_row < 2, matrix[:NB, :width], diag[:1, :1])
+            send = matrix[:NB, :width]
         else:
             column = min(tick, CHUNKS - 1) * width
             send = gate_call(column, place, matrix, received[-1], [*other[-2:-1], *done])
@@ -545,10 +549,10 @@
         other.append(lax.ppermute(send, "row", across))
         return [send]
 
-    move(blocks[2:])
-    extra = []
+    move([])
+    extra = move(blocks[1:])
     stride = grid_cols // 2
-    column = jnp.where(grid_col < 2, matrix[:, :NB], diag[:1, :1])
+    column = jnp.where(grid_col < 2, matrix[:, :NB], near)
     pairs = [(i, i + stride) for i in range(grid_cols) if i % (2 * stride) < 2]
     moved = lax.ppermute(column, "col", pairs)
 
@@ -557,12 +561,12 @@
     kept = []
     for section in range(2):
         for piece in range(PIECES):
-            if section + piece > 0:
+            if section > 0 and piece == 0:
                 extra = move(square[:1])
-            if section > 0 and piece == 0:
                 moved = hold_call(moved, extra)
                 extra = [*extra, moved]
             if piece > 0:
+                extra = []
                 body = functools.partial(next_kernel, piece * per_piece, per_piece, len(extra))
                 square = factor_call(body, 3, None, square, extra, cost)
             elif section == 0:

time: 201 us -> 199 us (0.990)
  waiting for transfers between devices: 56.2 us -> 53.6 us
  Pallas kernels: 94.2 us -> 96.8 us
    ppermute x1, waiting for transfers between devices: 11.6 us -> 2.56 us  [on_device(): moved = lax.ppermute(column, 'col', pairs)]
    ppermute x9, waiting for transfers between devices: 25.1 us -> 31.9 us  [move(): received.append(lax.ppermute(send, 'row', onward) if onward else send)]
    pallas_call x7, Pallas kernels: 58.9 us -> 61.6 us  [update_call(): pl.pallas_call(functools.partial(update_kernel, first, count, lines, len(...]
    ppermute x3 -> x2, starting transfers between devices: 5.36 us -> 4.69 us  [spread(): moved = lax.ppermute(block, axis, pairs)]
    ppermute x3 -> x2, waiting for transfers between devices: 13.2 us -> 13.1 us  [spread(): moved = lax.ppermute(block, axis, pairs)]
  transfers between devices with their start and end apart: 27 -> 27, of which waited for: 12 -> 12; matrix products, arithmetic and copies ran while one was open for 1% -> 1% of each run, Pallas kernels for 43% -> 44%
where the time goes in v5:
time: 199 us; the launch traced here: 198 us
  Pallas kernels  96.8 us (49%)
  waiting for transfers between devices  53.6 us (27%)
  starting transfers between devices  38.1 us (19%)
  other arithmetic  6.7 us (3%)
  local copies, waits for them, and re-layouts  2.49 us (1%)
    pallas_call x7, Pallas kernels, update_call(): pl.pallas_call(functools.partial(update_kernel, first, count, lines, len(...  61.6 us
    ppermute x9, waiting for transfers between devices, move(): received.append(lax.ppermute(send, 'row', onward) if onward else send)  31.9 us
    pallas_call x4, Pallas kernels, factor_call(): pl.pallas_call(body, out_shape=[square] * 3 + [panel] * (n_out - 3), in_s...  24.3 us
    ppermute x10, starting transfers between devices, move(): other.append(lax.ppermute(send, 'row', across))  15.9 us
    ppermute x2, waiting for transfers between devices, spread(): moved = lax.ppermute(block, axis, pairs)  13.1 us
    ppermute x9, starting transfers between devices, move(): received.append(lax.ppermute(send, 'row', onward) if onward else send)  10.4 us
    pallas_call x1, Pallas kernels, left_call(): pl.pallas_call(left_kernel, grid=(4,), out_shape=jax.ShapeDtypeStruct((ro...  5.61 us
    pallas_call x9, Pallas kernels, gate_call(): pl.pallas_call(functools.partial(gate_kernel, column), out_shape=jax.Shap...  5.33 us
  transfers between devices with their start and end apart: 27, of which 12 were waited for; matrix products, arithmetic and copies ran while one was open for 1% of the time, Pallas kernels for 44%

profile of v5, /device:TPU:24, one launch (start us, length us, event | category | flops | bytes accessed | tf_op | source)
XLA Modules:
  0.0 198.4 jit_solution(12897931801765417796)
XLA Ops:
  0.0 0.9 slice.13
  0.9 3.4 %collective-permute-start = (bf16[256,256]{1,0:T(8,128)(2,1)S(1)}, bf16[256,256]{1,0:T(8,128)(2,1)S(1)}, u32[]{:S(2)}, u32[]{:S(2)}) collective-permute-start(bf16[256,256]{1,0:T(8,128)(2,1)S(1)} %slice.13), channel_id=1, source_target_pairs={{0,2},{1,3},{4,6},{5,7},{8,10},{9,11},{12,14},{13,15},{16,18},{17,... | collective-permute-start | bytes 393224 | tf_op jit(solution)/shard_map/ppermute | solution.py:499
  4.3 2.7 %collective-permute-done = bf16[256,256]{1,0:T(8,128)(2,1)S(1)} collective-permute-done((bf16[256,256]{1,0:T(8,128)(2,1)S(1)}, bf16[256,256]{1,0:T(8,128)(2,1)S(1)}, u32[]{:S(2)}, u32[]{:S(2)}) %collective-permute-start) | collective-permute-done | bytes 131104 | tf_op jit(solution)/shard_map/ppermute | solution.py:499
  7.1 0.9 broadcast_select_fusion.2
  9.2 3.4 %slice_select_fusion = bf16[3584,256]{1,0:T(8,128)(2,1)} fusion(bf16[3584,7168]{1,0:T(8,128)(2,1)} %matrix.31, pred[]{:T(512)S(6)} %lt.16, bf16[]{:T(256)} %bitcast.2), kind=kLoop, calls=%fused_computation | loop fusion | flops 917504 | bytes 3670019 | tf_op jit(solution)/shard_map/jit(_where)/select_n | solution.py:555
  12.6 4.5 %collective-permute-start.2 = (bf16[3584,256]{1,0:T(8,128)(2,1)}, bf16[3584,256]{1,0:T(8,128)(2,1)S(1)}, u32[]{:S(2)}, u32[]{:S(2)}) collective-permute-start(bf16[3584,256]{1,0:T(8,128)(2,1)} %slice_select_fusion), channel_id=1, source_target_pairs={{0,2},{1,3},{4,6},{5,7},{8,10},{9,11},{12,14},{13,15},{16,18},{17,... | collective-permute-start | bytes 5505032 | tf_op jit(solution)/shard_map/ppermute | solution.py:557
  17.1 1.1 slice.15.refs_0_
  18.2 0.7 collective-permute-start.3
  18.9 1.3 collective-permute-start.4
  20.2 10.4 %collective-permute-done.4 = bf16[256,256]{1,0:T(8,128)(2,1)S(1)} collective-permute-done((bf16[256,256]{1,0:T(8,128)(2,1)S(1)}, bf16[256,256]{1,0:T(8,128)(2,1)S(1)}, u32[]{:S(2)}, u32[]{:S(2)}) %collective-permute-start.4) | collective-permute-done | bytes 131104 | tf_op jit(solution)/shard_map/ppermute | solution.py:499
  30.7 1.6 collective-permute-start.6
  32.7 3.8 %collective-permute-done.7.refs_2_.d3 = bf16[256,256]{1,0:T(8,128)(2,1)S(1)} collective-permute-done((bf16[256,256]{1,0:T(8,128)(2,1)S(1)}, bf16[256,256]{1,0:T(8,128)(2,1)S(1)}, u32[]{:S(2)}, u32[]{:S(2)}) %collective-permute-start.7) | collective-permute-done | bytes 131104 | tf_op jit(solution)/shard_map/ppermute | solution.py:529
  37.1 2.2 %collective-permute-done.6.refs_1_.d2 = bf16[256,256]{1,0:T(8,128)(2,1)S(1)} collective-permute-done((bf16[256,256]{1,0:T(8,128)(2,1)S(1)}, bf16[256,256]{1,0:T(8,128)(2,1)S(1)}, u32[]{:S(2)}, u32[]{:S(2)}) %collective-permute-start.6) | collective-permute-done | bytes 131104 | tf_op jit(solution)/shard_map/ppermute | solution.py:528
  40.6 6.2 %shard_map.18 = (f32[256,256]{1,0:T(8,128)S(1)}, f32[256,256]{1,0:T(8,128)S(1)}, f32[256,256]{1,0:T(8,128)S(1)}) custom-call(s32[2]{0:T(128)S(1)} %pad_add_fusion.place_ref, bf16[256,256]{1,0:T(8,128)(2,1)S(1)} %broadcast_select_fusion.1.d0, bf16[256,256]{1,0:T(8,128)(2,1)S(1)} %collective-permute-done.5.refs_0_.d1, ...), custom_call_target="tpu_custom_call" | custom-call | flops 1000000000 | bytes 2097152 | tf_op jit(solution)/shard_map/pallas_call | solution.py:217
  46.9 5.6 %shard_map.19 = (f32[256,256]{1,0:T(8,128)S(1)}, f32[256,256]{1,0:T(8,128)S(1)}, f32[256,256]{1,0:T(8,128)S(1)}) custom-call(f32[256,256]{1,0:T(8,128)S(1)} %get-tuple-element.19.work_in, f32[256,256]{1,0:T(8,128)S(1)} %get-tuple-element.20.lower_in, f32[256,256]{1,0:T(8,128)S(1)} %get-tuple-element.21.upper_in), custom_call_target="tpu_custom_call" | custom-call | flops 1000000000 | bytes 2097152 | tf_op jit(solution)/shard_map/pallas_call | solution.py:217
  53.1 2.6 %collective-permute-done.2.refs_0_ = bf16[3584,256]{1,0:T(8,128)(2,1)S(1)} collective-permute-done((bf16[3584,256]{1,0:T(8,128)(2,1)}, bf16[3584,256]{1,0:T(8,128)(2,1)S(1)}, u32[]{:S(2)}, u32[]{:S(2)}) %collective-permute-start.2) | collective-permute-done | bytes 1835040 | tf_op jit(solution)/shard_map/ppermute | solution.py:557
  55.7 2.3 %broadcast_select_fusion.own = bf16[3584,256]{1,0:T(8,128)(2,1)S(1)} fusion(bf16[3584,256]{1,0:T(8,128)(2,1)S(1)} %shard_map.21.refs_1_, pred[]{:T(512)S(6)} %ge.10, bf16[]{:T(256)} %bitcast.2, bf16[3584,7168]{1,0:T(8,128)(2,1)} %matrix.31, pred[]{:T(512)S(6)} %lt.16), kind=kLoop, calls=%fused_computation.1 | loop fusion | flops 1835008 | bytes 5505028 | tf_op jit(solution)/shard_map/jit(_where)/select_n | solution.py:583
  58.0 0.7 collective-permute-start.12
  58.7 1.3 collective-permute-start.11
  60.0 0.9 collective-permute-start.14
  60.9 6.8 %shard_map.22 = (f32[256,256]{1,0:T(8,128)S(1)}, f32[256,256]{1,0:T(8,128)S(1)}, f32[256,256]{1,0:T(8,128)S(1)}, bf16[256,256]{1,0:T(8,128)(2,1)S(1)}, bf16[256,256]{1,0:T(8,128)(2,1)S(1)}) custom-call(s32[2]{0:T(128)S(1)} %pad_add_fusion.place_ref, bf16[256,256]{1,0:T(8,128)(2,1)S(1)} %broadcast_select_fusion.1.d0, ...), custom_call_target="tpu_custom_call" | custom-call | flops 1000000000 | bytes 2097152 | tf_op jit(solution)/shard_map/pallas_call | solution.py:217
  67.7 5.6 %shard_map.23 = (f32[256,256]{1,0:T(8,128)S(1)}, f32[256,256]{1,0:T(8,128)S(1)}, f32[256,256]{1,0:T(8,128)S(1)}) custom-call(f32[256,256]{1,0:T(8,128)S(1)} %get-tuple-element.25.work_in, f32[256,256]{1,0:T(8,128)S(1)} %get-tuple-element.26.lower_in, f32[256,256]{1,0:T(8,128)S(1)} %get-tuple-element.27.upper_in), custom_call_target="tpu_custom_call" | custom-call | flops 1000000000 | bytes 2097152 | tf_op jit(solution)/shard_map/pallas_call | solution.py:217
  73.4 7.9 %collective-permute-done.11.received = bf16[256,1024]{1,0:T(8,128)(2,1)S(1)} collective-permute-done((bf16[256,1024]{1,0:T(8,128)(2,1)S(1)}, bf16[256,1024]{1,0:T(8,128)(2,1)S(1)}, u32[]{:S(2)}, u32[]{:S(2)}) %collective-permute-start.11) | collective-permute-done | bytes 524320 | tf_op jit(solution)/shard_map/ppermute | solution.py:547
  81.9 1.3 collective-permute-start.13
  83.5 5.6 %shard_map.25.refs_1_.left_ref = bf16[3584,512]{1,0:T(8,128)(2,1)S(1)} custom-call(s32[2]{0:T(128)S(1)} %pad_add_fusion.place_ref, bf16[3584,256]{1,0:T(8,128)(2,1)S(1)} %broadcast_select_fusion.own, bf16[3584,256]{1,0:T(8,128)(2,1)S(1)} %collective-permute-done.10.other, f32[256,256]{1,0:T(8,128)S(1)} %get-tuple-element.23.inv_upper.inv_first, ...), custom_call_target="tpu_custom_call" | custom-call | flops 3288334336 | bytes 7340032 | tf_op jit(solution)/shard_map/pallas_call | solution.py:291
  89.1 9.5 %collective-permute-done.13.received = bf16[256,1024]{1,0:T(8,128)(2,1)S(1)} collective-permute-done((bf16[256,1024]{1,0:T(8,128)(2,1)S(1)}, bf16[256,1024]{1,0:T(8,128)(2,1)S(1)}, u32[]{:S(2)}, u32[]{:S(2)}) %collective-permute-start.13) | collective-permute-done | bytes 524320 | tf_op jit(solution)/shard_map/ppermute | solution.py:547
  99.2 1.7 collective-permute-start.18
  101.0 1.3 collective-permute-start.15
  102.3 9.1 %shard_map.27.refs_1_.refs_9_ = bf16[3584,7168]{1,0:T(8,128)(2,1)} custom-call(s32[2]{0:T(128)S(1)} %pad_add_fusion.place_ref, bf16[3584,512]{1,0:T(8,128)(2,1)S(1)} %shard_map.25.refs_1_.left_ref, f32[256,256]{1,0:T(8,128)S(1)} %get-tuple-element.22.refs_1_.packed_first, f32[256,256]{1,0:T(8,128)S(1)} %get-tuple-element.30.refs_1_.packed_second, ...), custom_call_target="tpu_custom_call" | custom-call | flops 5637144576 | bytes 22020096 | tf_op jit(solution)/shard_map/pallas_call | solution.py:462
  111.3 5.6 %collective-permute-done.15.received = bf16[256,1024]{1,0:T(8,128)(2,1)S(1)} collective-permute-done((bf16[256,1024]{1,0:T(8,128)(2,1)S(1)}, bf16[256,1024]{1,0:T(8,128)(2,1)S(1)}, u32[]{:S(2)}, u32[]{:S(2)}) %collective-permute-start.15) | collective-permute-done | bytes 524320 | tf_op jit(solution)/shard_map/ppermute | solution.py:547
  117.5 1.8 collective-permute-start.20
  119.3 1.3 collective-permute-start.17
  120.6 8.7 %shard_map.29.refs_1_.refs_9_ = bf16[3584,7168]{1,0:T(8,128)(2,1)} custom-call(s32[2]{0:T(128)S(1)} %pad_add_fusion.place_ref, bf16[3584,512]{1,0:T(8,128)(2,1)S(1)} %shard_map.25.refs_1_.left_ref, f32[256,256]{1,0:T(8,128)S(1)} %get-tuple-element.22.refs_1_.packed_first, ...), custom_call_target="tpu_custom_call", output_to_operand_aliasing={{}: (17, {})} | custom-call | flops 5637144576 | bytes 22020096 | tf_op jit(solution)/shard_map/pallas_call | solution.py:462
  129.3 3.9 %collective-permute-done.17.received = bf16[256,1024]{1,0:T(8,128)(2,1)S(1)} collective-permute-done((bf16[256,1024]{1,0:T(8,128)(2,1)S(1)}, bf16[256,1024]{1,0:T(8,128)(2,1)S(1)}, u32[]{:S(2)}, u32[]{:S(2)}) %collective-permute-start.17) | collective-permute-done | bytes 524320 | tf_op jit(solution)/shard_map/ppermute | solution.py:547
  134.2 1.3 collective-permute-start.19
  135.5 8.9 %shard_map.31.refs_1_.refs_9_ = bf16[3584,7168]{1,0:T(8,128)(2,1)} custom-call(s32[2]{0:T(128)S(1)} %pad_add_fusion.place_ref, bf16[3584,512]{1,0:T(8,128)(2,1)S(1)} %shard_map.25.refs_1_.left_ref, f32[256,256]{1,0:T(8,128)S(1)} %get-tuple-element.22.refs_1_.packed_first, ...), custom_call_target="tpu_custom_call", output_to_operand_aliasing={{}: (17, {})} | custom-call | flops 5637144576 | bytes 22020096 | tf_op jit(solution)/shard_map/pallas_call | solution.py:462
  144.4 2.4 %collective-permute-done.19.received = bf16[256,1024]{1,0:T(8,128)(2,1)S(1)} collective-permute-done((bf16[256,1024]{1,0:T(8,128)(2,1)S(1)}, bf16[256,1024]{1,0:T(8,128)(2,1)S(1)}, u32[]{:S(2)}, u32[]{:S(2)}) %collective-permute-start.19) | collective-permute-done | bytes 524320 | tf_op jit(solution)/shard_map/ppermute | solution.py:547
  147.4 3.6 %collective-permute-start.24 = (bf16[256,1024]{1,0:T(8,128)(2,1)S(1)}, bf16[256,1024]{1,0:T(8,128)(2,1)S(1)}, u32[]{:S(2)}, u32[]{:S(2)}) collective-permute-start(bf16[256,1024]{1,0:T(8,128)(2,1)S(1)} %shard_map.32.refs_8_.refs_3_.refs_2_.refs_1_), channel_id=1, source_target_pairs={{8,12},{12,8},{16,20},{20,16},{24,28},{28,24},{9,13},{13,9},{17,21... | collective-permute-start | bytes 1572872 | tf_op jit(solution)/shard_map/ppermute | solution.py:549
  151.1 1.3 collective-permute-start.21
  152.4 8.7 %shard_map.33.refs_1_.refs_9_ = bf16[3584,7168]{1,0:T(8,128)(2,1)} custom-call(s32[2]{0:T(128)S(1)} %pad_add_fusion.place_ref, bf16[3584,512]{1,0:T(8,128)(2,1)S(1)} %shard_map.25.refs_1_.left_ref, f32[256,256]{1,0:T(8,128)S(1)} %get-tuple-element.22.refs_1_.packed_first, ...), custom_call_target="tpu_custom_call", output_to_operand_aliasing={{}: (17, {})} | custom-call | flops 5637144576 | bytes 22020096 | tf_op jit(solution)/shard_map/pallas_call | solution.py:462
  161.1 1.5 collective-permute-done.21.received
  163.2 2.2 %collective-permute-start.25 = (bf16[256,1024]{1,0:T(8,128)(2,1)S(1)}, bf16[256,1024]{1,0:T(8,128)(2,1)S(1)}, u32[]{:S(2)}, u32[]{:S(2)}) collective-permute-start(bf16[256,1024]{1,0:T(8,128)(2,1)S(1)} %shard_map.34.refs_8_.refs_3_.refs_2_), channel_id=1, source_target_pairs={{16,20},{20,16},{24,28},{28,24},{17,21},{21,17},{25,29},{29,25},{1... | collective-permute-start | bytes 1572872 | tf_op jit(solution)/shard_map/ppermute | solution.py:549
  165.4 1.3 collective-permute-start.23
  166.7 8.7 %shard_map.35.refs_1_.refs_9_ = bf16[3584,7168]{1,0:T(8,128)(2,1)} custom-call(s32[2]{0:T(128)S(1)} %pad_add_fusion.place_ref, bf16[3584,512]{1,0:T(8,128)(2,1)S(1)} %shard_map.25.refs_1_.left_ref, f32[256,256]{1,0:T(8,128)S(1)} %get-tuple-element.22.refs_1_.packed_first, ...), custom_call_target="tpu_custom_call", output_to_operand_aliasing={{}: (17, {})} | custom-call | flops 5637144576 | bytes 22020096 | tf_op jit(solution)/shard_map/pallas_call | solution.py:462
  175.4 1.0 collective-permute-done.23.received
  177.1 3.6 %collective-permute-start.26 = (bf16[256,1024]{1,0:T(8,128)(2,1)S(1)}, bf16[256,1024]{1,0:T(8,128)(2,1)S(1)}, u32[]{:S(2)}, u32[]{:S(2)}) collective-permute-start(bf16[256,1024]{1,0:T(8,128)(2,1)S(1)} %shard_map.36.refs_8_.refs_3_), channel_id=1, source_target_pairs={{24,28},{28,24},{25,29},{29,25},{26,30},{30,26},{27,31},{31,27}} | collective-permute-start | bytes 1572872 | tf_op jit(solution)/shard_map/ppermute | solution.py:549
  180.7 8.7 %shard_map.37.refs_8_ = bf16[3584,7168]{1,0:T(8,128)(2,1)} custom-call(s32[2]{0:T(128)S(1)} %pad_add_fusion.place_ref, bf16[3584,512]{1,0:T(8,128)(2,1)S(1)} %shard_map.25.refs_1_.left_ref, f32[256,256]{1,0:T(8,128)S(1)} %get-tuple-element.22.refs_1_.packed_first, ...), custom_call_target="tpu_custom_call", output_to_operand_aliasing={{}: (17, {})} | custom-call | flops 5637144576 | bytes 22020096 | tf_op jit(solution)/shard_map/pallas_call | solution.py:462
  189.5 8.7 %shard_map.38 = bf16[3584,7168]{1,0:T(8,128)(2,1)} custom-call(s32[2]{0:T(128)S(1)} %pad_add_fusion.place_ref, bf16[3584,512]{1,0:T(8,128)(2,1)S(1)} %shard_map.25.refs_1_.left_ref, f32[256,256]{1,0:T(8,128)S(1)} %get-tuple-element.22.refs_1_.packed_first, f32[256,256]{1,0:T(8,128)S(1)} %get-tuple-element.30.refs_1_.packed_second, ...), custom_call_target="tpu_custom_call", output_to_operand_aliasing={{}: (16, {})} | custom-call | flops 5637144576 | bytes 22020096 | tf_op jit(solution)/shard_map/pallas_call | solution.py:462
  (37 shorter events, 9.1 us)
Async XLA Ops:
  0.9 6.1 %collective-permute-start = (bf16[256,256]{1,0:T(8,128)(2,1)S(1)}, bf16[256,256]{1,0:T(8,128)(2,1)S(1)}, u32[]{:S(2)}, u32[]{:S(2)}) collective-permute-start(bf16[256,256]{1,0:T(8,128)(2,1)S(1)} %slice.13), channel_id=1, source_target_pairs={{0,2},{1,3},{4,6},{5,7},{8,10},{9,11},{12,14},{13,15},{16,18},{17,... | collective-permute-start | bytes 393224 | tf_op jit(solution)/shard_map/ppermute | solution.py:499
  8.0 0.7 collective-permute-start.1
  12.6 43.1 %collective-permute-start.2 = (bf16[3584,256]{1,0:T(8,128)(2,1)}, bf16[3584,256]{1,0:T(8,128)(2,1)S(1)}, u32[]{:S(2)}, u32[]{:S(2)}) collective-permute-start(bf16[3584,256]{1,0:T(8,128)(2,1)} %slice_select_fusion), channel_id=1, source_target_pairs={{0,2},{1,3},{4,6},{5,7},{8,10},{9,11},{12,14},{13,15},{16,18},{17,... | collective-permute-start | bytes 5505032 | tf_op jit(solution)/shard_map/ppermute | solution.py:557
  18.2 21.1 %collective-permute-start.3 = (bf16[256,1024]{1,0:T(8,128)(2,1)S(1)}, bf16[256,1024]{1,0:T(8,128)(2,1)S(1)}, u32[]{:S(2)}, u32[]{:S(2)}) collective-permute-start(bf16[256,1024]{1,0:T(8,128)(2,1)S(1)} %slice.15.refs_0_), channel_id=1, source_target_pairs={{0,8},{4,12},{1,9},{5,13},{2,10},{6,14},{3,11},{7,15}} | collective-permute-start | bytes 1572872 | tf_op jit(solution)/shard_map/ppermute | solution.py:547
  18.9 11.7 %collective-permute-start.4 = (bf16[256,256]{1,0:T(8,128)(2,1)S(1)}, bf16[256,256]{1,0:T(8,128)(2,1)S(1)}, u32[]{:S(2)}, u32[]{:S(2)}) collective-permute-start(bf16[256,256]{1,0:T(8,128)(2,1)S(1)} %broadcast_select_fusion.3), channel_id=1, source_target_pairs={{0,8},{4,12},{16,24},{20,28},{1,9},{5,13},{17,25},{21,29},{2,10},{... | collective-permute-start | bytes 393224 | tf_op jit(solution)/shard_map/ppermute | solution.py:499
  30.7 5.8 %collective-permute-start.7 = (bf16[256,256]{1,0:T(8,128)(2,1)S(1)}, bf16[256,256]{1,0:T(8,128)(2,1)S(1)}, u32[]{:S(2)}, u32[]{:S(2)}) collective-permute-start(bf16[256,256]{1,0:T(8,128)(2,1)S(1)} %broadcast_select_fusion.1.d0), channel_id=1, source_target_pairs={{0,5},{1,4},{2,7},{3,6},{4,1},{5,0},{6,3},{7,2},{8,13},{9,12},{10,... | collective-permute-start | bytes 393224 | tf_op jit(solution)/shard_map/ppermute | solution.py:529
  30.7 8.6 %collective-permute-start.6 = (bf16[256,256]{1,0:T(8,128)(2,1)S(1)}, bf16[256,256]{1,0:T(8,128)(2,1)S(1)}, u32[]{:S(2)}, u32[]{:S(2)}) collective-permute-start(bf16[256,256]{1,0:T(8,128)(2,1)S(1)} %broadcast_select_fusion.1.d0), channel_id=1, source_target_pairs={{0,4},{4,0},{8,12},{12,8},{16,20},{20,16},{24,28},{28,24},{1,5},{5... | collective-permute-start | bytes 393224 | tf_op jit(solution)/shard_map/ppermute | solution.py:528
  32.3 7.0 %collective-permute-start.5 = (bf16[256,256]{1,0:T(8,128)(2,1)S(1)}, bf16[256,256]{1,0:T(8,128)(2,1)S(1)}, u32[]{:S(2)}, u32[]{:S(2)}) collective-permute-start(bf16[256,256]{1,0:T(8,128)(2,1)S(1)} %broadcast_select_fusion.1.d0), channel_id=1, source_target_pairs={{0,1},{1,0},{2,3},{3,2},{4,5},{5,4},{6,7},{7,6},{8,9},{9,8},{10,11... | collective-permute-start | bytes 393224 | tf_op jit(solution)/shard_map/ppermute | solution.py:527
  36.4 16.1 %collective-permute-start.9 = (bf16[256,1024]{1,0:T(8,128)(2,1)S(1)}, bf16[256,1024]{1,0:T(8,128)(2,1)S(1)}, u32[]{:S(2)}, u32[]{:S(2)}) collective-permute-start(bf16[256,1024]{1,0:T(8,128)(2,1)S(1)} %slice.15.refs_0_), channel_id=1, source_target_pairs={{0,4},{4,0},{1,5},{5,1},{2,6},{6,2},{3,7},{7,3}} | collective-permute-start | bytes 1572872 | tf_op jit(solution)/shard_map/ppermute | solution.py:549
  39.9 12.6 %collective-permute-start.8 = (bf16[256,1024]{1,0:T(8,128)(2,1)S(1)}, bf16[256,1024]{1,0:T(8,128)(2,1)S(1)}, u32[]{:S(2)}, u32[]{:S(2)}) collective-permute-start(bf16[256,1024]{1,0:T(8,128)(2,1)S(1)} %shard_map.17.refs_0_.refs_1_), channel_id=1, source_target_pairs={{0,8},{4,12},{8,16},{12,20},{1,9},{5,13},{9,17},{13,21},{2,10},{6,... | collective-permute-start | bytes 1572872 | tf_op jit(solution)/shard_map/ppermute | solution.py:547
  58.0 25.6 %collective-permute-start.10 = (bf16[3584,256]{1,0:T(8,128)(2,1)S(1)}, bf16[3584,256]{1,0:T(8,128)(2,1)S(1)}, u32[]{:S(2)}, u32[]{:S(2)}) collective-permute-start(bf16[3584,256]{1,0:T(8,128)(2,1)S(1)} %broadcast_select_fusion.own), channel_id=1, source_target_pairs={{0,1},{1,0},{2,3},{3,2},{4,5},{5,4},{6,7},{7,6},{8,9},{9,8},{10,11... | collective-permute-start | bytes 5505032 | tf_op jit(solution)/shard_map/ppermute | solution.py:585
  58.0 15.3 %collective-permute-start.12 = (bf16[256,1024]{1,0:T(8,128)(2,1)S(1)}, bf16[256,1024]{1,0:T(8,128)(2,1)S(1)}, u32[]{:S(2)}, u32[]{:S(2)}) collective-permute-start(bf16[256,1024]{1,0:T(8,128)(2,1)S(1)} %shard_map.17.refs_0_.refs_1_), channel_id=1, source_target_pairs={{0,4},{4,0},{8,12},{12,8},{1,5},{5,1},{9,13},{13,9},{2,6},{6,2},{1... | collective-permute-start | bytes 1572872 | tf_op jit(solution)/shard_map/ppermute | solution.py:549
  58.7 22.6 %collective-permute-start.11 = (bf16[256,1024]{1,0:T(8,128)(2,1)S(1)}, bf16[256,1024]{1,0:T(8,128)(2,1)S(1)}, u32[]{:S(2)}, u32[]{:S(2)}) collective-permute-start(bf16[256,1024]{1,0:T(8,128)(2,1)S(1)} %shard_map.20.refs_1_.refs_0_.refs_2_), channel_id=1, source_target_pairs={{0,8},{4,12},{8,16},{12,20},{16,24},{20,28},{1,9},{5,13},{9,17},{1... | collective-permute-start | bytes 1572872 | tf_op jit(solution)/shard_map/ppermute | solution.py:547
  60.0 29.1 %collective-permute-start.14 = (bf16[256,1024]{1,0:T(8,128)(2,1)S(1)}, bf16[256,1024]{1,0:T(8,128)(2,1)S(1)}, u32[]{:S(2)}, u32[]{:S(2)}) collective-permute-start(bf16[256,1024]{1,0:T(8,128)(2,1)S(1)} %shard_map.20.refs_1_.refs_0_.refs_2_), channel_id=1, source_target_pairs={{0,4},{4,0},{8,12},{12,8},{16,20},{20,16},{1,5},{5,1},{9,13},{13,9... | collective-permute-start | bytes 1572872 | tf_op jit(solution)/shard_map/ppermute | solution.py:549
  81.9 16.7 %collective-permute-start.13 = (bf16[256,1024]{1,0:T(8,128)(2,1)S(1)}, bf16[256,1024]{1,0:T(8,128)(2,1)S(1)}, u32[]{:S(2)}, u32[]{:S(2)}) collective-permute-start(bf16[256,1024]{1,0:T(8,128)(2,1)S(1)} %shard_map.24.refs_0_.refs_3_.refs_2_.refs_1_), channel_id=1, source_target_pairs={{0,8},{4,12},{8,16},{12,20},{16,24},{20,28},{1,9},{5,13},{9,17},{1... | collective-permute-start | bytes 1572872 | tf_op jit(solution)/shard_map/ppermute | solution.py:547
  83.2 19.0 %collective-permute-start.16 = (bf16[256,1024]{1,0:T(8,128)(2,1)S(1)}, bf16[256,1024]{1,0:T(8,128)(2,1)S(1)}, u32[]{:S(2)}, u32[]{:S(2)}) collective-permute-start(bf16[256,1024]{1,0:T(8,128)(2,1)S(1)} %shard_map.24.refs_0_.refs_3_.refs_2_.refs_1_), channel_id=1, source_target_pairs={{0,4},{4,0},{8,12},{12,8},{16,20},{20,16},{24,28},{28,24},{1,5},{5... | collective-permute-start | bytes 1572872 | tf_op jit(solution)/shard_map/ppermute | solution.py:549
  99.2 21.3 %collective-permute-start.18 = (bf16[256,1024]{1,0:T(8,128)(2,1)S(1)}, bf16[256,1024]{1,0:T(8,128)(2,1)S(1)}, u32[]{:S(2)}, u32[]{:S(2)}) collective-permute-start(bf16[256,1024]{1,0:T(8,128)(2,1)S(1)} %shard_map.26.refs_8_.refs_3_.refs_2_.refs_1_.refs_0_), channel_id=1, source_target_pairs={{0,4},{4,0},{8,12},{12,8},{16,20},{20,16},{24,28},{28,24},{1,5},{5... | collective-permute-start | bytes 1572872 | tf_op jit(solution)/shard_map/ppermute | solution.py:549
  101.0 16.0 %collective-permute-start.15 = (bf16[256,1024]{1,0:T(8,128)(2,1)S(1)}, bf16[256,1024]{1,0:T(8,128)(2,1)S(1)}, u32[]{:S(2)}, u32[]{:S(2)}) collective-permute-start(bf16[256,1024]{1,0:T(8,128)(2,1)S(1)} %shard_map.26.refs_8_.refs_3_.refs_2_.refs_1_.refs_0_), channel_id=1, source_target_pairs={{0,8},{4,12},{8,16},{12,20},{16,24},{20,28},{1,9},{5,13},{9,17},{1... | collective-permute-start | bytes 1572872 | tf_op jit(solution)/shard_map/ppermute | solution.py:547
  117.5 17.9 %collective-permute-start.20 = (bf16[256,1024]{1,0:T(8,128)(2,1)S(1)}, bf16[256,1024]{1,0:T(8,128)(2,1)S(1)}, u32[]{:S(2)}, u32[]{:S(2)}) collective-permute-start(bf16[256,1024]{1,0:T(8,128)(2,1)S(1)} %shard_map.28.refs_8_.refs_3_.refs_2_.refs_1_.refs_0_), channel_id=1, source_target_pairs={{0,4},{4,0},{8,12},{12,8},{16,20},{20,16},{24,28},{28,24},{1,5},{5... | collective-permute-start | bytes 1572872 | tf_op jit(solution)/shard_map/ppermute | solution.py:549
  119.3 13.9 %collective-permute-start.17 = (bf16[256,1024]{1,0:T(8,128)(2,1)S(1)}, bf16[256,1024]{1,0:T(8,128)(2,1)S(1)}, u32[]{:S(2)}, u32[]{:S(2)}) collective-permute-start(bf16[256,1024]{1,0:T(8,128)(2,1)S(1)} %shard_map.28.refs_8_.refs_3_.refs_2_.refs_1_.refs_0_), channel_id=1, source_target_pairs={{0,8},{4,12},{8,16},{12,20},{16,24},{20,28},{1,9},{5,13},{9,17},{1... | collective-permute-start | bytes 1572872 | tf_op jit(solution)/shard_map/ppermute | solution.py:547
  133.8 18.6 %collective-permute-start.22 = (bf16[256,1024]{1,0:T(8,128)(2,1)S(1)}, bf16[256,1024]{1,0:T(8,128)(2,1)S(1)}, u32[]{:S(2)}, u32[]{:S(2)}) collective-permute-start(bf16[256,1024]{1,0:T(8,128)(2,1)S(1)} %shard_map.30.refs_8_.refs_3_.refs_2_.refs_1_.refs_0_), channel_id=1, source_target_pairs={{0,4},{4,0},{8,12},{12,8},{16,20},{20,16},{24,28},{28,24},{1,5},{5... | collective-permute-start | bytes 1572872 | tf_op jit(solution)/shard_map/ppermute | solution.py:549
  134.2 12.7 %collective-permute-start.19 = (bf16[256,1024]{1,0:T(8,128)(2,1)S(1)}, bf16[256,1024]{1,0:T(8,128)(2,1)S(1)}, u32[]{:S(2)}, u32[]{:S(2)}) collective-permute-start(bf16[256,1024]{1,0:T(8,128)(2,1)S(1)} %shard_map.30.refs_8_.refs_3_.refs_2_.refs_1_.refs_0_), channel_id=1, source_target_pairs={{0,8},{4,12},{8,16},{12,20},{16,24},{20,28},{1,9},{5,13},{9,17},{1... | collective-permute-start | bytes 1572872 | tf_op jit(solution)/shard_map/ppermute | solution.py:547
  147.4 19.3 %collective-permute-start.24 = (bf16[256,1024]{1,0:T(8,128)(2,1)S(1)}, bf16[256,1024]{1,0:T(8,128)(2,1)S(1)}, u32[]{:S(2)}, u32[]{:S(2)}) collective-permute-start(bf16[256,1024]{1,0:T(8,128)(2,1)S(1)} %shard_map.32.refs_8_.refs_3_.refs_2_.refs_1_), channel_id=1, source_target_pairs={{8,12},{12,8},{16,20},{20,16},{24,28},{28,24},{9,13},{13,9},{17,21... | collective-permute-start | bytes 1572872 | tf_op jit(solution)/shard_map/ppermute | solution.py:549
  151.1 11.5 %collective-permute-start.21 = (bf16[256,1024]{1,0:T(8,128)(2,1)S(1)}, bf16[256,1024]{1,0:T(8,128)(2,1)S(1)}, u32[]{:S(2)}, u32[]{:S(2)}) collective-permute-start(bf16[256,1024]{1,0:T(8,128)(2,1)S(1)} %shard_map.32.refs_8_.refs_3_.refs_2_.refs_1_), channel_id=1, source_target_pairs={{8,16},{12,20},{16,24},{20,28},{9,17},{13,21},{17,25},{21,29},{10,... | collective-permute-start | bytes 1572872 | tf_op jit(solution)/shard_map/ppermute | solution.py:547
  163.2 17.5 %collective-permute-start.25 = (bf16[256,1024]{1,0:T(8,128)(2,1)S(1)}, bf16[256,1024]{1,0:T(8,128)(2,1)S(1)}, u32[]{:S(2)}, u32[]{:S(2)}) collective-permute-start(bf16[256,1024]{1,0:T(8,128)(2,1)S(1)} %shard_map.34.refs_8_.refs_3_.refs_2_), channel_id=1, source_target_pairs={{16,20},{20,16},{24,28},{28,24},{17,21},{21,17},{25,29},{29,25},{1... | collective-permute-start | bytes 1572872 | tf_op jit(solution)/shard_map/ppermute | solution.py:549
  165.4 11.1 %collective-permute-start.23 = (bf16[256,1024]{1,0:T(8,128)(2,1)S(1)}, bf16[256,1024]{1,0:T(8,128)(2,1)S(1)}, u32[]{:S(2)}, u32[]{:S(2)}) collective-permute-start(bf16[256,1024]{1,0:T(8,128)(2,1)S(1)} %shard_map.34.refs_8_.refs_3_.refs_2_), channel_id=1, source_target_pairs={{16,24},{20,28},{17,25},{21,29},{18,26},{22,30},{19,27},{23,31}} | collective-permute-start | bytes 1572872 | tf_op jit(solution)/shard_map/ppermute | solution.py:547
  177.1 12.4 %collective-permute-start.26 = (bf16[256,1024]{1,0:T(8,128)(2,1)S(1)}, bf16[256,1024]{1,0:T(8,128)(2,1)S(1)}, u32[]{:S(2)}, u32[]{:S(2)}) collective-permute-start(bf16[256,1024]{1,0:T(8,128)(2,1)S(1)} %shard_map.36.refs_8_.refs_3_), channel_id=1, source_target_pairs={{24,28},{28,24},{25,29},{29,25},{26,30},{30,26},{27,31},{31,27}} | collective-permute-start | bytes 1572872 | tf_op jit(solution)/shard_map/ppermute | solution.py:549

commit v6 on v5

--- a/solution.py
+++ b/solution.py
@@ -537,7 +537,7 @@
         if tick >= n_ticks:
             return done[:1]
         if tick == 0:
-            send = matrix[:NB, :width]
+            send = jnp.where(grid_row < 2, matrix[:NB, :width], diag[:1, :1])
         else:
             column = min(tick, CHUNKS - 1) * width
             send = gate_call(column, place, matrix, received[-1], [*other[-2:-1], *done])

time: 199 us -> 197 us (0.990)
  Pallas kernels: 96.8 us -> 94.4 us
  waiting for transfers between devices: 53.6 us -> 51.3 us
    pallas_call x7, Pallas kernels: 61.6 us -> 59.2 us  [update_call(): pl.pallas_call(functools.partial(update_kernel, first, count, lines, len(...]
where the time goes in v6:
time: 197 us; the launch traced here: 195 us
  Pallas kernels  94.4 us (48%)
  waiting for transfers between devices  51.3 us (26%)
  starting transfers between devices  38 us (19%)
  other arithmetic  8.56 us (4%)
  local copies, waits for them, and re-layouts  2 us (1%)
    pallas_call x7, Pallas kernels, update_call(): pl.pallas_call(functools.partial(update_kernel, first, count, lines, len(...  59.2 us
    ppermute x9, waiting for transfers between devices, move(): received.append(lax.ppermute(send, 'row', onward) if onward else send)  30.8 us
    pallas_call x4, Pallas kernels, factor_call(): pl.pallas_call(body, out_shape=[square] * 3 + [panel] * (n_out - 3), in_s...  24.3 us
    ppermute x10, starting transfers between devices, move(): other.append(lax.ppermute(send, 'row', across))  15.8 us
    ppermute x2, waiting for transfers between devices, spread(): moved = lax.ppermute(block, axis, pairs)  13.1 us
    ppermute x9, starting transfers between devices, move(): received.append(lax.ppermute(send, 'row', onward) if onward else send)  10.4 us
    pallas_call x1, Pallas kernels, left_call(): pl.pallas_call(left_kernel, grid=(4,), out_shape=jax.ShapeDtypeStruct((ro...  5.61 us
    pallas_call x9, Pallas kernels, gate_call(): pl.pallas_call(functools.partial(gate_kernel, column), out_shape=jax.Shap...  5.33 us
  transfers between devices with their start and end apart: 27, of which 12 were waited for; matrix products, arithmetic and copies ran while one was open for 1% of the time, Pallas kernels for 44%

profile of v6, /device:TPU:24, one launch (start us, length us, event | category | flops | bytes accessed | tf_op | source)
XLA Modules:
  0.0 195.0 jit_solution(3101955994401465235)
XLA Ops:
  0.0 0.9 slice.16
  0.9 3.4 %collective-permute-start = (bf16[256,256]{1,0:T(8,128)(2,1)S(1)}, bf16[256,256]{1,0:T(8,128)(2,1)S(1)}, u32[]{:S(2)}, u32[]{:S(2)}) collective-permute-start(bf16[256,256]{1,0:T(8,128)(2,1)S(1)} %slice.16), channel_id=1, source_target_pairs={{0,2},{1,3},{4,6},{5,7},{8,10},{9,11},{12,14},{13,15},{16,18},{17,... | collective-permute-start | bytes 393224 | tf_op jit(solution)/shard_map/ppermute | solution.py:499
  4.3 2.7 %collective-permute-done = bf16[256,256]{1,0:T(8,128)(2,1)S(1)} collective-permute-done((bf16[256,256]{1,0:T(8,128)(2,1)S(1)}, bf16[256,256]{1,0:T(8,128)(2,1)S(1)}, u32[]{:S(2)}, u32[]{:S(2)}) %collective-permute-start) | collective-permute-done | bytes 131104 | tf_op jit(solution)/shard_map/ppermute | solution.py:499
  7.1 0.9 broadcast_select_fusion.2
  9.2 3.4 %slice_select_fusion = bf16[3584,256]{1,0:T(8,128)(2,1)} fusion(bf16[3584,7168]{1,0:T(8,128)(2,1)} %matrix.31, pred[]{:T(512)S(6)} %lt.19, bf16[]{:T(256)} %bitcast.2), kind=kLoop, calls=%fused_computation | loop fusion | flops 917504 | bytes 3670019 | tf_op jit(solution)/shard_map/jit(_where)/select_n | solution.py:555
  12.6 4.5 %collective-permute-start.2 = (bf16[3584,256]{1,0:T(8,128)(2,1)}, bf16[3584,256]{1,0:T(8,128)(2,1)S(1)}, u32[]{:S(2)}, u32[]{:S(2)}) collective-permute-start(bf16[3584,256]{1,0:T(8,128)(2,1)} %slice_select_fusion), channel_id=1, source_target_pairs={{0,2},{1,3},{4,6},{5,7},{8,10},{9,11},{12,14},{13,15},{16,18},{17,... | collective-permute-start | bytes 5505032 | tf_op jit(solution)/shard_map/ppermute | solution.py:557
  17.1 1.3 collective-permute-start.3
  18.4 10.4 %collective-permute-done.3 = bf16[256,256]{1,0:T(8,128)(2,1)S(1)} collective-permute-done((bf16[256,256]{1,0:T(8,128)(2,1)S(1)}, bf16[256,256]{1,0:T(8,128)(2,1)S(1)}, u32[]{:S(2)}, u32[]{:S(2)}) %collective-permute-start.3) | collective-permute-done | bytes 131104 | tf_op jit(solution)/shard_map/ppermute | solution.py:499
  29.5 1.7 slice_select_fusion.1.refs_0_
  31.2 0.7 collective-permute-start.4
  32.0 1.6 collective-permute-start.6
  33.9 3.8 %collective-permute-done.7.refs_2_.d3 = bf16[256,256]{1,0:T(8,128)(2,1)S(1)} collective-permute-done((bf16[256,256]{1,0:T(8,128)(2,1)S(1)}, bf16[256,256]{1,0:T(8,128)(2,1)S(1)}, u32[]{:S(2)}, u32[]{:S(2)}) %collective-permute-start.7) | collective-permute-done | bytes 131104 | tf_op jit(solution)/shard_map/ppermute | solution.py:529
  38.3 2.2 %collective-permute-done.6.refs_1_.d2 = bf16[256,256]{1,0:T(8,128)(2,1)S(1)} collective-permute-done((bf16[256,256]{1,0:T(8,128)(2,1)S(1)}, bf16[256,256]{1,0:T(8,128)(2,1)S(1)}, u32[]{:S(2)}, u32[]{:S(2)}) %collective-permute-start.6) | collective-permute-done | bytes 131104 | tf_op jit(solution)/shard_map/ppermute | solution.py:528
  41.2 0.7 collective-permute-start.8
  41.9 6.2 %shard_map.18 = (f32[256,256]{1,0:T(8,128)S(1)}, f32[256,256]{1,0:T(8,128)S(1)}, f32[256,256]{1,0:T(8,128)S(1)}) custom-call(s32[2]{0:T(128)S(1)} %pad_add_fusion.place_ref, bf16[256,256]{1,0:T(8,128)(2,1)S(1)} %broadcast_select_fusion.1.d0, bf16[256,256]{1,0:T(8,128)(2,1)S(1)} %collective-permute-done.5.refs_0_.d1, ...), custom_call_target="tpu_custom_call" | custom-call | flops 1000000000 | bytes 2097152 | tf_op jit(solution)/shard_map/pallas_call | solution.py:217
  48.1 5.6 %shard_map.19 = (f32[256,256]{1,0:T(8,128)S(1)}, f32[256,256]{1,0:T(8,128)S(1)}, f32[256,256]{1,0:T(8,128)S(1)}) custom-call(f32[256,256]{1,0:T(8,128)S(1)} %get-tuple-element.19.work_in, f32[256,256]{1,0:T(8,128)S(1)} %get-tuple-element.20.lower_in, f32[256,256]{1,0:T(8,128)S(1)} %get-tuple-element.21.upper_in), custom_call_target="tpu_custom_call" | custom-call | flops 1000000000 | bytes 2097152 | tf_op jit(solution)/shard_map/pallas_call | solution.py:217
  54.4 1.3 collective-permute-done.2.refs_0_
  55.7 2.4 %broadcast_select_fusion.own = bf16[3584,256]{1,0:T(8,128)(2,1)S(1)} fusion(bf16[3584,256]{1,0:T(8,128)(2,1)S(1)} %shard_map.21.refs_1_, pred[]{:T(512)S(6)} %ge.10, bf16[]{:T(256)} %bitcast.2, bf16[3584,7168]{1,0:T(8,128)(2,1)} %matrix.31, pred[]{:T(512)S(6)} %lt.19), kind=kLoop, calls=%fused_computation.1 | loop fusion | flops 1835008 | bytes 5505028 | tf_op jit(solution)/shard_map/jit(_where)/select_n | solution.py:583
  58.9 1.3 collective-permute-start.11
  60.2 0.9 collective-permute-start.14
  61.1 6.8 %shard_map.22 = (f32[256,256]{1,0:T(8,128)S(1)}, f32[256,256]{1,0:T(8,128)S(1)}, f32[256,256]{1,0:T(8,128)S(1)}, bf16[256,256]{1,0:T(8,128)(2,1)S(1)}, bf16[256,256]{1,0:T(8,128)(2,1)S(1)}) custom-call(s32[2]{0:T(128)S(1)} %pad_add_fusion.place_ref, bf16[256,256]{1,0:T(8,128)(2,1)S(1)} %broadcast_select_fusion.1.d0, ...), custom_call_target="tpu_custom_call" | custom-call | flops 1000000000 | bytes 2097152 | tf_op jit(solution)/shard_map/pallas_call | solution.py:217
  67.9 5.7 %shard_map.23 = (f32[256,256]{1,0:T(8,128)S(1)}, f32[256,256]{1,0:T(8,128)S(1)}, f32[256,256]{1,0:T(8,128)S(1)}) custom-call(f32[256,256]{1,0:T(8,128)S(1)} %get-tuple-element.25.work_in, f32[256,256]{1,0:T(8,128)S(1)} %get-tuple-element.26.lower_in, f32[256,256]{1,0:T(8,128)S(1)} %get-tuple-element.27.upper_in), custom_call_target="tpu_custom_call" | custom-call | flops 1000000000 | bytes 2097152 | tf_op jit(solution)/shard_map/pallas_call | solution.py:217
  73.5 6.2 %collective-permute-done.11.received = bf16[256,1024]{1,0:T(8,128)(2,1)S(1)} collective-permute-done((bf16[256,1024]{1,0:T(8,128)(2,1)S(1)}, bf16[256,1024]{1,0:T(8,128)(2,1)S(1)}, u32[]{:S(2)}, u32[]{:S(2)}) %collective-permute-start.11) | collective-permute-done | bytes 524320 | tf_op jit(solution)/shard_map/ppermute | solution.py:547
  80.3 1.3 collective-permute-start.13
  81.6 1.6 collective-permute-start.16
  83.2 5.6 %shard_map.25.refs_1_.left_ref = bf16[3584,512]{1,0:T(8,128)(2,1)S(1)} custom-call(s32[2]{0:T(128)S(1)} %pad_add_fusion.place_ref, bf16[3584,256]{1,0:T(8,128)(2,1)S(1)} %broadcast_select_fusion.own, bf16[3584,256]{1,0:T(8,128)(2,1)S(1)} %collective-permute-done.10.other, f32[256,256]{1,0:T(8,128)S(1)} %get-tuple-element.23.inv_upper.inv_first, ...), custom_call_target="tpu_custom_call" | custom-call | flops 3288334336 | bytes 7340032 | tf_op jit(solution)/shard_map/pallas_call | solution.py:291
  88.8 9.2 %collective-permute-done.13.received = bf16[256,1024]{1,0:T(8,128)(2,1)S(1)} collective-permute-done((bf16[256,1024]{1,0:T(8,128)(2,1)S(1)}, bf16[256,1024]{1,0:T(8,128)(2,1)S(1)}, u32[]{:S(2)}, u32[]{:S(2)}) %collective-permute-start.13) | collective-permute-done | bytes 524320 | tf_op jit(solution)/shard_map/ppermute | solution.py:547
  99.2 1.3 collective-permute-start.15
  100.5 8.7 %shard_map.27.refs_1_.refs_9_ = bf16[3584,7168]{1,0:T(8,128)(2,1)} custom-call(s32[2]{0:T(128)S(1)} %pad_add_fusion.place_ref, bf16[3584,512]{1,0:T(8,128)(2,1)S(1)} %shard_map.25.refs_1_.left_ref, f32[256,256]{1,0:T(8,128)S(1)} %get-tuple-element.22.refs_1_.packed_first, f32[256,256]{1,0:T(8,128)S(1)} %get-tuple-element.30.refs_1_.packed_second, ...), custom_call_target="tpu_custom_call" | custom-call | flops 5637144576 | bytes 22020096 | tf_op jit(solution)/shard_map/pallas_call | solution.py:462
  109.3 5.1 %collective-permute-done.15.received = bf16[256,1024]{1,0:T(8,128)(2,1)S(1)} collective-permute-done((bf16[256,1024]{1,0:T(8,128)(2,1)S(1)}, bf16[256,1024]{1,0:T(8,128)(2,1)S(1)}, u32[]{:S(2)}, u32[]{:S(2)}) %collective-permute-start.15) | collective-permute-done | bytes 524320 | tf_op jit(solution)/shard_map/ppermute | solution.py:547
  115.0 1.6 collective-permute-start.20
  116.5 1.3 collective-permute-start.17
  117.8 8.4 %shard_map.29.refs_1_.refs_9_ = bf16[3584,7168]{1,0:T(8,128)(2,1)} custom-call(s32[2]{0:T(128)S(1)} %pad_add_fusion.place_ref, bf16[3584,512]{1,0:T(8,128)(2,1)S(1)} %shard_map.25.refs_1_.left_ref, f32[256,256]{1,0:T(8,128)S(1)} %get-tuple-element.22.refs_1_.packed_first, ...), custom_call_target="tpu_custom_call", output_to_operand_aliasing={{}: (17, {})} | custom-call | flops 5637144576 | bytes 22020096 | tf_op jit(solution)/shard_map/pallas_call | solution.py:462
  126.2 4.2 %collective-permute-done.17.received = bf16[256,1024]{1,0:T(8,128)(2,1)S(1)} collective-permute-done((bf16[256,1024]{1,0:T(8,128)(2,1)S(1)}, bf16[256,1024]{1,0:T(8,128)(2,1)S(1)}, u32[]{:S(2)}, u32[]{:S(2)}) %collective-permute-start.17) | collective-permute-done | bytes 524320 | tf_op jit(solution)/shard_map/ppermute | solution.py:547
  131.7 1.3 collective-permute-start.19
  133.0 8.6 %shard_map.31.refs_1_.refs_9_ = bf16[3584,7168]{1,0:T(8,128)(2,1)} custom-call(s32[2]{0:T(128)S(1)} %pad_add_fusion.place_ref, bf16[3584,512]{1,0:T(8,128)(2,1)S(1)} %shard_map.25.refs_1_.left_ref, f32[256,256]{1,0:T(8,128)S(1)} %get-tuple-element.22.refs_1_.packed_first, ...), custom_call_target="tpu_custom_call", output_to_operand_aliasing={{}: (17, {})} | custom-call | flops 5637144576 | bytes 22020096 | tf_op jit(solution)/shard_map/pallas_call | solution.py:462
  141.6 2.8 %collective-permute-done.19.received = bf16[256,1024]{1,0:T(8,128)(2,1)S(1)} collective-permute-done((bf16[256,1024]{1,0:T(8,128)(2,1)S(1)}, bf16[256,1024]{1,0:T(8,128)(2,1)S(1)}, u32[]{:S(2)}, u32[]{:S(2)}) %collective-permute-start.19) | collective-permute-done | bytes 524320 | tf_op jit(solution)/shard_map/ppermute | solution.py:547
  145.0 3.4 %collective-permute-start.24 = (bf16[256,1024]{1,0:T(8,128)(2,1)S(1)}, bf16[256,1024]{1,0:T(8,128)(2,1)S(1)}, u32[]{:S(2)}, u32[]{:S(2)}) collective-permute-start(bf16[256,1024]{1,0:T(8,128)(2,1)S(1)} %shard_map.32.refs_8_.refs_3_.refs_2_.refs_1_), channel_id=1, source_target_pairs={{8,12},{12,8},{16,20},{20,16},{24,28},{28,24},{9,13},{13,9},{17,21... | collective-permute-start | bytes 1572872 | tf_op jit(solution)/shard_map/ppermute | solution.py:549
  148.4 1.3 collective-permute-start.21
  149.7 8.4 %shard_map.33.refs_1_.refs_9_ = bf16[3584,7168]{1,0:T(8,128)(2,1)} custom-call(s32[2]{0:T(128)S(1)} %pad_add_fusion.place_ref, bf16[3584,512]{1,0:T(8,128)(2,1)S(1)} %shard_map.25.refs_1_.left_ref, f32[256,256]{1,0:T(8,128)S(1)} %get-tuple-element.22.refs_1_.packed_first, ...), custom_call_target="tpu_custom_call", output_to_operand_aliasing={{}: (17, {})} | custom-call | flops 5637144576 | bytes 22020096 | tf_op jit(solution)/shard_map/pallas_call | solution.py:462
  158.1 1.8 collective-permute-done.21.received
  160.5 2.5 %collective-permute-start.25 = (bf16[256,1024]{1,0:T(8,128)(2,1)S(1)}, bf16[256,1024]{1,0:T(8,128)(2,1)S(1)}, u32[]{:S(2)}, u32[]{:S(2)}) collective-permute-start(bf16[256,1024]{1,0:T(8,128)(2,1)S(1)} %shard_map.34.refs_8_.refs_3_.refs_2_), channel_id=1, source_target_pairs={{16,20},{20,16},{24,28},{28,24},{17,21},{21,17},{25,29},{29,25},{1... | collective-permute-start | bytes 1572872 | tf_op jit(solution)/shard_map/ppermute | solution.py:549
  163.0 1.3 collective-permute-start.23
  164.3 8.4 %shard_map.35.refs_1_.refs_9_ = bf16[3584,7168]{1,0:T(8,128)(2,1)} custom-call(s32[2]{0:T(128)S(1)} %pad_add_fusion.place_ref, bf16[3584,512]{1,0:T(8,128)(2,1)S(1)} %shard_map.25.refs_1_.left_ref, f32[256,256]{1,0:T(8,128)S(1)} %get-tuple-element.22.refs_1_.packed_first, ...), custom_call_target="tpu_custom_call", output_to_operand_aliasing={{}: (17, {})} | custom-call | flops 5637144576 | bytes 22020096 | tf_op jit(solution)/shard_map/pallas_call | solution.py:462
  172.7 1.4 collective-permute-done.23.received
  174.7 3.3 %collective-permute-start.26 = (bf16[256,1024]{1,0:T(8,128)(2,1)S(1)}, bf16[256,1024]{1,0:T(8,128)(2,1)S(1)}, u32[]{:S(2)}, u32[]{:S(2)}) collective-permute-start(bf16[256,1024]{1,0:T(8,128)(2,1)S(1)} %shard_map.36.refs_8_.refs_3_), channel_id=1, source_target_pairs={{24,28},{28,24},{25,29},{29,25},{26,30},{30,26},{27,31},{31,27}} | collective-permute-start | bytes 1572872 | tf_op jit(solution)/shard_map/ppermute | solution.py:549
  178.0 8.4 %shard_map.37.refs_8_ = bf16[3584,7168]{1,0:T(8,128)(2,1)} custom-call(s32[2]{0:T(128)S(1)} %pad_add_fusion.place_ref, bf16[3584,512]{1,0:T(8,128)(2,1)S(1)} %shard_map.25.refs_1_.left_ref, f32[256,256]{1,0:T(8,128)S(1)} %get-tuple-element.22.refs_1_.packed_first, ...), custom_call_target="tpu_custom_call", output_to_operand_aliasing={{}: (17, {})} | custom-call | flops 5637144576 | bytes 22020096 | tf_op jit(solution)/shard_map/pallas_call | solution.py:462
  186.4 8.4 %shard_map.38 = bf16[3584,7168]{1,0:T(8,128)(2,1)} custom-call(s32[2]{0:T(128)S(1)} %pad_add_fusion.place_ref, bf16[3584,512]{1,0:T(8,128)(2,1)S(1)} %shard_map.25.refs_1_.left_ref, f32[256,256]{1,0:T(8,128)S(1)} %get-tuple-element.22.refs_1_.packed_first, f32[256,256]{1,0:T(8,128)S(1)} %get-tuple-element.30.refs_1_.packed_second, ...), custom_call_target="tpu_custom_call", output_to_operand_aliasing={{}: (16, {})} | custom-call | flops 5637144576 | bytes 22020096 | tf_op jit(solution)/shard_map/pallas_call | solution.py:462
  (38 shorter events, 10.2 us)
Async XLA Ops:
  0.9 6.1 %collective-permute-start = (bf16[256,256]{1,0:T(8,128)(2,1)S(1)}, bf16[256,256]{1,0:T(8,128)(2,1)S(1)}, u32[]{:S(2)}, u32[]{:S(2)}) collective-permute-start(bf16[256,256]{1,0:T(8,128)(2,1)S(1)} %slice.16), channel_id=1, source_target_pairs={{0,2},{1,3},{4,6},{5,7},{8,10},{9,11},{12,14},{13,15},{16,18},{17,... | collective-permute-start | bytes 393224 | tf_op jit(solution)/shard_map/ppermute | solution.py:499
  8.0 0.7 collective-permute-start.1
  12.6 43.1 %collective-permute-start.2 = (bf16[3584,256]{1,0:T(8,128)(2,1)}, bf16[3584,256]{1,0:T(8,128)(2,1)S(1)}, u32[]{:S(2)}, u32[]{:S(2)}) collective-permute-start(bf16[3584,256]{1,0:T(8,128)(2,1)} %slice_select_fusion), channel_id=1, source_target_pairs={{0,2},{1,3},{4,6},{5,7},{8,10},{9,11},{12,14},{13,15},{16,18},{17,... | collective-permute-start | bytes 5505032 | tf_op jit(solution)/shard_map/ppermute | solution.py:557
  17.1 11.7 %collective-permute-start.3 = (bf16[256,256]{1,0:T(8,128)(2,1)S(1)}, bf16[256,256]{1,0:T(8,128)(2,1)S(1)}, u32[]{:S(2)}, u32[]{:S(2)}) collective-permute-start(bf16[256,256]{1,0:T(8,128)(2,1)S(1)} %broadcast_select_fusion.3), channel_id=1, source_target_pairs={{0,8},{4,12},{16,24},{20,28},{1,9},{5,13},{17,25},{21,29},{2,10},{... | collective-permute-start | bytes 393224 | tf_op jit(solution)/shard_map/ppermute | solution.py:499
  31.2 9.4 %collective-permute-start.4 = (bf16[256,1024]{1,0:T(8,128)(2,1)S(1)}, bf16[256,1024]{1,0:T(8,128)(2,1)S(1)}, u32[]{:S(2)}, u32[]{:S(2)}) collective-permute-start(bf16[256,1024]{1,0:T(8,128)(2,1)S(1)} %slice_select_fusion.1.refs_0_), channel_id=1, source_target_pairs={{0,8},{4,12},{1,9},{5,13},{2,10},{6,14},{3,11},{7,15}} | collective-permute-start | bytes 1572872 | tf_op jit(solution)/shard_map/ppermute | solution.py:547
  31.9 5.8 %collective-permute-start.7 = (bf16[256,256]{1,0:T(8,128)(2,1)S(1)}, bf16[256,256]{1,0:T(8,128)(2,1)S(1)}, u32[]{:S(2)}, u32[]{:S(2)}) collective-permute-start(bf16[256,256]{1,0:T(8,128)(2,1)S(1)} %broadcast_select_fusion.1.d0), channel_id=1, source_target_pairs={{0,5},{1,4},{2,7},{3,6},{4,1},{5,0},{6,3},{7,2},{8,13},{9,12},{10,... | collective-permute-start | bytes 393224 | tf_op jit(solution)/shard_map/ppermute | solution.py:529
  32.0 8.6 %collective-permute-start.6 = (bf16[256,256]{1,0:T(8,128)(2,1)S(1)}, bf16[256,256]{1,0:T(8,128)(2,1)S(1)}, u32[]{:S(2)}, u32[]{:S(2)}) collective-permute-start(bf16[256,256]{1,0:T(8,128)(2,1)S(1)} %broadcast_select_fusion.1.d0), channel_id=1, source_target_pairs={{0,4},{4,0},{8,12},{12,8},{16,20},{20,16},{24,28},{28,24},{1,5},{5... | collective-permute-start | bytes 393224 | tf_op jit(solution)/shard_map/ppermute | solution.py:528
  33.5 7.0 %collective-permute-start.5 = (bf16[256,256]{1,0:T(8,128)(2,1)S(1)}, bf16[256,256]{1,0:T(8,128)(2,1)S(1)}, u32[]{:S(2)}, u32[]{:S(2)}) collective-permute-start(bf16[256,256]{1,0:T(8,128)(2,1)S(1)} %broadcast_select_fusion.1.d0), channel_id=1, source_target_pairs={{0,1},{1,0},{2,3},{3,2},{4,5},{5,4},{6,7},{7,6},{8,9},{9,8},{10,11... | collective-permute-start | bytes 393224 | tf_op jit(solution)/shard_map/ppermute | solution.py:527
  37.7 16.1 %collective-permute-start.9 = (bf16[256,1024]{1,0:T(8,128)(2,1)S(1)}, bf16[256,1024]{1,0:T(8,128)(2,1)S(1)}, u32[]{:S(2)}, u32[]{:S(2)}) collective-permute-start(bf16[256,1024]{1,0:T(8,128)(2,1)S(1)} %slice_select_fusion.1.refs_0_), channel_id=1, source_target_pairs={{0,4},{4,0},{1,5},{5,1},{2,6},{6,2},{3,7},{7,3}} | collective-permute-start | bytes 1572872 | tf_op jit(solution)/shard_map/ppermute | solution.py:549
  41.2 12.6 %collective-permute-start.8 = (bf16[256,1024]{1,0:T(8,128)(2,1)S(1)}, bf16[256,1024]{1,0:T(8,128)(2,1)S(1)}, u32[]{:S(2)}, u32[]{:S(2)}) collective-permute-start(bf16[256,1024]{1,0:T(8,128)(2,1)S(1)} %shard_map.17.refs_0_.refs_1_), channel_id=1, source_target_pairs={{0,8},{4,12},{8,16},{12,20},{1,9},{5,13},{9,17},{13,21},{2,10},{6,... | collective-permute-start | bytes 1572872 | tf_op jit(solution)/shard_map/ppermute | solution.py:547
  58.1 25.1 %collective-permute-start.10 = (bf16[3584,256]{1,0:T(8,128)(2,1)S(1)}, bf16[3584,256]{1,0:T(8,128)(2,1)S(1)}, u32[]{:S(2)}, u32[]{:S(2)}) collective-permute-start(bf16[3584,256]{1,0:T(8,128)(2,1)S(1)} %broadcast_select_fusion.own), channel_id=1, source_target_pairs={{0,1},{1,0},{2,3},{3,2},{4,5},{5,4},{6,7},{7,6},{8,9},{9,8},{10,11... | collective-permute-start | bytes 5505032 | tf_op jit(solution)/shard_map/ppermute | solution.py:585
  58.2 15.3 %collective-permute-start.12 = (bf16[256,1024]{1,0:T(8,128)(2,1)S(1)}, bf16[256,1024]{1,0:T(8,128)(2,1)S(1)}, u32[]{:S(2)}, u32[]{:S(2)}) collective-permute-start(bf16[256,1024]{1,0:T(8,128)(2,1)S(1)} %shard_map.17.refs_0_.refs_1_), channel_id=1, source_target_pairs={{0,4},{4,0},{8,12},{12,8},{1,5},{5,1},{9,13},{13,9},{2,6},{6,2},{1... | collective-permute-start | bytes 1572872 | tf_op jit(solution)/shard_map/ppermute | solution.py:549
  58.9 20.8 %collective-permute-start.11 = (bf16[256,1024]{1,0:T(8,128)(2,1)S(1)}, bf16[256,1024]{1,0:T(8,128)(2,1)S(1)}, u32[]{:S(2)}, u32[]{:S(2)}) collective-permute-start(bf16[256,1024]{1,0:T(8,128)(2,1)S(1)} %shard_map.20.refs_1_.refs_0_.refs_2_), channel_id=1, source_target_pairs={{0,8},{4,12},{8,16},{12,20},{16,24},{20,28},{1,9},{5,13},{9,17},{1... | collective-permute-start | bytes 1572872 | tf_op jit(solution)/shard_map/ppermute | solution.py:547
  60.2 28.6 %collective-permute-start.14 = (bf16[256,1024]{1,0:T(8,128)(2,1)S(1)}, bf16[256,1024]{1,0:T(8,128)(2,1)S(1)}, u32[]{:S(2)}, u32[]{:S(2)}) collective-permute-start(bf16[256,1024]{1,0:T(8,128)(2,1)S(1)} %shard_map.20.refs_1_.refs_0_.refs_2_), channel_id=1, source_target_pairs={{0,4},{4,0},{8,12},{12,8},{16,20},{20,16},{1,5},{5,1},{9,13},{13,9... | collective-permute-start | bytes 1572872 | tf_op jit(solution)/shard_map/ppermute | solution.py:549
  80.3 17.7 %collective-permute-start.13 = (bf16[256,1024]{1,0:T(8,128)(2,1)S(1)}, bf16[256,1024]{1,0:T(8,128)(2,1)S(1)}, u32[]{:S(2)}, u32[]{:S(2)}) collective-permute-start(bf16[256,1024]{1,0:T(8,128)(2,1)S(1)} %shard_map.24.refs_0_.refs_3_.refs_2_.refs_1_), channel_id=1, source_target_pairs={{0,8},{4,12},{8,16},{12,20},{16,24},{20,28},{1,9},{5,13},{9,17},{1... | collective-permute-start | bytes 1572872 | tf_op jit(solution)/shard_map/ppermute | solution.py:547
  81.6 18.9 %collective-permute-start.16 = (bf16[256,1024]{1,0:T(8,128)(2,1)S(1)}, bf16[256,1024]{1,0:T(8,128)(2,1)S(1)}, u32[]{:S(2)}, u32[]{:S(2)}) collective-permute-start(bf16[256,1024]{1,0:T(8,128)(2,1)S(1)} %shard_map.24.refs_0_.refs_3_.refs_2_.refs_1_), channel_id=1, source_target_pairs={{0,4},{4,0},{8,12},{12,8},{16,20},{20,16},{24,28},{28,24},{1,5},{5... | collective-permute-start | bytes 1572872 | tf_op jit(solution)/shard_map/ppermute | solution.py:549
  98.7 19.2 %collective-permute-start.18 = (bf16[256,1024]{1,0:T(8,128)(2,1)S(1)}, bf16[256,1024]{1,0:T(8,128)(2,1)S(1)}, u32[]{:S(2)}, u32[]{:S(2)}) collective-permute-start(bf16[256,1024]{1,0:T(8,128)(2,1)S(1)} %shard_map.26.refs_8_.refs_3_.refs_2_.refs_1_.refs_0_), channel_id=1, source_target_pairs={{0,4},{4,0},{8,12},{12,8},{16,20},{20,16},{24,28},{28,24},{1,5},{5... | collective-permute-start | bytes 1572872 | tf_op jit(solution)/shard_map/ppermute | solution.py:549
  99.2 15.1 %collective-permute-start.15 = (bf16[256,1024]{1,0:T(8,128)(2,1)S(1)}, bf16[256,1024]{1,0:T(8,128)(2,1)S(1)}, u32[]{:S(2)}, u32[]{:S(2)}) collective-permute-start(bf16[256,1024]{1,0:T(8,128)(2,1)S(1)} %shard_map.26.refs_8_.refs_3_.refs_2_.refs_1_.refs_0_), channel_id=1, source_target_pairs={{0,8},{4,12},{8,16},{12,20},{16,24},{20,28},{1,9},{5,13},{9,17},{1... | collective-permute-start | bytes 1572872 | tf_op jit(solution)/shard_map/ppermute | solution.py:547
  115.0 18.0 %collective-permute-start.20 = (bf16[256,1024]{1,0:T(8,128)(2,1)S(1)}, bf16[256,1024]{1,0:T(8,128)(2,1)S(1)}, u32[]{:S(2)}, u32[]{:S(2)}) collective-permute-start(bf16[256,1024]{1,0:T(8,128)(2,1)S(1)} %shard_map.28.refs_8_.refs_3_.refs_2_.refs_1_.refs_0_), channel_id=1, source_target_pairs={{0,4},{4,0},{8,12},{12,8},{16,20},{20,16},{24,28},{28,24},{1,5},{5... | collective-permute-start | bytes 1572872 | tf_op jit(solution)/shard_map/ppermute | solution.py:549
  116.5 13.9 %collective-permute-start.17 = (bf16[256,1024]{1,0:T(8,128)(2,1)S(1)}, bf16[256,1024]{1,0:T(8,128)(2,1)S(1)}, u32[]{:S(2)}, u32[]{:S(2)}) collective-permute-start(bf16[256,1024]{1,0:T(8,128)(2,1)S(1)} %shard_map.28.refs_8_.refs_3_.refs_2_.refs_1_.refs_0_), channel_id=1, source_target_pairs={{0,8},{4,12},{8,16},{12,20},{16,24},{20,28},{1,9},{5,13},{9,17},{1... | collective-permute-start | bytes 1572872 | tf_op jit(solution)/shard_map/ppermute | solution.py:547
  131.0 18.6 %collective-permute-start.22 = (bf16[256,1024]{1,0:T(8,128)(2,1)S(1)}, bf16[256,1024]{1,0:T(8,128)(2,1)S(1)}, u32[]{:S(2)}, u32[]{:S(2)}) collective-permute-start(bf16[256,1024]{1,0:T(8,128)(2,1)S(1)} %shard_map.30.refs_8_.refs_3_.refs_2_.refs_1_.refs_0_), channel_id=1, source_target_pairs={{0,4},{4,0},{8,12},{12,8},{16,20},{20,16},{24,28},{28,24},{1,5},{5... | collective-permute-start | bytes 1572872 | tf_op jit(solution)/shard_map/ppermute | solution.py:549
  131.7 12.7 %collective-permute-start.19 = (bf16[256,1024]{1,0:T(8,128)(2,1)S(1)}, bf16[256,1024]{1,0:T(8,128)(2,1)S(1)}, u32[]{:S(2)}, u32[]{:S(2)}) collective-permute-start(bf16[256,1024]{1,0:T(8,128)(2,1)S(1)} %shard_map.30.refs_8_.refs_3_.refs_2_.refs_1_.refs_0_), channel_id=1, source_target_pairs={{0,8},{4,12},{8,16},{12,20},{16,24},{20,28},{1,9},{5,13},{9,17},{1... | collective-permute-start | bytes 1572872 | tf_op jit(solution)/shard_map/ppermute | solution.py:547
  145.0 19.3 %collective-permute-start.24 = (bf16[256,1024]{1,0:T(8,128)(2,1)S(1)}, bf16[256,1024]{1,0:T(8,128)(2,1)S(1)}, u32[]{:S(2)}, u32[]{:S(2)}) collective-permute-start(bf16[256,1024]{1,0:T(8,128)(2,1)S(1)} %shard_map.32.refs_8_.refs_3_.refs_2_.refs_1_), channel_id=1, source_target_pairs={{8,12},{12,8},{16,20},{20,16},{24,28},{28,24},{9,13},{13,9},{17,21... | collective-permute-start | bytes 1572872 | tf_op jit(solution)/shard_map/ppermute | solution.py:549
  148.4 11.5 %collective-permute-start.21 = (bf16[256,1024]{1,0:T(8,128)(2,1)S(1)}, bf16[256,1024]{1,0:T(8,128)(2,1)S(1)}, u32[]{:S(2)}, u32[]{:S(2)}) collective-permute-start(bf16[256,1024]{1,0:T(8,128)(2,1)S(1)} %shard_map.32.refs_8_.refs_3_.refs_2_.refs_1_), channel_id=1, source_target_pairs={{8,16},{12,20},{16,24},{20,28},{9,17},{13,21},{17,25},{21,29},{10,... | collective-permute-start | bytes 1572872 | tf_op jit(solution)/shard_map/ppermute | solution.py:547
  160.5 17.5 %collective-permute-start.25 = (bf16[256,1024]{1,0:T(8,128)(2,1)S(1)}, bf16[256,1024]{1,0:T(8,128)(2,1)S(1)}, u32[]{:S(2)}, u32[]{:S(2)}) collective-permute-start(bf16[256,1024]{1,0:T(8,128)(2,1)S(1)} %shard_map.34.refs_8_.refs_3_.refs_2_), channel_id=1, source_target_pairs={{16,20},{20,16},{24,28},{28,24},{17,21},{21,17},{25,29},{29,25},{1... | collective-permute-start | bytes 1572872 | tf_op jit(solution)/shard_map/ppermute | solution.py:549
  163.0 11.1 %collective-permute-start.23 = (bf16[256,1024]{1,0:T(8,128)(2,1)S(1)}, bf16[256,1024]{1,0:T(8,128)(2,1)S(1)}, u32[]{:S(2)}, u32[]{:S(2)}) collective-permute-start(bf16[256,1024]{1,0:T(8,128)(2,1)S(1)} %shard_map.34.refs_8_.refs_3_.refs_2_), channel_id=1, source_target_pairs={{16,24},{20,28},{17,25},{21,29},{18,26},{22,30},{19,27},{23,31}} | collective-permute-start | bytes 1572872 | tf_op jit(solution)/shard_map/ppermute | solution.py:547
  174.7 11.7 %collective-permute-start.26 = (bf16[256,1024]{1,0:T(8,128)(2,1)S(1)}, bf16[256,1024]{1,0:T(8,128)(2,1)S(1)}, u32[]{:S(2)}, u32[]{:S(2)}) collective-permute-start(bf16[256,1024]{1,0:T(8,128)(2,1)S(1)} %shard_map.36.refs_8_.refs_3_), channel_id=1, source_target_pairs={{24,28},{28,24},{25,29},{29,25},{26,30},{30,26},{27,31},{31,27}} | collective-permute-start | bytes 1572872 | tf_op jit(solution)/shard_map/ppermute | solution.py:549
